TPU v7x, 256 devices: a whole 4x4x8 slice. The times are simulated.
256 devices in a mesh: group: 4 (over y), block: 64 (over x, z, core).
Axes of the slice: x: 4, y: 4, z: 8, core: 2. Of those that a mesh axis runs over, the one named last changes fastest.
Arguments:
- estimate: float32 [3072, 64, 128], P('block'), may hold values from 0.5 to 2
- recorded: float32 [4, 64, 3072, 128], P('group', 'block'), may hold values from 0.2 to 3
- psf_x: float32 [4, 31], P('group'), may hold values from 0.05 to 1
- psf_y: float32 [4, 31], P('group'), may hold values from 0.05 to 1
- psf_z: float32 [4, 61], P('group'), may hold values from 0.05 to 1
- view_shifts: int32 [4], P('group'), may hold values from -8 to 8, as said below
- view_boxes: int32 [4, 2], P('group'), may hold values from 0 to 3072, as said below
Outputs:
- updated: float32 [3072, 64, 128], P('block')
Inputs may be any that keep to these rules, and one draw needn't show every extreme that they name: `view_shifts`: some view has shift 8 and some view has shift -8. `view_boxes`: each view's first cell lies in 0 to 768 and its end in 2304 to 3072; view 0 covers the whole grid.
All inputs are finite; a program needn't handle non-finite values.
Results may differ from a plain program's by a relative error of at most 0.0003.
Values sent between devices are 32-bit elements; how exact they have to be, the bound alone decides.
No kernel may reach another device: no remote copies, remote signals or barrier semaphores. Data moves between devices by JAX's collectives and lax.ppermute only.
A program may use at most 64 MiB of HBM per device.

v0:
```python
import jax
import jax.numpy as jnp
from jax import lax
from jax.sharding import PartitionSpec as P

PSFX = 31
SMAX = 8


def with_halo(block, sides, width):
    for axis, dim in sides:
        count = lax.axis_size(axis)
        forward = [(i, i + 1) for i in range(count - 1)]
        backward = [(target, source) for source, target in forward]
        low = lax.ppermute(
            lax.slice_in_dim(block, block.shape[dim] - width, None, axis=dim), axis, forward
        )
        high = lax.ppermute(lax.slice_in_dim(block, 0, width, axis=dim), axis, backward)
        block = jnp.concatenate([low, block, high], axis=dim)
    return block


def band_matrix(kernel_taps, length):
    half_width = kernel_taps.shape[0] // 2
    row_ids = jnp.arange(length)[:, None]
    col_ids = jnp.arange(length)[None, :]
    tap_index = col_ids - row_ids + half_width
    in_range = (tap_index >= 0) & (tap_index < kernel_taps.shape[0])
    return jnp.where(
        in_range, kernel_taps[jnp.clip(tap_index, 0, kernel_taps.shape[0] - 1)], jnp.float32(0.0)
    )


def slab_matrix(kernel_taps, slab_rows, wide_rows, forward, offset):
    row_ids = jnp.arange(slab_rows)[:, None]
    col_ids = jnp.arange(wide_rows)[None, :]
    if forward:
        tap_index = col_ids - row_ids - offset
    else:
        tap_index = row_ids - col_ids + offset
    in_range = (tap_index >= 0) & (tap_index < kernel_taps.shape[0])
    return jnp.where(
        in_range, kernel_taps[jnp.clip(tap_index, 0, kernel_taps.shape[0] - 1)], jnp.float32(0.0)
    )


def blur_plane(volume, band_y, band_z):
    partial_value = jnp.einsum("xbz,yb->xyz", volume, band_y, precision=lax.Precision.HIGHEST)
    return jnp.einsum("xyz,wz->xyw", partial_value, band_z, precision=lax.Precision.HIGHEST)


def extend(volume, margin):
    return with_halo(volume, (("block", 0),), margin)


def body(estimate, recorded, psf_x, psf_y, psf_z, view_shifts, view_boxes):
    slab_rows = estimate.shape[0]
    local_views = recorded.shape[0]
    half_x = PSFX // 2
    margin = half_x + SMAX
    wide_rows = slab_rows + 2 * margin
    first_row = lax.axis_index("block") * slab_rows
    positions = first_row + jnp.arange(slab_rows)
    fetched = lax.all_to_all(recorded, "block", split_axis=2, concat_axis=1, tiled=True)
    taps_x = psf_x[0] / jnp.sum(psf_x[0])
    taps_y = psf_y[0] / jnp.sum(psf_y[0])
    taps_z = psf_z[0] / jnp.sum(psf_z[0])
    band_y = band_matrix(taps_y, estimate.shape[1])
    band_z = band_matrix(taps_z, estimate.shape[2])
    shift_view = view_shifts[0]
    extended = extend(blur_plane(estimate, band_y, band_z), margin)
    forward_band = slab_matrix(taps_x, slab_rows, wide_rows, True, shift_view + margin - half_x)
    predicted = jnp.einsum("xe,eyz->xyz", forward_band, extended, precision=lax.Precision.HIGHEST)
    inside = (positions >= view_boxes[0, 0]) & (positions < view_boxes[0, 1])
    observed = jnp.transpose(fetched[0], (1, 0, 2))
    quotient = jnp.where(inside[:, None, None], observed / predicted, jnp.float32(1.0))
    adjoint_part = blur_plane(quotient, band_y.T, band_z.T)
    adjoint_wide = with_halo(adjoint_part, (("block", 0),), margin)
    backward_band = slab_matrix(taps_x, slab_rows, wide_rows, False, margin + half_x - shift_view)
    summed = jnp.einsum("xe,eyz->xyz", backward_band, adjoint_wide, precision=lax.Precision.HIGHEST)
    combined = lax.psum(summed, "group")
    return estimate * combined / (local_views * lax.axis_size("group"))


def solution(mesh):
    return jax.shard_map(
        body,
        mesh=mesh,
        in_specs=(
            P("block", None, None),
            P("group", "block", None, None),
            P("group", None),
            P("group", None),
            P("group", None),
            P("group"),
            P("group", None),
        ),
        out_specs=P("block", None, None),
        check_vma=False,
    )
```

profile of v0, /device:TPU:24, one launch (start us, length us, event | category | flops | bytes accessed | tf_op | source)
XLA Modules:
  0.0 304.4 jit_solution(3279910453212012902)
XLA Ops:
  6.5 12.3 %all-to-all-start = ((f32[1,1,3072,128]{3,1,0,2:T(1,128)}), f32[1,1,3072,128]{3,1,0,2:T(1,128)}, u32[]{:S(2)}, u32[]{:S(2)}) async-start(f32[1,1,3072,128]{3,1,0,2:T(1,128)} %bitcast.56), calls=%async_computation | async-start | bytes 3145728 | tf_op jit(solution)/shard_map/all_to_all | solution.py:64
  19.6 0.6 divide_bitcast_fusion.1
  20.3 24.7 %gather_fusion.1 = f32[4096]{0:T(1024)S(1)} fusion(f32[31]{0:T(128)S(1)} %divide_bitcast_fusion.1, s32[4096]{0:T(1024)S(1)} %broadcast_clamp_fusion), kind=kCustom, calls=%fused_computation.1 | custom fusion | bytes 49152 | tf_op jit(solution)/shard_map/gather | solution.py:30
  46.4 97.2 %gather_fusion.3 = f32[16384]{0:T(1024)S(1)} fusion(f32[61]{0:T(128)S(1)} %divide_bitcast_fusion, s32[16384]{0:T(1024)S(1)} %fusion.14), kind=kCustom, calls=%fused_computation.3 | custom fusion | bytes 196608 | tf_op jit(solution)/shard_map/gather | solution.py:30
  143.6 1.5 fusion.20
  145.1 1.4 fusion.6
  146.6 1.2 fusion.88
  147.8 2.8 collective-permute-start
  150.6 1.5 collective-permute-start.1
  154.2 25.7 %gather_fusion.2 = f32[4512]{0:T(1024)S(1)} fusion(f32[31]{0:T(128)S(1)} %divide_bitcast_fusion.2, s32[5120]{0:T(1024)S(1)} %pad_clamp_fusion), kind=kCustom, calls=%fused_computation.2 | custom fusion | bytes 54144 | tf_op jit(solution)/shard_map/gather | solution.py:43
  180.7 1.3 compare_and_fusion
  181.9 3.3 %pad_maximum_fusion = f32[94,64,128]{2,1,0:T(8,128)} fusion(f32[23,64,128]{2,1,0:T(8,128)} %collective-permute-done.1, f32[48,64,128]{2,1,0:T(8,128)S(1)} %fusion.6, f32[23,64,128]{2,1,0:T(8,128)} %collective-permute-done), kind=kLoop, calls=%fused_computation.8 | loop fusion | flops 1540096 | bytes 6160384 | tf_op jit(solution)/shard_map/concatenate | solution.py:19
  185.3 5.8 %divide_select_fusion = f32[48,64,128]{2,0,1:T(8,128)S(1)} fusion(f32[48,64,128]{2,0,1:T(8,128)} %bitcast.9, f32[94,64,128]{2,1,0:T(8,128)} %pad_maximum_fusion, pred[48]{0:T(512)(128)(4,1)S(1)} %compare_and_fusion, f32[48,94]{1,0:T(8,128)S(1)} %reshape.162, s32[]{:T(128)} %bitcast.10), kind=kOutput, calls=%fused_computation.18 | convolution fusion | flops 444361152 | bytes 6244020 | tf_op jit(solution)/shard_map/xe,eyz->xyz/dot_general | solution.py:73
  191.1 1.9 fusion.9
  193.0 1.4 fusion.4
  194.4 1.2 fusion.87
  195.7 4.1 %collective-permute-start.2 = (f32[23,64,128]{2,1,0:T(8,128)}, f32[23,64,128]{2,1,0:T(8,128)}, u32[]{:S(2)}, u32[]{:S(2)}) collective-permute-start(f32[23,64,128]{2,1,0:T(8,128)} %get-tuple-element.5), channel_id=1, source_target_pairs={{0,1},{1,2},{2,3},{3,4},{4,5},{5,6},{6,7},{7,8},{8,9},{9,10},{10,1... | collective-permute-start | bytes 2261000 | tf_op jit(solution)/shard_map/ppermute | solution.py:15
  199.8 1.5 collective-permute-start.3
  201.4 25.7 %gather_fusion = f32[4512]{0:T(1024)S(1)} fusion(f32[31]{0:T(128)S(1)} %divide_bitcast_fusion.2, s32[5120]{0:T(1024)S(1)} %pad_clamp_fusion.1), kind=kCustom, calls=%fused_computation | custom fusion | bytes 54144 | tf_op jit(solution)/shard_map/gather | solution.py:43
  227.3 1.7 pad_maximum_fusion.1
  229.0 4.6 %fusion = f32[48,64,128]{2,0,1:T(8,128)} fusion(f32[94,64,128]{2,1,0:T(8,128)S(1)} %pad_maximum_fusion.1, f32[48,94]{1,0:T(8,128)S(1)} %reshape.146, s32[]{:T(128)} %bitcast), kind=kOutput, calls=%fused_computation.4 | convolution fusion | flops 443574720 | bytes 4671108 | tf_op jit(solution)/shard_map/xe,eyz->xyz/dot_general | solution.py:80
  233.6 59.9 %all-reduce.2.cloned.1.call-done = f32[48,64,128]{2,0,1:T(8,128)} async-done(((f32[48,64,128]{2,0,1:T(8,128)}), f32[48,64,128]{2,0,1:T(8,128)}) %all-reduce.2.cloned.1.call-update) | async-done | bytes 1572880 | tf_op jit(solution)/shard_map/psum | solution.py:81
  293.5 2.4 fusion.8
  295.9 1.6 copy.27
  (36 shorter events, 4.6 us)
Async XLA Ops:
  6.5 12.5 %copy-start.2 = (f32[1,31]{1,0:T(1,128)S(1)}, f32[1,31]{1,0:T(1,128)}, u32[]{:S(2)}) copy-start(f32[1,31]{1,0:T(1,128)} %param.10) | copy-start | bytes 376
  6.5 178.8 %all-to-all-start = ((f32[1,1,3072,128]{3,1,0,2:T(1,128)}), f32[1,1,3072,128]{3,1,0,2:T(1,128)}, u32[]{:S(2)}, u32[]{:S(2)}) async-start(f32[1,1,3072,128]{3,1,0,2:T(1,128)} %bitcast.56), calls=%async_computation | async-start | bytes 3145728 | tf_op jit(solution)/shard_map/all_to_all | solution.py:64
  18.8 274.7 %all-reduce.2.cloned.1.call-start = ((), (), s32[]{:S(2)}) async-start(), calls=%async_computation.1 | async-start | bytes 3145728 | tf_op jit(solution)/shard_map/psum | solution.py:81
  20.3 24.8 %copy-start.3 = (f32[1,61]{1,0:T(1,128)S(1)}, f32[1,61]{1,0:T(1,128)}, u32[]{:S(2)}) copy-start(f32[1,61]{1,0:T(1,128)} %param.11) | copy-start | bytes 736
  46.4 97.2 %copy-start = (f32[48,64,128]{2,1,0:T(8,128)S(1)}, f32[48,64,128]{2,1,0:T(8,128)}, u32[]{:S(2)}) copy-start(f32[48,64,128]{2,1,0:T(8,128)} %param.7) | copy-start | bytes 4718596
  146.6 6.3 %copy-start.4 = (f32[1,31]{1,0:T(1,128)S(1)}, f32[1,31]{1,0:T(1,128)}, u32[]{:S(2)}) copy-start(f32[1,31]{1,0:T(1,128)} %param.9) | copy-start | bytes 376
  147.8 34.1 %collective-permute-start = (f32[23,64,128]{2,1,0:T(8,128)}, f32[23,64,128]{2,1,0:T(8,128)}, u32[]{:S(2)}, u32[]{:S(2)}) collective-permute-start(f32[23,64,128]{2,1,0:T(8,128)} %get-tuple-element.7), channel_id=1, source_target_pairs={{0,1},{1,2},{2,3},{3,4},{4,5},{5,6},{6,7},{7,8},{8,9},{9,10},{10,1... | collective-permute-start | bytes 2261000 | tf_op jit(solution)/shard_map/ppermute | solution.py:15
  150.6 31.3 %collective-permute-start.1 = (f32[23,64,128]{2,1,0:T(8,128)}, f32[23,64,128]{2,1,0:T(8,128)}, u32[]{:S(2)}, u32[]{:S(2)}) collective-permute-start(f32[23,64,128]{2,1,0:T(8,128)} %get-tuple-element.8), channel_id=1, source_target_pairs={{1,0},{2,1},{3,2},{4,3},{5,4},{6,5},{7,6},{8,7},{9,8},{10,9},{11,1... | collective-permute-start | bytes 2261000 | tf_op jit(solution)/shard_map/ppermute | solution.py:18
  154.2 25.8 %copy-start.1 = (s32[1,2]{1,0:T(1,128)S(1)}, s32[1,2]{1,0:T(1,128)}, u32[]{:S(2)}) copy-start(s32[1,2]{1,0:T(1,128)} %param.13) | copy-start | bytes 28
  195.7 31.6 %collective-permute-start.2 = (f32[23,64,128]{2,1,0:T(8,128)}, f32[23,64,128]{2,1,0:T(8,128)}, u32[]{:S(2)}, u32[]{:S(2)}) collective-permute-start(f32[23,64,128]{2,1,0:T(8,128)} %get-tuple-element.5), channel_id=1, source_target_pairs={{0,1},{1,2},{2,3},{3,4},{4,5},{5,6},{6,7},{7,8},{8,9},{9,10},{10,1... | collective-permute-start | bytes 2261000 | tf_op jit(solution)/shard_map/ppermute | solution.py:15
  199.8 27.5 %collective-permute-start.3 = (f32[23,64,128]{2,1,0:T(8,128)}, f32[23,64,128]{2,1,0:T(8,128)}, u32[]{:S(2)}, u32[]{:S(2)}) collective-permute-start(f32[23,64,128]{2,1,0:T(8,128)} %get-tuple-element.6), channel_id=1, source_target_pairs={{1,0},{2,1},{3,2},{4,3},{5,4},{6,5},{7,6},{8,7},{9,8},{10,9},{11,1... | collective-permute-start | bytes 2261000 | tf_op jit(solution)/shard_map/ppermute | solution.py:18
Sparse Core Ops, SparseCore 0:
  233.7 59.7 all-reduce.1
where the time goes:
time: 307 us; the launch traced here: 304 us
  local copies, waits for them, and re-layouts  179 us (58%)
  waiting for transfers between devices  59.9 us (20%)
  starting transfers between devices  22.2 us (7%)
  matrix products  16.7 us (5%)
  between operations  14.4 us (5%)
  other arithmetic  12.6 us (4%)
    gather x3, local copies, waits for them, and re-layouts, band_matrix(): kernel_taps[jnp.clip(tap_index, 0, kernel_taps.shape[0] - 1)]  122 us
    psum x1, waiting for transfers between devices, body(): combined = lax.psum(summed, 'group')  59.9 us
    gather x4, local copies, waits for them, and re-layouts, slab_matrix(): kernel_taps[jnp.clip(tap_index, 0, kernel_taps.shape[0] - 1)]  51.6 us
    all_to_all x1, starting transfers between devices, body(): lax.all_to_all(recorded, 'block', split_axis=2, concat_axis=1, tiled=True)  12.3 us
    ppermute x2, starting transfers between devices, with_halo(): lax.ppermute(lax.slice_in_dim(block, block.shape[dim] - width, None, axis...  6.94 us
  transfers between devices with their start and end apart: 6, of which 1 were waited for; matrix products, arithmetic and copies ran while one was open for 61% of the time, Pallas kernels for 0%

commit v1 on v0

v1 whole, which is shorter than its diff:
```python
import jax
import jax.numpy as jnp
from jax import lax
from jax.sharding import PartitionSpec as P

PSFX = 31
SMAX = 8


def with_halo(block, axis, width):
    count = lax.axis_size(axis)
    forward = [(i, i + 1) for i in range(count - 1)]
    backward = [(target, source) for source, target in forward]
    low = lax.ppermute(block[block.shape[0] - width :], axis, forward)
    high = lax.ppermute(block[:width], axis, backward)
    return jnp.concatenate([low, block, high], axis=0)


def pick_taps(kernel_taps, tap_index):
    taps = jnp.arange(kernel_taps.shape[0])[:, None, None]
    return jnp.sum(jnp.where(tap_index[None] == taps, kernel_taps[:, None, None], jnp.float32(0.0)), axis=0)


def band_matrix(kernel_taps, length):
    half_width = kernel_taps.shape[0] // 2
    row_ids = jnp.arange(length)[:, None]
    col_ids = jnp.arange(length)[None, :]
    return pick_taps(kernel_taps, col_ids - row_ids + half_width)


def slab_matrix(kernel_taps, slab_rows, wide_rows, forward, offset):
    row_ids = jnp.arange(slab_rows)[:, None]
    col_ids = jnp.arange(wide_rows)[None, :]
    if forward:
        tap_index = col_ids - row_ids - offset
    else:
        tap_index = row_ids - col_ids + offset
    return pick_taps(kernel_taps, tap_index)


def ring_sum(value, axis):
    me = lax.axis_index(axis)
    rows = value.shape[0] // 8
    up = [(i, (i + 1) % 4) for i in range(4)]
    down = [(i, (i + 3) % 4) for i in range(4)]

    def part(step, half):
        start = lax.rem(me + step, 4) * (2 * rows) + half * rows
        return lax.dynamic_slice_in_dim(value, start, rows, 0)

    def send(block, way):
        return lax.ppermute(block, axis, way)

    far_a, far_b = send(part(2, 0), up), send(part(2, 1), down)
    near_b, near_a = send(part(1, 1), up), send(part(3, 0), down)
    sum_a = send(part(1, 0) + far_a, up)
    sum_b = send(part(3, 1) + far_b, down)
    mine_a = part(0, 0) + near_a + sum_a
    mine_b = part(0, 1) + near_b + sum_b
    low_a, high_b = send(mine_a, up), send(mine_b, down)
    low_b, high_a = send(mine_b, up), send(mine_a, down)
    opposite_a, opposite_b = send(low_a, up), send(high_b, down)
    out = jnp.zeros_like(value)
    for step, half, block in (
        (0, 0, mine_a), (0, 1, mine_b), (3, 0, low_a), (3, 1, low_b),
        (1, 0, high_a), (1, 1, high_b), (2, 0, opposite_a), (2, 1, opposite_b),
    ):
        start = lax.rem(me + step, 4) * (2 * rows) + half * rows
        out = lax.dynamic_update_slice_in_dim(out, block, start, 0)
    return out


def blur_plane(volume, band_y, band_z):
    partial_value = jnp.einsum("xbz,yb->xyz", volume, band_y, precision=lax.Precision.HIGHEST)
    return jnp.einsum("xyz,wz->xyw", partial_value, band_z, precision=lax.Precision.HIGHEST)


def body(estimate, recorded, psf_x, psf_y, psf_z, view_shifts, view_boxes):
    slab_rows = estimate.shape[0]
    local_views = recorded.shape[0]
    half_x = PSFX // 2
    margin = half_x + SMAX
    wide_rows = slab_rows + 2 * margin
    first_row = lax.axis_index("block") * slab_rows
    positions = first_row + jnp.arange(slab_rows)
    fetched = lax.all_to_all(recorded, "block", split_axis=2, concat_axis=1, tiled=True)
    taps_x = psf_x[0] / jnp.sum(psf_x[0])
    taps_y = psf_y[0] / jnp.sum(psf_y[0])
    taps_z = psf_z[0] / jnp.sum(psf_z[0])
    band_y = band_matrix(taps_y, estimate.shape[1])
    band_z = band_matrix(taps_z, estimate.shape[2])
    shift_view = view_shifts[0]
    extended = blur_plane(with_halo(estimate, "block", margin), band_y, band_z)
    forward_band = slab_matrix(taps_x, slab_rows, wide_rows, True, shift_view + margin - half_x)
    predicted = jnp.einsum("xe,eyz->xyz", forward_band, extended, precision=lax.Precision.HIGHEST)
    inside = (positions >= view_boxes[0, 0]) & (positions < view_boxes[0, 1])
    observed = jnp.transpose(fetched[0], (1, 0, 2))
    quotient = jnp.where(inside[:, None, None], observed / predicted, jnp.float32(1.0))
    adjoint_part = blur_plane(quotient, band_y.T, band_z.T)
    adjoint_wide = with_halo(adjoint_part, "block", margin)
    backward_band = slab_matrix(taps_x, slab_rows, wide_rows, False, margin + half_x - shift_view)
    summed = jnp.einsum("xe,eyz->xyz", backward_band, adjoint_wide, precision=lax.Precision.HIGHEST)
    combined = ring_sum(summed, "group")
    return estimate * combined / (local_views * lax.axis_size("group"))


def solution(mesh):
    return jax.shard_map(
        body,
        mesh=mesh,
        in_specs=(
            P("block", None, None),
            P("group", "block", None, None),
            P("group", None),
            P("group", None),
            P("group", None),
            P("group"),
            P("group", None),
        ),
        out_specs=P("block", None, None),
        check_vma=False,
    )
```

time: 307 us -> 160 us (0.52)
  the two profiles are of different devices: /device:TPU:24 before, /device:TPU:38 now
where the time goes in v1:
time: 160 us
  waiting for transfers between devices  73.1 us (46%)
  starting transfers between devices  43.2 us (27%)
  matrix products  21.2 us (13%)
  other arithmetic  15.6 us (10%)
  local copies, waits for them, and re-layouts  5.45 us (3%)
    ppermute x2, waiting for transfers between devices, with_halo(): low = lax.ppermute(block[block.shape[0] - width:], axis, forward)  36.6 us
    ppermute x12, waiting for transfers between devices, send(): return lax.ppermute(block, axis, way)  34.8 us
    ppermute x12, starting transfers between devices, send(): return lax.ppermute(block, axis, way)  20.2 us
    all_to_all x1, starting transfers between devices, body(): lax.all_to_all(recorded, 'block', split_axis=2, concat_axis=1, tiled=True)  11.9 us
    dot_general x2, matrix products, blur_plane(): jnp.einsum('xyz,wz->xyw', partial_value, band_z, precision=lax.Precision....  7.86 us
    ppermute x2, starting transfers between devices, with_halo(): high = lax.ppermute(block[:width], axis, backward)  6.42 us
    dot_general x2, matrix products, blur_plane(): jnp.einsum('xbz,yb->xyz', volume, band_y, precision=lax.Precision.HIGHEST)  6.32 us
    ppermute x2, starting transfers between devices, with_halo(): low = lax.ppermute(block[block.shape[0] - width:], axis, forward)  4.68 us
  transfers between devices with their start and end apart: 17, of which 10 were waited for; matrix products, arithmetic and copies ran while one was open for 15% of the time, Pallas kernels for 0%

profile of v1, /device:TPU:38, one launch (start us, length us, event | category | flops | bytes accessed | tf_op | source)
XLA Modules:
  0.0 159.6 jit_solution(8104028351030104239)
XLA Ops:
  0.0 11.9 %all-to-all-start = ((f32[1,1,3072,128]{3,1,0,2:T(1,128)}), f32[1,1,3072,128]{3,1,0,2:T(1,128)S(1)}, u32[]{:S(2)}, u32[]{:S(2)}) async-start(f32[1,1,3072,128]{3,1,0,2:T(1,128)} %bitcast.38), calls=%async_computation | async-start | bytes 3145728 | tf_op jit(solution)/shard_map/all_to_all | solution.py:86
  13.2 2.0 %collective-permute-start = (f32[23,64,128]{2,1,0:T(8,128)}, f32[23,64,128]{2,1,0:T(8,128)}, u32[]{:S(2)}, u32[]{:S(2)}) collective-permute-start(f32[23,64,128]{2,1,0:T(8,128)} %get-tuple-element.14), channel_id=1, source_target_pairs={{0,1},{1,2},{2,3},{3,4},{4,5},{5,6},{6,7},{7,8},{8,9},{9,10},{10,1... | collective-permute-start | bytes 2261000 | tf_op jit(solution)/shard_map/ppermute | solution.py:14
  15.3 3.5 %collective-permute-start.1 = (f32[23,64,128]{2,1,0:T(8,128)}, f32[23,64,128]{2,1,0:T(8,128)}, u32[]{:S(2)}, u32[]{:S(2)}) collective-permute-start(f32[23,64,128]{2,1,0:T(8,128)} %get-tuple-element.15), channel_id=1, source_target_pairs={{1,0},{2,1},{3,2},{4,3},{5,4},{6,5},{7,6},{8,7},{9,8},{10,9},{11,1... | collective-permute-start | bytes 2261000 | tf_op jit(solution)/shard_map/ppermute | solution.py:15
  26.2 28.9 %collective-permute-done = f32[23,64,128]{2,1,0:T(8,128)} collective-permute-done((f32[23,64,128]{2,1,0:T(8,128)}, f32[23,64,128]{2,1,0:T(8,128)}, u32[]{:S(2)}, u32[]{:S(2)}) %collective-permute-start) | collective-permute-done | bytes 753696 | tf_op jit(solution)/shard_map/ppermute | solution.py:14
  55.1 4.2 %fusion.10 = f32[94,64,128]{2,1,0:T(8,128)S(1)} fusion(f32[23,64,128]{2,1,0:T(8,128)} %collective-permute-done.1, f32[48,64,128]{2,1,0:T(8,128)S(1)} %copy-done, f32[23,64,128]{2,1,0:T(8,128)} %collective-permute-done, f32[64,64]{1,0:T(8,128)S(1)} %select_reduce_fusion.1), kind=kOutput, calls=%fused_computation.13 | convolution fusion | flops 592936960 | bytes 6176768 | tf_op jit(solution)/shard_map/xbz,yb->xyz/dot_general | solution.py:74
  59.4 6.5 %fusion = f32[94,64,128]{2,0,1:T(8,128)} fusion(f32[94,64,128]{2,1,0:T(8,128)S(1)} %fusion.10, f32[128,128]{1,0:T(8,128)S(1)} %select_reduce_fusion), kind=kOutput, calls=%fused_computation.2 | convolution fusion | flops 1182793728 | bytes 6225920 | tf_op jit(solution)/shard_map/xyz,wz->xyw/dot_general | solution.py:75
  65.9 3.6 %divide_select_fusion = f32[48,64,128]{2,0,1:T(8,128)S(1)} fusion(f32[48,64,128]{2,0,1:T(8,128)S(1)} %bitcast.37, f32[94,64,128]{2,0,1:T(8,128)} %fusion, pred[48]{0:T(512)(128)(4,1)S(1)} %compare_and_fusion, f32[48,94]{1,0:T(8,128)S(1)} %get-tuple-element.6), kind=kOutput, calls=%fused_computation.19 | convolution fusion | flops 444334080 | bytes 6244016 | tf_op jit(solution)/shard_map/xe,eyz->xyz/dot_general | solution.py:95
  69.5 2.1 %fusion.15 = f32[64,48,128]{2,0,1:T(8,128)S(1)} fusion(f32[48,64,128]{2,0,1:T(8,128)S(1)} %divide_select_fusion, f32[64,64]{1,0:T(8,128)S(1)} %select_reduce_fusion.1), kind=kOutput, calls=%fused_computation.16 | convolution fusion | flops 301989888 | bytes 3162112 | tf_op jit(solution)/shard_map/xbz,yb->xyz/dot_general | solution.py:74
  74.2 2.6 %collective-permute-start.2 = (f32[23,64,128]{2,1,0:T(8,128)}, f32[23,64,128]{2,1,0:T(8,128)}, u32[]{:S(2)}, u32[]{:S(2)}) collective-permute-start(f32[23,64,128]{2,1,0:T(8,128)} %get-tuple-element.12), channel_id=1, source_target_pairs={{0,1},{1,2},{2,3},{3,4},{4,5},{5,6},{6,7},{7,8},{8,9},{9,10},{10,1... | collective-permute-start | bytes 2261000 | tf_op jit(solution)/shard_map/ppermute | solution.py:14
  76.8 2.9 %collective-permute-start.3 = (f32[23,64,128]{2,1,0:T(8,128)}, f32[23,64,128]{2,1,0:T(8,128)}, u32[]{:S(2)}, u32[]{:S(2)}) collective-permute-start(f32[23,64,128]{2,1,0:T(8,128)} %get-tuple-element.13), channel_id=1, source_target_pairs={{1,0},{2,1},{3,2},{4,3},{5,4},{6,5},{7,6},{8,7},{9,8},{10,9},{11,1... | collective-permute-start | bytes 2261000 | tf_op jit(solution)/shard_map/ppermute | solution.py:15
  79.8 7.7 %collective-permute-done.2 = f32[23,64,128]{2,1,0:T(8,128)} collective-permute-done((f32[23,64,128]{2,1,0:T(8,128)}, f32[23,64,128]{2,1,0:T(8,128)}, u32[]{:S(2)}, u32[]{:S(2)}) %collective-permute-start.2) | collective-permute-done | bytes 753696 | tf_op jit(solution)/shard_map/ppermute | solution.py:14
  90.9 3.5 %fusion.2 = f32[48,64,128]{2,0,1:T(8,128)S(1)} fusion(f32[94,64,128]{2,1,0:T(8,128)S(1)} %pad_maximum_fusion, f32[48,94]{1,0:T(8,128)S(1)} %get-tuple-element.5), kind=kOutput, calls=%fused_computation.4 | convolution fusion | flops 443547648 | bytes 4671104 | tf_op jit(solution)/shard_map/xe,eyz->xyz/dot_general | solution.py:102
  95.1 3.0 %collective-permute-start.8 = (f32[6,64,128]{2,0,1:T(8,128)}, f32[6,64,128]{2,0,1:T(8,128)}, u32[]{:S(2)}, u32[]{:S(2)}) collective-permute-start(f32[6,64,128]{2,0,1:T(8,128)} %get-tuple-element.11), channel_id=1, source_target_pairs={{0,192},{64,0},{128,64},{192,128},{1,193},{65,1},{129,65},{193,129... | collective-permute-start | bytes 589832 | tf_op jit(solution)/shard_map/ppermute | solution.py:52
  98.1 6.3 %collective-permute-done.8 = f32[6,64,128]{2,0,1:T(8,128)} collective-permute-done((f32[6,64,128]{2,0,1:T(8,128)}, f32[6,64,128]{2,0,1:T(8,128)}, u32[]{:S(2)}, u32[]{:S(2)}) %collective-permute-start.8) | collective-permute-done | bytes 196640 | tf_op jit(solution)/shard_map/ppermute | solution.py:52
  106.1 3.7 %collective-permute-start.9 = (f32[6,64,128]{2,0,1:T(8,128)}, f32[6,64,128]{2,0,1:T(8,128)}, u32[]{:S(2)}, u32[]{:S(2)}) collective-permute-start(f32[6,64,128]{2,0,1:T(8,128)} %dynamic-slice_add_fusion), channel_id=1, source_target_pairs={{0,192},{64,0},{128,64},{192,128},{1,193},{65,1},{129,65},{193,129... | collective-permute-start | bytes 589832 | tf_op jit(solution)/shard_map/ppermute | solution.py:52
  109.8 6.6 %collective-permute-done.9 = f32[6,64,128]{2,0,1:T(8,128)} collective-permute-done((f32[6,64,128]{2,0,1:T(8,128)}, f32[6,64,128]{2,0,1:T(8,128)}, u32[]{:S(2)}, u32[]{:S(2)}) %collective-permute-start.9) | collective-permute-done | bytes 196640 | tf_op jit(solution)/shard_map/ppermute | solution.py:52
  118.5 3.6 %collective-permute-start.4 = (f32[6,64,128]{2,0,1:T(8,128)}, f32[6,64,128]{2,0,1:T(8,128)}, u32[]{:S(2)}, u32[]{:S(2)}) collective-permute-start(f32[6,64,128]{2,0,1:T(8,128)} %get-tuple-element.9), channel_id=1, source_target_pairs={{0,192},{64,0},{128,64},{192,128},{1,193},{65,1},{129,65},{193,129... | collective-permute-start | bytes 589832 | tf_op jit(solution)/shard_map/ppermute | solution.py:52
  124.1 4.5 %collective-permute-done.5 = f32[6,64,128]{2,0,1:T(8,128)} collective-permute-done((f32[6,64,128]{2,0,1:T(8,128)}, f32[6,64,128]{2,0,1:T(8,128)}, u32[]{:S(2)}, u32[]{:S(2)}) %collective-permute-start.5) | collective-permute-done | bytes 196640 | tf_op jit(solution)/shard_map/ppermute | solution.py:52
  131.0 2.4 %collective-permute-done.13 = f32[6,64,128]{2,0,1:T(8,128)} collective-permute-done((f32[6,64,128]{2,0,1:T(8,128)S(1)}, f32[6,64,128]{2,0,1:T(8,128)}, u32[]{:S(2)}, u32[]{:S(2)}) %collective-permute-start.13) | collective-permute-done | bytes 196640 | tf_op jit(solution)/shard_map/ppermute | solution.py:52
  133.4 3.8 %collective-permute-start.15 = (f32[6,64,128]{2,0,1:T(8,128)}, f32[6,64,128]{2,0,1:T(8,128)S(1)}, u32[]{:S(2)}, u32[]{:S(2)}) collective-permute-start(f32[6,64,128]{2,0,1:T(8,128)} %collective-permute-done.13), channel_id=1, source_target_pairs={{0,192},{64,0},{128,64},{192,128},{1,193},{65,1},{129,65},{193,129... | collective-permute-start | bytes 589832 | tf_op jit(solution)/shard_map/ppermute | solution.py:52
  137.2 3.9 %collective-permute-done.6 = f32[6,64,128]{2,0,1:T(8,128)} collective-permute-done((f32[6,64,128]{2,0,1:T(8,128)}, f32[6,64,128]{2,0,1:T(8,128)}, u32[]{:S(2)}, u32[]{:S(2)}) %collective-permute-start.6) | collective-permute-done | bytes 196640 | tf_op jit(solution)/shard_map/ppermute | solution.py:52
  142.3 3.2 %collective-permute-start.12 = (f32[6,64,128]{2,0,1:T(8,128)S(1)}, f32[6,64,128]{2,0,1:T(8,128)S(1)}, u32[]{:S(2)}, u32[]{:S(2)}) collective-permute-start(f32[6,64,128]{2,0,1:T(8,128)S(1)} %add_add_fusion.1), channel_id=1, source_target_pairs={{0,192},{64,0},{128,64},{192,128},{1,193},{65,1},{129,65},{193,129... | collective-permute-start | bytes 589832 | tf_op jit(solution)/shard_map/ppermute | solution.py:52
  145.8 4.6 %collective-permute-done.10 = f32[6,64,128]{2,0,1:T(8,128)S(1)} collective-permute-done((f32[6,64,128]{2,0,1:T(8,128)S(1)}, f32[6,64,128]{2,0,1:T(8,128)S(1)}, u32[]{:S(2)}, u32[]{:S(2)}) %collective-permute-start.10) | collective-permute-done | bytes 196640 | tf_op jit(solution)/shard_map/ppermute | solution.py:52
  151.6 6.4 %collective-permute-done.14 = f32[6,64,128]{2,0,1:T(8,128)S(1)} collective-permute-done((f32[6,64,128]{2,0,1:T(8,128)S(1)}, f32[6,64,128]{2,0,1:T(8,128)S(1)}, u32[]{:S(2)}, u32[]{:S(2)}) %collective-permute-start.14) | collective-permute-done | bytes 196640 | tf_op jit(solution)/shard_map/ppermute | solution.py:52
  (58 shorter events, 27.1 us)
Async XLA Ops:
  0.0 11.9 %copy-start = (f32[48,64,128]{2,1,0:T(8,128)S(1)}, f32[48,64,128]{2,1,0:T(8,128)}, u32[]{:S(2)}) copy-start(f32[48,64,128]{2,1,0:T(8,128)} %param.7) | copy-start | bytes 4718596
  0.0 65.9 %all-to-all-start = ((f32[1,1,3072,128]{3,1,0,2:T(1,128)}), f32[1,1,3072,128]{3,1,0,2:T(1,128)S(1)}, u32[]{:S(2)}, u32[]{:S(2)}) async-start(f32[1,1,3072,128]{3,1,0,2:T(1,128)} %bitcast.38), calls=%async_computation | async-start | bytes 3145728 | tf_op jit(solution)/shard_map/all_to_all | solution.py:86
  11.9 7.6 %copy-start.2 = (f32[1,31]{1,0:T(1,128)S(1)}, f32[1,31]{1,0:T(1,128)}, u32[]{:S(2)}) copy-start(f32[1,31]{1,0:T(1,128)} %param.9) | copy-start | bytes 376
  11.9 8.2 %copy-start.3 = (f32[1,31]{1,0:T(1,128)S(1)}, f32[1,31]{1,0:T(1,128)}, u32[]{:S(2)}) copy-start(f32[1,31]{1,0:T(1,128)} %param.10) | copy-start | bytes 376
  11.9 8.8 %copy-start.1 = (s32[1,2]{1,0:T(1,128)S(1)}, s32[1,2]{1,0:T(1,128)}, u32[]{:S(2)}) copy-start(s32[1,2]{1,0:T(1,128)} %param.13) | copy-start | bytes 28
  11.9 12.0 %copy-start.4 = (f32[1,61]{1,0:T(1,128)S(1)}, f32[1,61]{1,0:T(1,128)}, u32[]{:S(2)}) copy-start(f32[1,61]{1,0:T(1,128)} %param.11) | copy-start | bytes 736
  13.2 41.9 %collective-permute-start = (f32[23,64,128]{2,1,0:T(8,128)}, f32[23,64,128]{2,1,0:T(8,128)}, u32[]{:S(2)}, u32[]{:S(2)}) collective-permute-start(f32[23,64,128]{2,1,0:T(8,128)} %get-tuple-element.14), channel_id=1, source_target_pairs={{0,1},{1,2},{2,3},{3,4},{4,5},{5,6},{6,7},{7,8},{8,9},{9,10},{10,1... | collective-permute-start | bytes 2261000 | tf_op jit(solution)/shard_map/ppermute | solution.py:14
  15.3 39.9 %collective-permute-start.1 = (f32[23,64,128]{2,1,0:T(8,128)}, f32[23,64,128]{2,1,0:T(8,128)}, u32[]{:S(2)}, u32[]{:S(2)}) collective-permute-start(f32[23,64,128]{2,1,0:T(8,128)} %get-tuple-element.15), channel_id=1, source_target_pairs={{1,0},{2,1},{3,2},{4,3},{5,4},{6,5},{7,6},{8,7},{9,8},{10,9},{11,1... | collective-permute-start | bytes 2261000 | tf_op jit(solution)/shard_map/ppermute | solution.py:15
  74.2 13.3 %collective-permute-start.2 = (f32[23,64,128]{2,1,0:T(8,128)}, f32[23,64,128]{2,1,0:T(8,128)}, u32[]{:S(2)}, u32[]{:S(2)}) collective-permute-start(f32[23,64,128]{2,1,0:T(8,128)} %get-tuple-element.12), channel_id=1, source_target_pairs={{0,1},{1,2},{2,3},{3,4},{4,5},{5,6},{6,7},{7,8},{8,9},{9,10},{10,1... | collective-permute-start | bytes 2261000 | tf_op jit(solution)/shard_map/ppermute | solution.py:14
  76.8 12.4 %collective-permute-start.3 = (f32[23,64,128]{2,1,0:T(8,128)}, f32[23,64,128]{2,1,0:T(8,128)}, u32[]{:S(2)}, u32[]{:S(2)}) collective-permute-start(f32[23,64,128]{2,1,0:T(8,128)} %get-tuple-element.13), channel_id=1, source_target_pairs={{1,0},{2,1},{3,2},{4,3},{5,4},{6,5},{7,6},{8,7},{9,8},{10,9},{11,1... | collective-permute-start | bytes 2261000 | tf_op jit(solution)/shard_map/ppermute | solution.py:15
  95.1 9.3 %collective-permute-start.8 = (f32[6,64,128]{2,0,1:T(8,128)}, f32[6,64,128]{2,0,1:T(8,128)}, u32[]{:S(2)}, u32[]{:S(2)}) collective-permute-start(f32[6,64,128]{2,0,1:T(8,128)} %get-tuple-element.11), channel_id=1, source_target_pairs={{0,192},{64,0},{128,64},{192,128},{1,193},{65,1},{129,65},{193,129... | collective-permute-start | bytes 589832 | tf_op jit(solution)/shard_map/ppermute | solution.py:52
  98.1 11.7 %collective-permute-start.7 = (f32[6,64,128]{2,0,1:T(8,128)S(1)}, f32[6,64,128]{2,0,1:T(8,128)}, u32[]{:S(2)}, u32[]{:S(2)}) collective-permute-start(f32[6,64,128]{2,0,1:T(8,128)S(1)} %get-tuple-element.10), channel_id=1, source_target_pairs={{0,64},{64,128},{128,192},{192,0},{1,65},{65,129},{129,193},{193,1... | collective-permute-start | bytes 589832 | tf_op jit(solution)/shard_map/ppermute | solution.py:52
  106.1 10.3 %collective-permute-start.9 = (f32[6,64,128]{2,0,1:T(8,128)}, f32[6,64,128]{2,0,1:T(8,128)}, u32[]{:S(2)}, u32[]{:S(2)}) collective-permute-start(f32[6,64,128]{2,0,1:T(8,128)} %dynamic-slice_add_fusion), channel_id=1, source_target_pairs={{0,192},{64,0},{128,64},{192,128},{1,193},{65,1},{129,65},{193,129... | collective-permute-start | bytes 589832 | tf_op jit(solution)/shard_map/ppermute | solution.py:52
  118.4 10.3 %collective-permute-start.5 = (f32[6,64,128]{2,0,1:T(8,128)}, f32[6,64,128]{2,0,1:T(8,128)}, u32[]{:S(2)}, u32[]{:S(2)}) collective-permute-start(f32[6,64,128]{2,0,1:T(8,128)} %get-tuple-element.8), channel_id=1, source_target_pairs={{0,64},{64,128},{128,192},{192,0},{1,65},{65,129},{129,193},{193,1... | collective-permute-start | bytes 589832 | tf_op jit(solution)/shard_map/ppermute | solution.py:52
  118.5 18.7 %collective-permute-start.4 = (f32[6,64,128]{2,0,1:T(8,128)}, f32[6,64,128]{2,0,1:T(8,128)}, u32[]{:S(2)}, u32[]{:S(2)}) collective-permute-start(f32[6,64,128]{2,0,1:T(8,128)} %get-tuple-element.9), channel_id=1, source_target_pairs={{0,192},{64,0},{128,64},{192,128},{1,193},{65,1},{129,65},{193,129... | collective-permute-start | bytes 589832 | tf_op jit(solution)/shard_map/ppermute | solution.py:52
  122.1 11.3 %collective-permute-start.13 = (f32[6,64,128]{2,0,1:T(8,128)S(1)}, f32[6,64,128]{2,0,1:T(8,128)}, u32[]{:S(2)}, u32[]{:S(2)}) collective-permute-start(f32[6,64,128]{2,0,1:T(8,128)S(1)} %get-tuple-element.7), channel_id=1, source_target_pairs={{0,192},{64,0},{128,64},{192,128},{1,193},{65,1},{129,65},{193,129... | collective-permute-start | bytes 589832 | tf_op jit(solution)/shard_map/ppermute | solution.py:52
  130.3 10.8 %collective-permute-start.6 = (f32[6,64,128]{2,0,1:T(8,128)}, f32[6,64,128]{2,0,1:T(8,128)}, u32[]{:S(2)}, u32[]{:S(2)}) collective-permute-start(f32[6,64,128]{2,0,1:T(8,128)} %dynamic-slice_add_fusion.1), channel_id=1, source_target_pairs={{0,64},{64,128},{128,192},{192,0},{1,65},{65,129},{129,193},{193,1... | collective-permute-start | bytes 589832 | tf_op jit(solution)/shard_map/ppermute | solution.py:52
  130.3 20.1 %collective-permute-start.11 = (f32[6,64,128]{2,0,1:T(8,128)S(1)}, f32[6,64,128]{2,0,1:T(8,128)S(1)}, u32[]{:S(2)}, u32[]{:S(2)}) collective-permute-start(f32[6,64,128]{2,0,1:T(8,128)S(1)} %get-tuple-element.7), channel_id=1, source_target_pairs={{0,64},{64,128},{128,192},{192,0},{1,65},{65,129},{129,193},{193,1... | collective-permute-start | bytes 589832 | tf_op jit(solution)/shard_map/ppermute | solution.py:52
  133.4 24.7 %collective-permute-start.15 = (f32[6,64,128]{2,0,1:T(8,128)}, f32[6,64,128]{2,0,1:T(8,128)S(1)}, u32[]{:S(2)}, u32[]{:S(2)}) collective-permute-start(f32[6,64,128]{2,0,1:T(8,128)} %collective-permute-done.13), channel_id=1, source_target_pairs={{0,192},{64,0},{128,64},{192,128},{1,193},{65,1},{129,65},{193,129... | collective-permute-start | bytes 589832 | tf_op jit(solution)/shard_map/ppermute | solution.py:52
  142.2 8.2 %collective-permute-start.10 = (f32[6,64,128]{2,0,1:T(8,128)S(1)}, f32[6,64,128]{2,0,1:T(8,128)S(1)}, u32[]{:S(2)}, u32[]{:S(2)}) collective-permute-start(f32[6,64,128]{2,0,1:T(8,128)S(1)} %add_add_fusion.1), channel_id=1, source_target_pairs={{0,64},{64,128},{128,192},{192,0},{1,65},{65,129},{129,193},{193,1... | collective-permute-start | bytes 589832 | tf_op jit(solution)/shard_map/ppermute | solution.py:52
  142.3 8.3 %collective-permute-start.12 = (f32[6,64,128]{2,0,1:T(8,128)S(1)}, f32[6,64,128]{2,0,1:T(8,128)S(1)}, u32[]{:S(2)}, u32[]{:S(2)}) collective-permute-start(f32[6,64,128]{2,0,1:T(8,128)S(1)} %add_add_fusion.1), channel_id=1, source_target_pairs={{0,192},{64,0},{128,64},{192,128},{1,193},{65,1},{129,65},{193,129... | collective-permute-start | bytes 589832 | tf_op jit(solution)/shard_map/ppermute | solution.py:52
  150.4 7.6 %collective-permute-start.14 = (f32[6,64,128]{2,0,1:T(8,128)S(1)}, f32[6,64,128]{2,0,1:T(8,128)S(1)}, u32[]{:S(2)}, u32[]{:S(2)}) collective-permute-start(f32[6,64,128]{2,0,1:T(8,128)S(1)} %collective-permute-done.10), channel_id=1, source_target_pairs={{0,64},{64,128},{128,192},{192,0},{1,65},{65,129},{129,193},{193,1... | collective-permute-start | bytes 589832 | tf_op jit(solution)/shard_map/ppermute | solution.py:52

commit v2 on v0

v2 whole, which is shorter than its diff:
```python
import functools
import jax
import jax.numpy as jnp
from jax import lax
from jax.experimental import pallas as pl
from jax.experimental.pallas import tpu as pltpu
from jax.sharding import PartitionSpec as P

NX, NY, NZ = 3072, 64, 128
SLAB = 48
HALO = 16
WIDE = SLAB + 2 * HALO
SMAX = 8
TAPS_X, TAPS_Y, TAPS_Z = 31, 31, 61
HALF_X, HALF_Y, HALF_Z = 15, 15, 30
F32, BF16 = jnp.float32, jnp.bfloat16
VMEM_LIMIT = 48 * 1024 * 1024

SMEM_SPEC = pl.BlockSpec(memory_space=pltpu.SMEM)
VMEM_SPEC = pl.BlockSpec(memory_space=pltpu.VMEM)
ANY_SPEC = pl.BlockSpec(memory_space=pl.ANY)
PARAMS = pltpu.CompilerParams(vmem_limit_bytes=VMEM_LIMIT)


def iota(shape, axis):
    return lax.broadcasted_iota(jnp.int32, shape, axis)


def split(value):
    high = value.astype(BF16)
    return high, (value - high.astype(F32)).astype(BF16)


def roll_kernel(shift_ref, source, target, sems):
    shift = shift_ref[0]
    body = NX - 2 * SMAX
    parts = 4
    size = body // parts
    copies = []
    for part in range(parts):
        first = SMAX + part * size
        copies.append(
            pltpu.make_async_copy(
                source.at[pl.ds(first, size)], target.at[pl.ds(first + shift, size)], sems.at[part]
            )
        )
    for edge in range(2 * SMAX):
        row = (NX - SMAX + edge) % NX
        place = lax.rem(row + shift + NX, NX)
        copies.append(
            pltpu.make_async_copy(source.at[pl.ds(row, 1)], target.at[pl.ds(place, 1)], sems.at[parts + edge])
        )
    for copy in copies:
        copy.start()
    for copy in copies:
        copy.wait()


def roll_rows(recorded, shift):
    return pl.pallas_call(
        roll_kernel,
        out_shape=jax.ShapeDtypeStruct((NX, 1, NZ), F32),
        in_specs=[SMEM_SPEC, ANY_SPEC],
        out_specs=ANY_SPEC,
        scratch_shapes=[pltpu.SemaphoreType.DMA((4 + 2 * SMAX,))],
        cost_estimate=pl.CostEstimate(flops=0, bytes_accessed=3 * 2**20, transcendentals=0),
        name="roll_rows",
    )(shift, recorded.reshape(NX, 1, NZ))


def pick_taps(taps_ref, count, tap_index, valid):
    total = taps_ref[0, 0]
    picked = jnp.zeros(tap_index.shape, F32)
    for tap in range(count):
        if tap:
            total = total + taps_ref[0, tap]
        picked = jnp.where(tap_index == tap, taps_ref[0, tap], picked)
    if valid is not None:
        picked = jnp.where(valid, picked, 0.0)
    return picked / jnp.full(tap_index.shape, total, F32)


def packed(matrix, part):
    high, low = split(matrix)
    return jnp.where(part < 2, high.astype(F32), low.astype(F32)).astype(BF16)


def bands_kernel(place_ref, shift_ref, x_ref, y_ref, z_ref, yf_ref, yb_ref, zf_ref, zb_ref, xf_ref, xb_ref):
    shift = shift_ref[0]
    first = place_ref[1] * SLAB
    shape = (NY, 3 * NY)
    row, col = iota(shape, 0), iota(shape, 1)
    part = jnp.where(col >= 2 * NY, 2, jnp.where(col >= NY, 1, 0))
    col = col - part * NY
    yf_ref[...] = packed(pick_taps(y_ref, TAPS_Y, col - row + HALF_Y, None), part)
    yb_ref[...] = packed(pick_taps(y_ref, TAPS_Y, row - col + HALF_Y, None), part)
    shape = (NZ, NZ)
    row, col = iota(shape, 0), iota(shape, 1)
    for ref, index in ((zf_ref, row - col + HALF_Z), (zb_ref, col - row + HALF_Z)):
        high, low = split(pick_taps(z_ref, TAPS_Z, index, None))
        ref[:NZ, :NZ] = high
        ref[NZ:, :NZ] = high
        ref[:NZ, NZ:] = low
        ref[NZ:, NZ:] = jnp.zeros(shape, BF16)
    shape = (SLAB, 3 * WIDE)
    row, col = iota(shape, 0), iota(shape, 1)
    part = jnp.where(col >= 2 * WIDE, 2, jnp.where(col >= WIDE, 1, 0))
    step = col - part * WIDE - HALO - row
    place = first + row
    view_row = place - shift
    view_row = jnp.where(view_row < 0, view_row + NX, view_row)
    view_row = jnp.where(view_row >= NX, view_row - NX, view_row)
    met = view_row + shift + step
    xf_ref[...] = packed(pick_taps(x_ref, TAPS_X, step + HALF_X, (met >= 0) & (met < NX)), part)
    met = place - shift + step
    xb_ref[...] = packed(pick_taps(x_ref, TAPS_X, HALF_X - step, (met >= 0) & (met < NX)), part)


def make_bands(place, shift, psf_x, psf_y, psf_z):
    shapes = [(NY, 3 * NY)] * 2 + [(2 * NZ, 2 * NZ)] * 2 + [(SLAB, 3 * WIDE)] * 2
    return pl.pallas_call(
        bands_kernel,
        out_shape=[jax.ShapeDtypeStruct(shape, BF16) for shape in shapes],
        in_specs=[SMEM_SPEC] * 5,
        out_specs=[VMEM_SPEC] * 6,
        compiler_params=PARAMS,
        name="make_bands",
    )(place, shift, psf_x, psf_y, psf_z)


def blur_z(value, band):
    both = jnp.dot(jnp.concatenate(split(value), axis=1), band, preferred_element_type=F32)
    return both[:, :NZ] + both[:, NZ:]


def blur_rows(band, left, right):
    high, low = split(jnp.concatenate([left, right], axis=1))
    both = jnp.dot(band, jnp.concatenate([high, low, high], axis=0), preferred_element_type=F32)
    return both[:, :NZ], both[:, NZ:]


def forward_kernel(low_ref, own_ref, high_ref, yf_ref, zf_ref, xf_ref, out_ref, blurred, wide):
    for ref, count, base in ((low_ref, HALO, 0), (own_ref, SLAB, HALO), (high_ref, HALO, HALO + SLAB)):

        def along_z(block, carry, ref=ref, base=base):
            rows = ref[pl.ds(block * 8, 8)].reshape(8 * NY, NZ)
            start = pl.multiple_of((base + block * 8) * NY, 8)
            blurred[pl.ds(start, 8 * NY), :] = blur_z(rows, zf_ref[...])
            return carry

        lax.fori_loop(0, count // 8, along_z, 0)

    def along_y(pair, carry):
        start = pl.multiple_of(pair * 2 * NY, 2 * NY)
        left, right = blur_rows(yf_ref[...], blurred[pl.ds(start, NY), :], blurred[pl.ds(start + NY, NY), :])
        wide[pl.ds(start, NY), :] = left
        wide[pl.ds(start + NY, NY), :] = right
        return carry

    lax.fori_loop(0, WIDE // 2, along_y, 0, unroll=4)

    def along_x(pair, carry):
        y = pair * 2
        left, right = blur_rows(
            xf_ref[...], wide[pl.ds(y, WIDE, stride=NY), :], wide[pl.ds(y + 1, WIDE, stride=NY), :]
        )
        out_ref[y] = left
        out_ref[y + 1] = right
        return carry

    lax.fori_loop(0, NY // 2, along_x, 0, unroll=4)


def forward(low, own, high, band_y, band_z, band_x):
    return pl.pallas_call(
        forward_kernel,
        out_shape=jax.ShapeDtypeStruct((NY, SLAB, NZ), F32),
        in_specs=[VMEM_SPEC] * 6,
        out_specs=VMEM_SPEC,
        scratch_shapes=[pltpu.VMEM((WIDE * NY, NZ), F32), pltpu.VMEM((WIDE * NY, NZ), F32)],
        compiler_params=PARAMS,
        cost_estimate=pl.CostEstimate(flops=10**9, bytes_accessed=6 * 2**20, transcendentals=0),
        name="forward",
    )(low, own, high, band_y, band_z, band_x)


def quotient_kernel(chunks, place_ref, shift_ref, box_ref, seen_ref, predicted_ref, yb_ref, zb_ref, *rest):
    out_refs, blurred = rest[:-1], rest[-1]
    step = pl.program_id(0)
    chunk = chunks[0] + step * ((chunks[-1] - chunks[0]) // max(len(chunks) - 1, 1))
    row = place_ref[1] * SLAB + chunk * HALO - shift_ref[0] + iota((HALO, NZ), 0)
    row = jnp.where(row < 0, row + NX, row)
    row = jnp.where(row >= NX, row - NX, row)
    inside = (row >= box_ref[0, 0]) & (row < box_ref[0, 1])

    def along_z(block, carry):
        span = pl.ds(block * 16, 16)
        ratio = jnp.where(inside[None], seen_ref[span] / predicted_ref[span], 1.0)
        start = pl.multiple_of(block * 16 * HALO, 16 * HALO)
        blurred[pl.ds(start, 16 * HALO), :] = blur_z(ratio.reshape(16 * HALO, NZ), zb_ref[...])
        return carry

    lax.fori_loop(0, NY // 16, along_z, 0, unroll=2)

    for index in range(len(chunks)):

        @pl.when(step == index)
        def _(out_ref=out_refs[index]):
            for x in range(0, HALO, 2):
                left, right = blur_rows(
                    yb_ref[...],
                    blurred[pl.ds(x, NY, stride=HALO), :],
                    blurred[pl.ds(x + 1, NY, stride=HALO), :],
                )
                out_ref[x] = left
                out_ref[x + 1] = right


def quotient(chunks, place, shift, box, seen, predicted, band_y, band_z):
    count = len(chunks)
    gap = (chunks[-1] - chunks[0]) // max(count - 1, 1)
    piece = pl.BlockSpec((NY, HALO, NZ), lambda step: (0, chunks[0] + step * gap, 0))
    return pl.pallas_call(
        functools.partial(quotient_kernel, chunks),
        grid=(count,),
        out_shape=[jax.ShapeDtypeStruct((HALO, NY, NZ), F32)] * count,
        in_specs=[SMEM_SPEC] * 3 + [piece, piece] + [VMEM_SPEC] * 2,
        out_specs=[VMEM_SPEC] * count,
        scratch_shapes=[pltpu.VMEM((NY * HALO, NZ), F32)],
        compiler_params=PARAMS,
        cost_estimate=pl.CostEstimate(flops=10**8 * count, bytes_accessed=2**20 * count, transcendentals=0),
        name="quotient",
    )(place, shift, box, seen, predicted, band_y, band_z)


def backward_kernel(parts, place_ref, *rest):
    wide_refs, xb_ref, out_refs = rest[:5], rest[5], rest[6:]
    for out_ref, (turn, half) in zip(out_refs, parts):
        base = lax.rem(place_ref[0] + turn, 4) * 16 + half * 8
        for y in range(0, 8, 2):
            planes = [
                jnp.concatenate([ref[pl.ds(base + y + side, HALO, stride=NY), :] for ref in wide_refs], axis=0)
                for side in (0, 1)
            ]
            left, right = blur_rows(xb_ref[...], *planes)
            out_ref[y] = left
            out_ref[y + 1] = right


def backward(parts, place, wide, band_x):
    return pl.pallas_call(
        functools.partial(backward_kernel, parts),
        out_shape=[jax.ShapeDtypeStruct((8, SLAB, NZ), F32)] * len(parts),
        in_specs=[SMEM_SPEC] + [VMEM_SPEC] * 6,
        out_specs=[VMEM_SPEC] * len(parts),
        compiler_params=PARAMS,
        cost_estimate=pl.CostEstimate(flops=5 * 10**7 * len(parts), bytes_accessed=4 * 2**20, transcendentals=0),
        name="backward",
    )(place, *[piece.reshape(HALO * NY, NZ) for piece in wide], band_x)


def finish_kernel(parts, place_ref, estimate_ref, *rest):
    piece_refs, out_ref = rest[:-1], rest[-1]
    for piece_ref, (turn, half) in zip(piece_refs, parts):
        base = pl.multiple_of(lax.rem(place_ref[0] + turn, 4) * 16 + half * 8, 8)

        def row(x, carry, piece_ref=piece_ref, base=base):
            value = piece_ref[pl.ds(x, 8, stride=SLAB), :]
            out_ref[x, pl.ds(base, 8), :] = estimate_ref[x, pl.ds(base, 8), :] * value * 0.25
            return carry

        lax.fori_loop(0, SLAB, row, 0, unroll=8)


def finish(parts, place, estimate, pieces):
    return pl.pallas_call(
        functools.partial(finish_kernel, parts),
        out_shape=jax.ShapeDtypeStruct((SLAB, NY, NZ), F32),
        in_specs=[SMEM_SPEC] + [VMEM_SPEC] * 9,
        out_specs=VMEM_SPEC,
        compiler_params=PARAMS,
        cost_estimate=pl.CostEstimate(flops=10**6, bytes_accessed=5 * 2**20, transcendentals=0),
        name="finish",
    )(place, estimate, *[piece.reshape(8 * SLAB, NZ) for piece in pieces])


def turn(block, axis, step):
    size = lax.axis_size(axis)
    return lax.ppermute(block, axis, [(i, (i + step) % size) for i in range(size)])


def body(estimate, recorded, psf_x, psf_y, psf_z, view_shifts, view_boxes):
    place = jnp.stack([lax.axis_index("group"), lax.axis_index("block")]).astype(jnp.int32)
    low = turn(estimate[SLAB - HALO :], "block", 1)
    high = turn(estimate[:HALO], "block", -1)
    rolled = roll_rows(recorded, view_shifts).reshape(NY, SLAB, NZ)
    seen = lax.all_to_all(rolled, "block", 0, 0)
    yf, yb, zf, zb, xf, xb = make_bands(place, view_shifts, psf_x, psf_y, psf_z)
    predicted = forward(low, estimate, high, yf, zf, xf)

    args = (place, view_shifts, view_boxes, seen, predicted, yb, zb)
    edge_low, edge_high = quotient((0, 2), *args)
    from_low = turn(edge_high, "block", 1)
    from_high = turn(edge_low, "block", -1)
    (middle,) = quotient((1,), *args)
    wide = (from_low, edge_low, middle, edge_high, from_high)

    far_a, far_b, near_b, near_a = backward(((2, 0), (2, 1), (1, 1), (3, 0)), place, wide, xb)
    far_a, far_b = turn(far_a, "group", 1), turn(far_b, "group", -1)
    near_b, near_a = turn(near_b, "group", 1), turn(near_a, "group", -1)
    next_a, prev_b, own_a, own_b = backward(((1, 0), (3, 1), (0, 0), (0, 1)), place, wide, xb)
    sum_a = turn(next_a + far_a, "group", 1)
    sum_b = turn(prev_b + far_b, "group", -1)
    own_a = own_a + near_a + sum_a
    own_b = own_b + near_b + sum_b
    low_a, high_b = turn(own_a, "group", 1), turn(own_b, "group", -1)
    low_b, high_a = turn(own_b, "group", 1), turn(own_a, "group", -1)
    across_a, across_b = turn(low_a, "group", 1), turn(high_b, "group", -1)
    return finish(
        ((0, 0), (0, 1), (3, 0), (3, 1), (1, 0), (1, 1), (2, 0), (2, 1)),
        place,
        estimate,
        (own_a, own_b, low_a, low_b, high_a, high_b, across_a, across_b),
    )


def solution(mesh):
    return jax.shard_map(
        body,
        mesh=mesh,
        in_specs=(
            P("block", None, None),
            P("group", "block", None, None),
            P("group", None),
            P("group", None),
            P("group", None),
            P("group"),
            P("group", None),
        ),
        out_specs=P("block", None, None),
        check_vma=False,
    )
```

time: 307 us -> 171 us (0.56)
  local copies, waits for them, and re-layouts: 179 us -> 6.19 us
  Pallas kernels: 0 us -> 67.2 us
  matrix products: 16.7 us -> 0 us
  starting transfers between devices: 22.2 us -> 36.2 us
  between operations: 14.4 us -> 0.82 us
  other arithmetic: 12.6 us -> 0.21 us
    gather x7 -> x0, local copies, waits for them, and re-layouts: 174 us -> none  [the longest x3 122 us: band_matrix(): kernel_taps[jnp.clip(tap_index, 0, kernel_taps.shape[0] - 1)]]
    pallas_call x0 -> x8, Pallas kernels: none -> 67.2 us  [the longest x1 48.9 us: roll_rows(): pl.pallas_call(roll_kernel, out_shape=jax.ShapeDtypeStruct((NX, 1, NZ), F...]
    ppermute x4 -> x16, waiting for transfers between devices: 0.01 us -> 59.9 us  [turn(): lax.ppermute(block, axis, [(i, (i + step) % size) for i in range(size)])]
    psum x1 -> x0, waiting for transfers between devices: 59.9 us -> none  [body(): combined = lax.psum(summed, 'group')]
    dot_general x6 -> x0, matrix products: 16.7 us -> none  [the longest x1 5.81 us: body(): jnp.einsum('xe,eyz->xyz', forward_band, extended, precision=lax.Precision...]
    ppermute x4 -> x16, starting transfers between devices: 9.9 us -> 24.1 us  [turn(): lax.ppermute(block, axis, [(i, (i + step) % size) for i in range(size)])]
    unnamed x10 -> x22, local copies, waits for them, and re-layouts: 0.03 us -> 5.12 us
    concatenate x2 -> x0, other arithmetic: 5.04 us -> none  [with_halo(): block = jnp.concatenate([low, block, high], axis=dim)]
  transfers between devices with their start and end apart: 6 -> 17, of which waited for: 1 -> 10; matrix products, arithmetic and copies ran while one was open for 61% -> 1% of each run, Pallas kernels for 0% -> 7%
where the time goes in v2:
time: 171 us; the launch traced here: 170 us
  Pallas kernels  67.2 us (39%)
  waiting for transfers between devices  59.9 us (35%)
  starting transfers between devices  36.2 us (21%)
  local copies, waits for them, and re-layouts  6.19 us (4%)
    ppermute x16, waiting for transfers between devices, turn(): lax.ppermute(block, axis, [(i, (i + step) % size) for i in range(size)])  59.9 us
    pallas_call x1, Pallas kernels, roll_rows(): pl.pallas_call(roll_kernel, out_shape=jax.ShapeDtypeStruct((NX, 1, NZ), F...  48.9 us
    ppermute x16, starting transfers between devices, turn(): lax.ppermute(block, axis, [(i, (i + step) % size) for i in range(size)])  24.1 us
    all_to_all x1, starting transfers between devices, body(): seen = lax.all_to_all(rolled, 'block', 0, 0)  12.1 us
    pallas_call x1, Pallas kernels, forward(): pl.pallas_call(forward_kernel, out_shape=jax.ShapeDtypeStruct((NY, SLAB,...  7.07 us
    unnamed x22, local copies, waits for them, and re-layouts  5.12 us
    pallas_call x2, Pallas kernels, quotient(): pl.pallas_call(functools.partial(quotient_kernel, chunks), grid=(count,),...  3.68 us
  transfers between devices with their start and end apart: 17, of which 10 were waited for; matrix products, arithmetic and copies ran while one was open for 1% of the time, Pallas kernels for 7%

profile of v2, /device:TPU:24, one launch (start us, length us, event | category | flops | bytes accessed | tf_op | source)
XLA Modules:
  0.0 170.5 jit_solution(10280409009109186702)
XLA Ops:
  0.7 48.9 %roll_rows.1 = f32[3072,1,128]{2,1,0:T(1,128)} custom-call(s32[1]{0:T(128)S(6)} %copy.8.shift_ref, f32[3072,1,128]{2,1,0:T(1,128)} %bitcast.36), custom_call_target="tpu_custom_call" | custom-call | bytes 3145728 | tf_op jit(solution)/shard_map/roll_rows/pallas_call | solution.py:60
  49.6 12.1 %all-to-all-start = ((f32[64,48,128]{2,1,0:T(8,128)}), f32[64,48,128]{2,1,0:T(8,128)S(1)}, u32[]{:S(2)}, u32[]{:S(2)}) async-start(f32[64,48,128]{2,1,0:T(8,128)} %bitcast.35), calls=%async_computation | async-start | bytes 3145728 | tf_op jit(solution)/shard_map/all_to_all | solution.py:297
  62.8 4.9 %collective-permute-start.1 = (f32[16,64,128]{2,1,0:T(8,128)}, f32[16,64,128]{2,1,0:T(8,128)S(1)}, u32[]{:S(2)}, u32[]{:S(2)}) collective-permute-start(f32[16,64,128]{2,1,0:T(8,128)} %get-tuple-element.37), channel_id=1, source_target_pairs={{0,63},{1,0},{2,1},{3,2},{4,3},{5,4},{6,5},{7,6},{8,7},{9,8},{10,9... | collective-permute-start | bytes 1572872 | tf_op jit(solution)/shard_map/ppermute | solution.py:289
  67.8 2.0 %make_bands.1 = (bf16[64,192]{1,0:T(8,128)(2,1)S(1)}, bf16[64,192]{1,0:T(8,128)(2,1)S(1)}, bf16[256,256]{1,0:T(8,128)(2,1)S(1)}, bf16[256,256]{1,0:T(8,128)(2,1)...) custom-call(s32[2]{0:T(128)S(1)} %pad_add_fusion.place_ref, s32[1]{0:T(128)S(6)} %copy.8.shift_ref, ...), custom_call_target="tpu_custom_call" | custom-call | tf_op jit(solution)/shard_map/make_bands/pallas_call | solution.py:121
  69.8 31.7 %collective-permute-done.1.high_ref = f32[16,64,128]{2,1,0:T(8,128)S(1)} collective-permute-done((f32[16,64,128]{2,1,0:T(8,128)}, f32[16,64,128]{2,1,0:T(8,128)S(1)}, u32[]{:S(2)}, u32[]{:S(2)}) %collective-permute-start.1) | collective-permute-done | bytes 524320 | tf_op jit(solution)/shard_map/ppermute | solution.py:289
  102.3 4.7 %collective-permute-done.low_ref = f32[16,64,128]{2,1,0:T(8,128)S(1)} collective-permute-done((f32[16,64,128]{2,1,0:T(8,128)}, f32[16,64,128]{2,1,0:T(8,128)S(1)}, u32[]{:S(2)}, u32[]{:S(2)}) %collective-permute-start) | collective-permute-done | bytes 524320 | tf_op jit(solution)/shard_map/ppermute | solution.py:289
  111.3 7.1 %forward.1.predicted_ref = f32[64,48,128]{2,1,0:T(8,128)S(1)} custom-call(f32[16,64,128]{2,1,0:T(8,128)S(1)} %copy-done.6, f32[48,64,128]{2,1,0:T(8,128)S(1)} %copy-done.1, f32[16,64,128]{2,1,0:T(8,128)S(1)} %copy-done.4, bf16[64,192]{1,0:T(8,128)(2,1)S(1)} %get-tuple-element.21.yf_ref, bf16[256,256]{1,0:T(8,128)(2,1)S(1)} %get-tuple-element.22.zf_ref, ...), custom_call_target="tpu_custom_call" | custom-call | flops 1000000000 | bytes 6291456 | tf_op jit(solution)/shard_map/forward/pallas_call | solution.py:175
  118.4 2.3 %quotient.2 = (f32[16,64,128]{2,1,0:T(8,128)S(1)}, f32[16,64,128]{2,1,0:T(8,128)S(1)}) custom-call(s32[2]{0:T(128)S(1)} %pad_add_fusion.place_ref, s32[1]{0:T(128)S(6)} %copy.8.shift_ref, s32[1,2]{1,0:T(1,128)S(1)} %copy-done.7, f32[64,48,128]{2,1,0:T(8,128)S(1)} %all-to-all-done.seen_ref, f32[64,48,128]{2,1,0:T(8,128)S(1)} %forward.1.predicted_ref, ...), custom_call_target="tpu_custom_call" | custom-call | flops 200000000 | bytes 2097152 | tf_op jit(solution)/shard_map/quotient/pallas_call | solution.py:223
  120.9 5.1 %collective-permute-start.3 = (f32[16,64,128]{2,1,0:T(8,128)S(1)}, f32[16,64,128]{2,1,0:T(8,128)S(1)}, u32[]{:S(2)}, u32[]{:S(2)}) collective-permute-start(f32[16,64,128]{2,1,0:T(8,128)S(1)} %get-tuple-element.27), channel_id=1, source_target_pairs={{0,63},{1,0},{2,1},{3,2},{4,3},{5,4},{6,5},{7,6},{8,7},{9,8},{10,9... | collective-permute-start | bytes 1572872 | tf_op jit(solution)/shard_map/ppermute | solution.py:289
  127.3 5.5 %collective-permute-done.2 = f32[16,64,128]{2,1,0:T(8,128)S(1)} collective-permute-done((f32[16,64,128]{2,1,0:T(8,128)S(1)}, f32[16,64,128]{2,1,0:T(8,128)S(1)}, u32[]{:S(2)}, u32[]{:S(2)}) %collective-permute-start.2) | collective-permute-done | bytes 524320 | tf_op jit(solution)/shard_map/ppermute | solution.py:289
  132.8 1.5 backward.3
  134.6 1.8 %collective-permute-start.8 = (f32[8,48,128]{2,1,0:T(8,128)S(1)}, f32[8,48,128]{2,1,0:T(8,128)S(1)}, u32[]{:S(2)}, u32[]{:S(2)}) collective-permute-start(f32[8,48,128]{2,1,0:T(8,128)S(1)} %get-tuple-element.36), channel_id=1, source_target_pairs={{0,192},{64,0},{128,64},{192,128},{1,193},{65,1},{129,65},{193,129... | collective-permute-start | bytes 589832 | tf_op jit(solution)/shard_map/ppermute | solution.py:289
  138.8 3.5 %collective-permute-done.5 = f32[8,48,128]{2,1,0:T(8,128)S(1)} collective-permute-done((f32[8,48,128]{2,1,0:T(8,128)S(1)}, f32[8,48,128]{2,1,0:T(8,128)S(1)}, u32[]{:S(2)}, u32[]{:S(2)}) %collective-permute-start.5) | collective-permute-done | bytes 196640 | tf_op jit(solution)/shard_map/ppermute | solution.py:289
  142.2 1.6 collective-permute-start.6
  144.3 1.6 collective-permute-start.9
  146.0 3.9 %collective-permute-done.6 = f32[8,48,128]{2,1,0:T(8,128)S(1)} collective-permute-done((f32[8,48,128]{2,1,0:T(8,128)S(1)}, f32[8,48,128]{2,1,0:T(8,128)S(1)}, u32[]{:S(2)}, u32[]{:S(2)}) %collective-permute-start.6) | collective-permute-done | bytes 196640 | tf_op jit(solution)/shard_map/ppermute | solution.py:289
  149.9 2.1 %collective-permute-start.10 = (f32[8,48,128]{2,1,0:T(8,128)S(1)}, f32[8,48,128]{2,1,0:T(8,128)S(1)}, u32[]{:S(2)}, u32[]{:S(2)}) collective-permute-start(f32[8,48,128]{2,1,0:T(8,128)S(1)} %add_add_fusion.1), channel_id=1, source_target_pairs={{0,64},{64,128},{128,192},{192,0},{1,65},{65,129},{129,193},{193,1... | collective-permute-start | bytes 589832 | tf_op jit(solution)/shard_map/ppermute | solution.py:289
  152.0 2.1 %collective-permute-done.7 = f32[8,48,128]{2,1,0:T(8,128)S(1)} collective-permute-done((f32[8,48,128]{2,1,0:T(8,128)S(1)}, f32[8,48,128]{2,1,0:T(8,128)S(1)}, u32[]{:S(2)}, u32[]{:S(2)}) %collective-permute-start.7) | collective-permute-done | bytes 196640 | tf_op jit(solution)/shard_map/ppermute | solution.py:289
  154.5 3.0 %collective-permute-start.11 = (f32[8,48,128]{2,1,0:T(8,128)S(1)}, f32[8,48,128]{2,1,0:T(8,128)S(1)}, u32[]{:S(2)}, u32[]{:S(2)}) collective-permute-start(f32[8,48,128]{2,1,0:T(8,128)S(1)} %add_add_fusion), channel_id=1, source_target_pairs={{0,64},{64,128},{128,192},{192,0},{1,65},{65,129},{129,193},{193,1... | collective-permute-start | bytes 589832 | tf_op jit(solution)/shard_map/ppermute | solution.py:289
  157.5 1.9 %collective-permute-start.14 = (f32[8,48,128]{2,1,0:T(8,128)S(1)}, f32[8,48,128]{2,1,0:T(8,128)S(1)}, u32[]{:S(2)}, u32[]{:S(2)}) collective-permute-start(f32[8,48,128]{2,1,0:T(8,128)S(1)} %collective-permute-done.10), channel_id=1, source_target_pairs={{0,64},{64,128},{128,192},{192,0},{1,65},{65,129},{129,193},{193,1... | collective-permute-start | bytes 589832 | tf_op jit(solution)/shard_map/ppermute | solution.py:289
  159.5 1.6 collective-permute-done.13
  161.1 2.1 %collective-permute-done.12 = f32[8,48,128]{2,1,0:T(8,128)S(1)} collective-permute-done((f32[8,48,128]{2,1,0:T(8,128)S(1)}, f32[8,48,128]{2,1,0:T(8,128)S(1)}, u32[]{:S(2)}, u32[]{:S(2)}) %collective-permute-start.12) | collective-permute-done | bytes 196640 | tf_op jit(solution)/shard_map/ppermute | solution.py:289
  163.4 4.6 %collective-permute-done.15 = f32[8,48,128]{2,1,0:T(8,128)S(1)} collective-permute-done((f32[8,48,128]{2,1,0:T(8,128)S(1)}, f32[8,48,128]{2,1,0:T(8,128)S(1)}, u32[]{:S(2)}, u32[]{:S(2)}) %collective-permute-start.15) | collective-permute-done | bytes 196640 | tf_op jit(solution)/shard_map/ppermute | solution.py:289
  168.0 2.5 %finish.1 = f32[48,64,128]{2,1,0:T(8,128)} custom-call(s32[2]{0:T(128)S(1)} %pad_add_fusion.place_ref, f32[48,64,128]{2,1,0:T(8,128)S(1)} %copy-done.2, f32[384,128]{1,0:T(8,128)S(1)} %bitcast.27, f32[384,128]{1,0:T(8,128)S(1)} %bitcast.28, f32[384,128]{1,0:T(8,128)S(1)} %bitcast.29, f32[384,128]{1,0:T(8,128)S(1)} %bitcast.32, f32[384,128]{1,0:T(8,128)S(1)} %bitcast.31, ...), custom_call_target="tpu_custom_call" | custom-call | flops 1000000 | bytes 5242880 | tf_op jit(solution)/shard_map/finish/pallas_call | solution.py:276
  (46 shorter events, 11.5 us)
Async XLA Ops:
  49.6 12.1 %copy-start = (f32[48,64,128]{2,1,0:T(8,128)S(1)}, f32[48,64,128]{2,1,0:T(8,128)}, u32[]{:S(2)}) copy-start(f32[48,64,128]{2,1,0:T(8,128)} %estimate_ref.1) | copy-start | bytes 4718596
  49.6 68.8 %all-to-all-start = ((f32[64,48,128]{2,1,0:T(8,128)}), f32[64,48,128]{2,1,0:T(8,128)S(1)}, u32[]{:S(2)}, u32[]{:S(2)}) async-start(f32[64,48,128]{2,1,0:T(8,128)} %bitcast.35), calls=%async_computation | async-start | bytes 3145728 | tf_op jit(solution)/shard_map/all_to_all | solution.py:297
  61.7 6.1 %copy-start.8 = (f32[1,31]{1,0:T(1,128)S(1)}, f32[1,31]{1,0:T(1,128)}, u32[]{:S(2)}) copy-start(f32[1,31]{1,0:T(1,128)} %x_ref.1) | copy-start | bytes 376
  61.7 6.1 %copy-start.9 = (f32[1,31]{1,0:T(1,128)S(1)}, f32[1,31]{1,0:T(1,128)}, u32[]{:S(2)}) copy-start(f32[1,31]{1,0:T(1,128)} %y_ref.1) | copy-start | bytes 376
  61.7 6.1 %copy-start.10 = (f32[1,61]{1,0:T(1,128)S(1)}, f32[1,61]{1,0:T(1,128)}, u32[]{:S(2)}) copy-start(f32[1,61]{1,0:T(1,128)} %z_ref.1) | copy-start | bytes 736
  62.8 38.7 %collective-permute-start.1 = (f32[16,64,128]{2,1,0:T(8,128)}, f32[16,64,128]{2,1,0:T(8,128)S(1)}, u32[]{:S(2)}, u32[]{:S(2)}) collective-permute-start(f32[16,64,128]{2,1,0:T(8,128)} %get-tuple-element.37), channel_id=1, source_target_pairs={{0,63},{1,0},{2,1},{3,2},{4,3},{5,4},{6,5},{7,6},{8,7},{9,8},{10,9... | collective-permute-start | bytes 1572872 | tf_op jit(solution)/shard_map/ppermute | solution.py:289
  67.8 39.3 %collective-permute-start = (f32[16,64,128]{2,1,0:T(8,128)}, f32[16,64,128]{2,1,0:T(8,128)S(1)}, u32[]{:S(2)}, u32[]{:S(2)}) collective-permute-start(f32[16,64,128]{2,1,0:T(8,128)} %get-tuple-element.38), channel_id=1, source_target_pairs={{0,1},{1,2},{2,3},{3,4},{4,5},{5,6},{6,7},{7,8},{8,9},{9,10},{10,1... | collective-permute-start | bytes 1572872 | tf_op jit(solution)/shard_map/ppermute | solution.py:289
  107.8 1.4 copy-start.1
  111.3 7.1 %copy-start.7 = (s32[1,2]{1,0:T(1,128)S(1)}, s32[1,2]{1,0:T(1,128)}, u32[]{:S(2)}) copy-start(s32[1,2]{1,0:T(1,128)} %box_ref.3) | copy-start | bytes 28
  120.8 12.0 %collective-permute-start.2 = (f32[16,64,128]{2,1,0:T(8,128)S(1)}, f32[16,64,128]{2,1,0:T(8,128)S(1)}, u32[]{:S(2)}, u32[]{:S(2)}) collective-permute-start(f32[16,64,128]{2,1,0:T(8,128)S(1)} %get-tuple-element.26), channel_id=1, source_target_pairs={{0,1},{1,2},{2,3},{3,4},{4,5},{5,6},{6,7},{7,8},{8,9},{9,10},{10,1... | collective-permute-start | bytes 1572872 | tf_op jit(solution)/shard_map/ppermute | solution.py:289
  120.9 11.9 %collective-permute-start.3 = (f32[16,64,128]{2,1,0:T(8,128)S(1)}, f32[16,64,128]{2,1,0:T(8,128)S(1)}, u32[]{:S(2)}, u32[]{:S(2)}) collective-permute-start(f32[16,64,128]{2,1,0:T(8,128)S(1)} %get-tuple-element.27), channel_id=1, source_target_pairs={{0,63},{1,0},{2,1},{3,2},{4,3},{5,4},{6,5},{7,6},{8,7},{9,8},{10,9... | collective-permute-start | bytes 1572872 | tf_op jit(solution)/shard_map/ppermute | solution.py:289
  134.3 7.9 %collective-permute-start.5 = (f32[8,48,128]{2,1,0:T(8,128)S(1)}, f32[8,48,128]{2,1,0:T(8,128)S(1)}, u32[]{:S(2)}, u32[]{:S(2)}) collective-permute-start(f32[8,48,128]{2,1,0:T(8,128)S(1)} %get-tuple-element.32), channel_id=1, source_target_pairs={{0,64},{64,128},{128,192},{192,0},{1,65},{65,129},{129,193},{193,1... | collective-permute-start | bytes 589832 | tf_op jit(solution)/shard_map/ppermute | solution.py:289
  134.6 9.7 %collective-permute-start.8 = (f32[8,48,128]{2,1,0:T(8,128)S(1)}, f32[8,48,128]{2,1,0:T(8,128)S(1)}, u32[]{:S(2)}, u32[]{:S(2)}) collective-permute-start(f32[8,48,128]{2,1,0:T(8,128)S(1)} %get-tuple-element.36), channel_id=1, source_target_pairs={{0,192},{64,0},{128,64},{192,128},{1,193},{65,1},{129,65},{193,129... | collective-permute-start | bytes 589832 | tf_op jit(solution)/shard_map/ppermute | solution.py:289
  137.9 30.1 %copy-start.2 = (f32[48,64,128]{2,1,0:T(8,128)S(1)}, f32[48,64,128]{2,1,0:T(8,128)}, u32[]{:S(2)}) copy-start(f32[48,64,128]{2,1,0:T(8,128)} %estimate_ref.1) | copy-start | bytes 4718596
  137.9 8.1 %collective-permute-start.4 = (f32[8,48,128]{2,1,0:T(8,128)S(1)}, f32[8,48,128]{2,1,0:T(8,128)S(1)}, u32[]{:S(2)}, u32[]{:S(2)}) collective-permute-start(f32[8,48,128]{2,1,0:T(8,128)S(1)} %get-tuple-element.30), channel_id=1, source_target_pairs={{0,192},{64,0},{128,64},{192,128},{1,193},{65,1},{129,65},{193,129... | collective-permute-start | bytes 589832 | tf_op jit(solution)/shard_map/ppermute | solution.py:289
  142.2 7.6 %collective-permute-start.6 = (f32[8,48,128]{2,1,0:T(8,128)S(1)}, f32[8,48,128]{2,1,0:T(8,128)S(1)}, u32[]{:S(2)}, u32[]{:S(2)}) collective-permute-start(f32[8,48,128]{2,1,0:T(8,128)S(1)} %add.19), channel_id=1, source_target_pairs={{0,64},{64,128},{128,192},{192,0},{1,65},{65,129},{129,193},{193,1... | collective-permute-start | bytes 589832 | tf_op jit(solution)/shard_map/ppermute | solution.py:289
  143.8 10.2 %collective-permute-start.7 = (f32[8,48,128]{2,1,0:T(8,128)S(1)}, f32[8,48,128]{2,1,0:T(8,128)S(1)}, u32[]{:S(2)}, u32[]{:S(2)}) collective-permute-start(f32[8,48,128]{2,1,0:T(8,128)S(1)} %get-tuple-element.34), channel_id=1, source_target_pairs={{0,64},{64,128},{128,192},{192,0},{1,65},{65,129},{129,193},{193,1... | collective-permute-start | bytes 589832 | tf_op jit(solution)/shard_map/ppermute | solution.py:289
  144.3 9.8 %collective-permute-start.9 = (f32[8,48,128]{2,1,0:T(8,128)S(1)}, f32[8,48,128]{2,1,0:T(8,128)S(1)}, u32[]{:S(2)}, u32[]{:S(2)}) collective-permute-start(f32[8,48,128]{2,1,0:T(8,128)S(1)} %add.22), channel_id=1, source_target_pairs={{0,192},{64,0},{128,64},{192,128},{1,193},{65,1},{129,65},{193,129... | collective-permute-start | bytes 589832 | tf_op jit(solution)/shard_map/ppermute | solution.py:289
  149.9 7.6 %collective-permute-start.10 = (f32[8,48,128]{2,1,0:T(8,128)S(1)}, f32[8,48,128]{2,1,0:T(8,128)S(1)}, u32[]{:S(2)}, u32[]{:S(2)}) collective-permute-start(f32[8,48,128]{2,1,0:T(8,128)S(1)} %add_add_fusion.1), channel_id=1, source_target_pairs={{0,64},{64,128},{128,192},{192,0},{1,65},{65,129},{129,193},{193,1... | collective-permute-start | bytes 589832 | tf_op jit(solution)/shard_map/ppermute | solution.py:289
  154.1 7.0 %collective-permute-start.13 = (f32[8,48,128]{2,1,0:T(8,128)S(1)}, f32[8,48,128]{2,1,0:T(8,128)S(1)}, u32[]{:S(2)}, u32[]{:S(2)}) collective-permute-start(f32[8,48,128]{2,1,0:T(8,128)S(1)} %add_add_fusion), channel_id=1, source_target_pairs={{0,192},{64,0},{128,64},{192,128},{1,193},{65,1},{129,65},{193,129... | collective-permute-start | bytes 589832 | tf_op jit(solution)/shard_map/ppermute | solution.py:289
  154.2 9.0 %collective-permute-start.12 = (f32[8,48,128]{2,1,0:T(8,128)S(1)}, f32[8,48,128]{2,1,0:T(8,128)S(1)}, u32[]{:S(2)}, u32[]{:S(2)}) collective-permute-start(f32[8,48,128]{2,1,0:T(8,128)S(1)} %add_add_fusion.1), channel_id=1, source_target_pairs={{0,192},{64,0},{128,64},{192,128},{1,193},{65,1},{129,65},{193,129... | collective-permute-start | bytes 589832 | tf_op jit(solution)/shard_map/ppermute | solution.py:289
  154.5 8.7 %collective-permute-start.11 = (f32[8,48,128]{2,1,0:T(8,128)S(1)}, f32[8,48,128]{2,1,0:T(8,128)S(1)}, u32[]{:S(2)}, u32[]{:S(2)}) collective-permute-start(f32[8,48,128]{2,1,0:T(8,128)S(1)} %add_add_fusion), channel_id=1, source_target_pairs={{0,64},{64,128},{128,192},{192,0},{1,65},{65,129},{129,193},{193,1... | collective-permute-start | bytes 589832 | tf_op jit(solution)/shard_map/ppermute | solution.py:289
  157.5 5.8 %collective-permute-start.14 = (f32[8,48,128]{2,1,0:T(8,128)S(1)}, f32[8,48,128]{2,1,0:T(8,128)S(1)}, u32[]{:S(2)}, u32[]{:S(2)}) collective-permute-start(f32[8,48,128]{2,1,0:T(8,128)S(1)} %collective-permute-done.10), channel_id=1, source_target_pairs={{0,64},{64,128},{128,192},{192,0},{1,65},{65,129},{129,193},{193,1... | collective-permute-start | bytes 589832 | tf_op jit(solution)/shard_map/ppermute | solution.py:289
  161.1 6.9 %collective-permute-start.15 = (f32[8,48,128]{2,1,0:T(8,128)S(1)}, f32[8,48,128]{2,1,0:T(8,128)S(1)}, u32[]{:S(2)}, u32[]{:S(2)}) collective-permute-start(f32[8,48,128]{2,1,0:T(8,128)S(1)} %collective-permute-done.13), channel_id=1, source_target_pairs={{0,192},{64,0},{128,64},{192,128},{1,193},{65,1},{129,65},{193,129... | collective-permute-start | bytes 589832 | tf_op jit(solution)/shard_map/ppermute | solution.py:289
  (4 other events, 3.7 us)

commit v3 on v2

--- a/solution.py
+++ b/solution.py
@@ -31,41 +31,31 @@
     return high, (value - high.astype(F32)).astype(BF16)
 
 
-def roll_kernel(shift_ref, source, target, sems):
-    shift = shift_ref[0]
-    body = NX - 2 * SMAX
-    parts = 4
-    size = body // parts
-    copies = []
-    for part in range(parts):
-        first = SMAX + part * size
-        copies.append(
-            pltpu.make_async_copy(
-                source.at[pl.ds(first, size)], target.at[pl.ds(first + shift, size)], sems.at[part]
-            )
-        )
-    for edge in range(2 * SMAX):
-        row = (NX - SMAX + edge) % NX
-        place = lax.rem(row + shift + NX, NX)
-        copies.append(
-            pltpu.make_async_copy(source.at[pl.ds(row, 1)], target.at[pl.ds(place, 1)], sems.at[parts + edge])
-        )
-    for copy in copies:
-        copy.start()
-    for copy in copies:
-        copy.wait()
+def roll_kernel(shift_ref, source, target, padded):
+    padded[pl.ds(SMAX, NX), :] = source[...]
+    padded[pl.ds(0, SMAX), :] = source[pl.ds(NX - SMAX, SMAX), :]
+    padded[pl.ds(SMAX + NX, SMAX), :] = source[pl.ds(0, SMAX), :]
+    start = SMAX - shift_ref[0]
+
+    def move(block, carry):
+        base = block * 128
+        target[pl.ds(pl.multiple_of(base, 128), 128), :] = padded[pl.ds(start + base, 128), :]
+        return carry
+
+    lax.fori_loop(0, NX // 128, move, 0)
 
 
 def roll_rows(recorded, shift):
     return pl.pallas_call(
         roll_kernel,
-        out_shape=jax.ShapeDtypeStruct((NX, 1, NZ), F32),
-        in_specs=[SMEM_SPEC, ANY_SPEC],
-        out_specs=ANY_SPEC,
-        scratch_shapes=[pltpu.SemaphoreType.DMA((4 + 2 * SMAX,))],
-        cost_estimate=pl.CostEstimate(flops=0, bytes_accessed=3 * 2**20, transcendentals=0),
+        out_shape=jax.ShapeDtypeStruct((NX, NZ), F32),
+        in_specs=[SMEM_SPEC, VMEM_SPEC],
+        out_specs=VMEM_SPEC,
+        scratch_shapes=[pltpu.VMEM((NX + 2 * SMAX, NZ), F32)],
+        compiler_params=PARAMS,
+        cost_estimate=pl.CostEstimate(flops=10**6, bytes_accessed=3 * 2**20, transcendentals=0),
         name="roll_rows",
-    )(shift, recorded.reshape(NX, 1, NZ))
+    )(shift, recorded.reshape(NX, NZ))
 
 
 def pick_taps(taps_ref, count, tap_index, valid):
@@ -179,7 +169,7 @@
         out_specs=VMEM_SPEC,
         scratch_shapes=[pltpu.VMEM((WIDE * NY, NZ), F32), pltpu.VMEM((WIDE * NY, NZ), F32)],
         compiler_params=PARAMS,
-        cost_estimate=pl.CostEstimate(flops=10**9, bytes_accessed=6 * 2**20, transcendentals=0),
+        cost_estimate=pl.CostEstimate(flops=2 * 10**11, bytes_accessed=6 * 2**20, transcendentals=0),
         name="forward",
     )(low, own, high, band_y, band_z, band_x)
 

time: 171 us -> 111 us (0.65)
  Pallas kernels: 67.2 us -> 20.6 us
  waiting for transfers between devices: 59.9 us -> 46.8 us
    pallas_call x1, Pallas kernels: 48.9 us -> 1.44 us  [roll_rows(): pl.pallas_call(roll_kernel, out_shape=jax.ShapeDtypeStruct((NX, NZ), F32)...]
    ppermute x16, waiting for transfers between devices: 59.9 us -> 20.2 us  [turn(): lax.ppermute(block, axis, [(i, (i + step) % size) for i in range(size)])]
    all_to_all x1, waiting for transfers between devices: 0.01 us -> 26.6 us  [body(): seen = lax.all_to_all(rolled, 'block', 0, 0)]
    all_to_all x1, starting transfers between devices: 12.1 us -> 7.72 us  [body(): seen = lax.all_to_all(rolled, 'block', 0, 0)]
    ppermute x16, starting transfers between devices: 24.1 us -> 26.9 us  [turn(): lax.ppermute(block, axis, [(i, (i + step) % size) for i in range(size)])]
    unnamed x22 -> x24, local copies, waits for them, and re-layouts: 5.12 us -> 3.69 us
  transfers between devices with their start and end apart: 17 -> 17, of which waited for: 10 -> 11; matrix products, arithmetic and copies ran while one was open for 1% -> 0% of each run, Pallas kernels for 7% -> 13%
where the time goes in v3:
time: 111 us; the launch traced here: 109 us
  waiting for transfers between devices  46.8 us (42%)
  starting transfers between devices  34.6 us (31%)
  Pallas kernels  20.6 us (19%)
  local copies, waits for them, and re-layouts  6.11 us (6%)
    ppermute x16, starting transfers between devices, turn(): lax.ppermute(block, axis, [(i, (i + step) % size) for i in range(size)])  26.9 us
    all_to_all x1, waiting for transfers between devices, body(): seen = lax.all_to_all(rolled, 'block', 0, 0)  26.6 us
    ppermute x16, waiting for transfers between devices, turn(): lax.ppermute(block, axis, [(i, (i + step) % size) for i in range(size)])  20.2 us
    all_to_all x1, starting transfers between devices, body(): seen = lax.all_to_all(rolled, 'block', 0, 0)  7.72 us
    pallas_call x1, Pallas kernels, forward(): pl.pallas_call(forward_kernel, out_shape=jax.ShapeDtypeStruct((NY, SLAB,...  7.05 us
    pallas_call x2, Pallas kernels, quotient(): pl.pallas_call(functools.partial(quotient_kernel, chunks), grid=(count,),...  4.61 us
    unnamed x24, local copies, waits for them, and re-layouts  3.69 us
    pallas_call x2, Pallas kernels, backward(): pl.pallas_call(functools.partial(backward_kernel, parts), out_shape=[jax....  3.02 us
  transfers between devices with their start and end apart: 17, of which 11 were waited for; matrix products, arithmetic and copies ran while one was open for 0% of the time, Pallas kernels for 13%

profile of v3, /device:TPU:24, one launch (start us, length us, event | category | flops | bytes accessed | tf_op | source)
XLA Modules:
  0.0 109.1 jit_solution(8134747584256483112)
XLA Ops:
  0.0 2.4 %fusion = (f32[16,64,128]{2,1,0:T(8,128)}, f32[16,64,128]{2,1,0:T(8,128)}) fusion(f32[48,64,128]{2,1,0:T(8,128)} %estimate_ref.1), kind=kLoop, calls=%fused_computation.3 | loop fusion | bytes 2097152 | tf_op jit(solution)/shard_map/slice | solution.py:285
  2.4 7.5 %collective-permute-start.1 = (f32[16,64,128]{2,1,0:T(8,128)}, f32[16,64,128]{2,1,0:T(8,128)S(1)}, u32[]{:S(2)}, u32[]{:S(2)}) collective-permute-start(f32[16,64,128]{2,1,0:T(8,128)} %get-tuple-element.37), channel_id=1, source_target_pairs={{0,63},{1,0},{2,1},{3,2},{4,3},{5,4},{6,5},{7,6},{8,7},{9,8},{10,9... | collective-permute-start | bytes 1572872 | tf_op jit(solution)/shard_map/ppermute | solution.py:279
  10.6 1.4 %roll_rows.1 = f32[3072,128]{1,0:T(8,128)} custom-call(s32[1]{0:T(128)S(6)} %copy.8.shift_ref, f32[3072,128]{1,0:T(8,128)S(1)} %bitcast.27), custom_call_target="tpu_custom_call" | custom-call | flops 1000000 | bytes 3145728 | tf_op jit(solution)/shard_map/roll_rows/pallas_call | solution.py:49
  12.0 7.7 %all-to-all-start = ((f32[64,48,128]{2,1,0:T(8,128)}), f32[64,48,128]{2,1,0:T(8,128)}, u32[]{:S(2)}, u32[]{:S(2)}) async-start(f32[64,48,128]{2,1,0:T(8,128)} %bitcast.3), calls=%async_computation | async-start | bytes 3145728 | tf_op jit(solution)/shard_map/all_to_all | solution.py:287
  19.9 2.0 %make_bands.1 = (bf16[64,192]{1,0:T(8,128)(2,1)S(1)}, bf16[64,192]{1,0:T(8,128)(2,1)S(1)}, bf16[256,256]{1,0:T(8,128)(2,1)S(1)}, bf16[256,256]{1,0:T(8,128)(2,1)...) custom-call(s32[2]{0:T(128)S(1)} %pad_add_fusion.place_ref, s32[1]{0:T(128)S(6)} %copy.8.shift_ref, ...), custom_call_target="tpu_custom_call" | custom-call | tf_op jit(solution)/shard_map/make_bands/pallas_call | solution.py:111
  25.5 7.1 %forward.1.predicted_ref = f32[64,48,128]{2,1,0:T(8,128)S(1)} custom-call(f32[16,64,128]{2,1,0:T(8,128)S(1)} %copy-done.11, f32[48,64,128]{2,1,0:T(8,128)S(1)} %copy-done, f32[16,64,128]{2,1,0:T(8,128)S(1)} %copy-done.9, bf16[64,192]{1,0:T(8,128)(2,1)S(1)} %get-tuple-element.21.yf_ref, bf16[256,256]{1,0:T(8,128)(2,1)S(1)} %get-tuple-element.22.zf_ref, ...), custom_call_target="tpu_custom_call" | custom-call | flops 199999995904 | bytes 6291456 | tf_op jit(solution)/shard_map/forward/pallas_call | solution.py:165
  32.6 26.6 %all-to-all-done.seen_ref = f32[64,48,128]{2,1,0:T(8,128)} async-done(((f32[64,48,128]{2,1,0:T(8,128)}), f32[64,48,128]{2,1,0:T(8,128)}, u32[]{:S(2)}, u32[]{:S(2)}) %all-to-all-start) | async-done | bytes 1572896 | tf_op jit(solution)/shard_map/all_to_all | solution.py:287
  59.1 2.7 %quotient.2 = (f32[16,64,128]{2,1,0:T(8,128)S(1)}, f32[16,64,128]{2,1,0:T(8,128)S(1)}) custom-call(s32[2]{0:T(128)S(1)} %copy-done.3, s32[1]{0:T(128)S(6)} %copy.8.shift_ref, s32[1,2]{1,0:T(1,128)S(1)} %copy-done.4, f32[64,48,128]{2,1,0:T(8,128)} %all-to-all-done.seen_ref, f32[64,48,128]{2,1,0:T(8,128)S(1)} %forward.1.predicted_ref, ...), custom_call_target="tpu_custom_call" | custom-call | flops 200000000 | bytes 2097152 | tf_op jit(solution)/shard_map/quotient/pallas_call | solution.py:213
  62.3 4.7 %collective-permute-start.3 = (f32[16,64,128]{2,1,0:T(8,128)S(1)}, f32[16,64,128]{2,1,0:T(8,128)S(1)}, u32[]{:S(2)}, u32[]{:S(2)}) collective-permute-start(f32[16,64,128]{2,1,0:T(8,128)S(1)} %get-tuple-element.27), channel_id=1, source_target_pairs={{0,63},{1,0},{2,1},{3,2},{4,3},{5,4},{6,5},{7,6},{8,7},{9,8},{10,9... | collective-permute-start | bytes 1572872 | tf_op jit(solution)/shard_map/ppermute | solution.py:279
  67.0 1.9 %quotient.3 = f32[16,64,128]{2,1,0:T(8,128)S(1)} custom-call(s32[2]{0:T(128)S(1)} %copy-done.3, s32[1]{0:T(128)S(6)} %copy.8.shift_ref, s32[1,2]{1,0:T(1,128)S(1)} %copy-done.4, f32[64,48,128]{2,1,0:T(8,128)} %all-to-all-done.seen_ref, f32[64,48,128]{2,1,0:T(8,128)S(1)} %forward.1.predicted_ref, bf16[64,192]{1,0:T(8,128)(2,1)S(1)} %get-tuple-element.24.yb_ref, ...), custom_call_target="tpu_custom_call" | custom-call | flops 100000000 | bytes 1048576 | tf_op jit(solution)/shard_map/quotient/pallas_call | solution.py:213
  68.9 5.0 %collective-permute-done.2 = f32[16,64,128]{2,1,0:T(8,128)S(1)} collective-permute-done((f32[16,64,128]{2,1,0:T(8,128)S(1)}, f32[16,64,128]{2,1,0:T(8,128)S(1)}, u32[]{:S(2)}, u32[]{:S(2)}) %collective-permute-start.2) | collective-permute-done | bytes 524320 | tf_op jit(solution)/shard_map/ppermute | solution.py:279
  73.9 1.5 %backward.3 = (f32[8,48,128]{2,1,0:T(8,128)S(1)}, f32[8,48,128]{2,1,0:T(8,128)S(1)}, f32[8,48,128]{2,1,0:T(8,128)S(1)}, f32[8,48,128]{2,1,0:T(8,128)S(1)}) custom-call(s32[2]{0:T(128)S(1)} %copy-done.3, f32[1024,128]{1,0:T(8,128)S(1)} %bitcast.23, f32[1024,128]{1,0:T(8,128)S(1)} %bitcast.19, f32[1024,128]{1,0:T(8,128)S(1)} %bitcast.17, ...), custom_call_target="tpu_custom_call" | custom-call | flops 200000000 | bytes 4194304 | tf_op jit(solution)/shard_map/backward/pallas_call | solution.py:241
  75.7 1.8 %collective-permute-start.8 = (f32[8,48,128]{2,1,0:T(8,128)S(1)}, f32[8,48,128]{2,1,0:T(8,128)S(1)}, u32[]{:S(2)}, u32[]{:S(2)}) collective-permute-start(f32[8,48,128]{2,1,0:T(8,128)S(1)} %get-tuple-element.36), channel_id=1, source_target_pairs={{0,192},{64,0},{128,64},{192,128},{1,193},{65,1},{129,65},{193,129... | collective-permute-start | bytes 589832 | tf_op jit(solution)/shard_map/ppermute | solution.py:279
  77.5 1.5 %backward.2 = (f32[8,48,128]{2,1,0:T(8,128)S(1)}, f32[8,48,128]{2,1,0:T(8,128)S(1)}, f32[8,48,128]{2,1,0:T(8,128)S(1)}, f32[8,48,128]{2,1,0:T(8,128)S(1)}) custom-call(s32[2]{0:T(128)S(1)} %copy-done.3, f32[1024,128]{1,0:T(8,128)S(1)} %bitcast.24, f32[1024,128]{1,0:T(8,128)S(1)} %bitcast.20, f32[1024,128]{1,0:T(8,128)S(1)} %bitcast.18, ...), custom_call_target="tpu_custom_call" | custom-call | flops 200000000 | bytes 4194304 | tf_op jit(solution)/shard_map/backward/pallas_call | solution.py:241
  79.9 1.3 %collective-permute-done.5 = f32[8,48,128]{2,1,0:T(8,128)S(1)} collective-permute-done((f32[8,48,128]{2,1,0:T(8,128)S(1)}, f32[8,48,128]{2,1,0:T(8,128)S(1)}, u32[]{:S(2)}, u32[]{:S(2)}) %collective-permute-start.5) | collective-permute-done | bytes 196640 | tf_op jit(solution)/shard_map/ppermute | solution.py:279
  81.2 1.7 %collective-permute-start.6 = (f32[8,48,128]{2,1,0:T(8,128)S(1)}, f32[8,48,128]{2,1,0:T(8,128)S(1)}, u32[]{:S(2)}, u32[]{:S(2)}) collective-permute-start(f32[8,48,128]{2,1,0:T(8,128)S(1)} %add.19), channel_id=1, source_target_pairs={{0,64},{64,128},{128,192},{192,0},{1,65},{65,129},{129,193},{193,1... | collective-permute-start | bytes 589832 | tf_op jit(solution)/shard_map/ppermute | solution.py:279
  83.2 1.3 %collective-permute-done.8 = f32[8,48,128]{2,1,0:T(8,128)S(1)} collective-permute-done((f32[8,48,128]{2,1,0:T(8,128)S(1)}, f32[8,48,128]{2,1,0:T(8,128)S(1)}, u32[]{:S(2)}, u32[]{:S(2)}) %collective-permute-start.8) | collective-permute-done | bytes 196640 | tf_op jit(solution)/shard_map/ppermute | solution.py:279
  85.0 3.8 %collective-permute-done.4 = f32[8,48,128]{2,1,0:T(8,128)S(1)} collective-permute-done((f32[8,48,128]{2,1,0:T(8,128)S(1)}, f32[8,48,128]{2,1,0:T(8,128)S(1)}, u32[]{:S(2)}, u32[]{:S(2)}) %collective-permute-start.4) | collective-permute-done | bytes 196640 | tf_op jit(solution)/shard_map/ppermute | solution.py:279
  88.8 1.9 %collective-permute-start.10 = (f32[8,48,128]{2,1,0:T(8,128)S(1)}, f32[8,48,128]{2,1,0:T(8,128)S(1)}, u32[]{:S(2)}, u32[]{:S(2)}) collective-permute-start(f32[8,48,128]{2,1,0:T(8,128)S(1)} %add_add_fusion.1), channel_id=1, source_target_pairs={{0,64},{64,128},{128,192},{192,0},{1,65},{65,129},{129,193},{193,1... | collective-permute-start | bytes 589832 | tf_op jit(solution)/shard_map/ppermute | solution.py:279
  93.1 2.7 %collective-permute-start.11 = (f32[8,48,128]{2,1,0:T(8,128)S(1)}, f32[8,48,128]{2,1,0:T(8,128)S(1)}, u32[]{:S(2)}, u32[]{:S(2)}) collective-permute-start(f32[8,48,128]{2,1,0:T(8,128)S(1)} %add_add_fusion), channel_id=1, source_target_pairs={{0,64},{64,128},{128,192},{192,0},{1,65},{65,129},{129,193},{193,1... | collective-permute-start | bytes 589832 | tf_op jit(solution)/shard_map/ppermute | solution.py:279
  96.6 2.8 %collective-permute-start.14 = (f32[8,48,128]{2,1,0:T(8,128)S(1)}, f32[8,48,128]{2,1,0:T(8,128)S(1)}, u32[]{:S(2)}, u32[]{:S(2)}) collective-permute-start(f32[8,48,128]{2,1,0:T(8,128)S(1)} %collective-permute-done.10), channel_id=1, source_target_pairs={{0,64},{64,128},{128,192},{192,0},{1,65},{65,129},{129,193},{193,1... | collective-permute-start | bytes 589832 | tf_op jit(solution)/shard_map/ppermute | solution.py:279
  99.7 3.7 %collective-permute-done.12 = f32[8,48,128]{2,1,0:T(8,128)S(1)} collective-permute-done((f32[8,48,128]{2,1,0:T(8,128)S(1)}, f32[8,48,128]{2,1,0:T(8,128)S(1)}, u32[]{:S(2)}, u32[]{:S(2)}) %collective-permute-start.12) | collective-permute-done | bytes 196640 | tf_op jit(solution)/shard_map/ppermute | solution.py:279
  103.4 3.2 %collective-permute-done.15 = f32[8,48,128]{2,1,0:T(8,128)S(1)} collective-permute-done((f32[8,48,128]{2,1,0:T(8,128)S(1)}, f32[8,48,128]{2,1,0:T(8,128)S(1)}, u32[]{:S(2)}, u32[]{:S(2)}) %collective-permute-start.15) | collective-permute-done | bytes 196640 | tf_op jit(solution)/shard_map/ppermute | solution.py:279
  106.5 2.5 %finish.1 = f32[48,64,128]{2,1,0:T(8,128)} custom-call(s32[2]{0:T(128)S(1)} %copy-done.3, f32[48,64,128]{2,1,0:T(8,128)S(1)} %copy-done, f32[384,128]{1,0:T(8,128)S(1)} %bitcast.28, f32[384,128]{1,0:T(8,128)S(1)} %bitcast.29, f32[384,128]{1,0:T(8,128)S(1)} %bitcast.30, f32[384,128]{1,0:T(8,128)S(1)} %bitcast.33, f32[384,128]{1,0:T(8,128)S(1)} %bitcast.32, ...), custom_call_target="tpu_custom_call" | custom-call | flops 1000000 | bytes 5242880 | tf_op jit(solution)/shard_map/finish/pallas_call | solution.py:266
  (48 shorter events, 9.7 us)
Async XLA Ops:
  0.0 10.6 %copy-start.1 = (f32[1,1,3072,128]{3,2,1,0:T(8,128)S(1)}, f32[1,1,3072,128]{3,2,1,0:T(8,128)}, u32[]{:S(2)}) copy-start(f32[1,1,3072,128]{3,2,1,0:T(8,128)} %param.8) | copy-start | bytes 4718596
  2.4 19.4 %collective-permute-start.1 = (f32[16,64,128]{2,1,0:T(8,128)}, f32[16,64,128]{2,1,0:T(8,128)S(1)}, u32[]{:S(2)}, u32[]{:S(2)}) collective-permute-start(f32[16,64,128]{2,1,0:T(8,128)} %get-tuple-element.37), channel_id=1, source_target_pairs={{0,63},{1,0},{2,1},{3,2},{4,3},{5,4},{6,5},{7,6},{8,7},{9,8},{10,9... | collective-permute-start | bytes 1572872 | tf_op jit(solution)/shard_map/ppermute | solution.py:279
  9.9 12.7 %collective-permute-start = (f32[16,64,128]{2,1,0:T(8,128)}, f32[16,64,128]{2,1,0:T(8,128)S(1)}, u32[]{:S(2)}, u32[]{:S(2)}) collective-permute-start(f32[16,64,128]{2,1,0:T(8,128)} %get-tuple-element.38), channel_id=1, source_target_pairs={{0,1},{1,2},{2,3},{3,4},{4,5},{5,6},{6,7},{7,8},{8,9},{9,10},{10,1... | collective-permute-start | bytes 1572872 | tf_op jit(solution)/shard_map/ppermute | solution.py:279
  12.0 7.8 %copy-start.5 = (f32[1,31]{1,0:T(1,128)S(1)}, f32[1,31]{1,0:T(1,128)}, u32[]{:S(2)}) copy-start(f32[1,31]{1,0:T(1,128)} %x_ref.1) | copy-start | bytes 376
  12.0 7.8 %copy-start.6 = (f32[1,31]{1,0:T(1,128)S(1)}, f32[1,31]{1,0:T(1,128)}, u32[]{:S(2)}) copy-start(f32[1,31]{1,0:T(1,128)} %y_ref.1) | copy-start | bytes 376
  12.0 7.8 %copy-start.7 = (f32[1,61]{1,0:T(1,128)S(1)}, f32[1,61]{1,0:T(1,128)}, u32[]{:S(2)}) copy-start(f32[1,61]{1,0:T(1,128)} %z_ref.1) | copy-start | bytes 736
  12.0 11.4 %copy-start = (f32[48,64,128]{2,1,0:T(8,128)S(1)}, f32[48,64,128]{2,1,0:T(8,128)}, u32[]{:S(2)}) copy-start(f32[48,64,128]{2,1,0:T(8,128)} %estimate_ref.1) | copy-start | bytes 4718596
  12.0 47.1 %all-to-all-start = ((f32[64,48,128]{2,1,0:T(8,128)}), f32[64,48,128]{2,1,0:T(8,128)}, u32[]{:S(2)}, u32[]{:S(2)}) async-start(f32[64,48,128]{2,1,0:T(8,128)} %bitcast.3), calls=%async_computation | async-start | bytes 3145728 | tf_op jit(solution)/shard_map/all_to_all | solution.py:287
  25.5 33.6 %copy-start.3 = (s32[2]{0:T(128)S(1)}, s32[2]{0:T(128)}, u32[]{:S(2)}) copy-start(s32[2]{0:T(128)} %copy-done.2) | copy-start | bytes 28
  25.5 33.6 %copy-start.4 = (s32[1,2]{1,0:T(1,128)S(1)}, s32[1,2]{1,0:T(1,128)}, u32[]{:S(2)}) copy-start(s32[1,2]{1,0:T(1,128)} %box_ref.3) | copy-start | bytes 28
  61.9 12.0 %collective-permute-start.2 = (f32[16,64,128]{2,1,0:T(8,128)S(1)}, f32[16,64,128]{2,1,0:T(8,128)S(1)}, u32[]{:S(2)}, u32[]{:S(2)}) collective-permute-start(f32[16,64,128]{2,1,0:T(8,128)S(1)} %get-tuple-element.26), channel_id=1, source_target_pairs={{0,1},{1,2},{2,3},{3,4},{4,5},{5,6},{6,7},{7,8},{8,9},{9,10},{10,1... | collective-permute-start | bytes 1572872 | tf_op jit(solution)/shard_map/ppermute | solution.py:279
  62.3 11.6 %collective-permute-start.3 = (f32[16,64,128]{2,1,0:T(8,128)S(1)}, f32[16,64,128]{2,1,0:T(8,128)S(1)}, u32[]{:S(2)}, u32[]{:S(2)}) collective-permute-start(f32[16,64,128]{2,1,0:T(8,128)S(1)} %get-tuple-element.27), channel_id=1, source_target_pairs={{0,63},{1,0},{2,1},{3,2},{4,3},{5,4},{6,5},{7,6},{8,7},{9,8},{10,9... | collective-permute-start | bytes 1572872 | tf_op jit(solution)/shard_map/ppermute | solution.py:279
  75.4 5.7 %collective-permute-start.5 = (f32[8,48,128]{2,1,0:T(8,128)S(1)}, f32[8,48,128]{2,1,0:T(8,128)S(1)}, u32[]{:S(2)}, u32[]{:S(2)}) collective-permute-start(f32[8,48,128]{2,1,0:T(8,128)S(1)} %get-tuple-element.32), channel_id=1, source_target_pairs={{0,64},{64,128},{128,192},{192,0},{1,65},{65,129},{129,193},{193,1... | collective-permute-start | bytes 589832 | tf_op jit(solution)/shard_map/ppermute | solution.py:279
  75.7 8.9 %collective-permute-start.8 = (f32[8,48,128]{2,1,0:T(8,128)S(1)}, f32[8,48,128]{2,1,0:T(8,128)S(1)}, u32[]{:S(2)}, u32[]{:S(2)}) collective-permute-start(f32[8,48,128]{2,1,0:T(8,128)S(1)} %get-tuple-element.36), channel_id=1, source_target_pairs={{0,192},{64,0},{128,64},{192,128},{1,193},{65,1},{129,65},{193,129... | collective-permute-start | bytes 589832 | tf_op jit(solution)/shard_map/ppermute | solution.py:279
  79.0 9.7 %collective-permute-start.4 = (f32[8,48,128]{2,1,0:T(8,128)S(1)}, f32[8,48,128]{2,1,0:T(8,128)S(1)}, u32[]{:S(2)}, u32[]{:S(2)}) collective-permute-start(f32[8,48,128]{2,1,0:T(8,128)S(1)} %get-tuple-element.30), channel_id=1, source_target_pairs={{0,192},{64,0},{128,64},{192,128},{1,193},{65,1},{129,65},{193,129... | collective-permute-start | bytes 589832 | tf_op jit(solution)/shard_map/ppermute | solution.py:279
  81.2 7.6 %collective-permute-start.6 = (f32[8,48,128]{2,1,0:T(8,128)S(1)}, f32[8,48,128]{2,1,0:T(8,128)S(1)}, u32[]{:S(2)}, u32[]{:S(2)}) collective-permute-start(f32[8,48,128]{2,1,0:T(8,128)S(1)} %add.19), channel_id=1, source_target_pairs={{0,64},{64,128},{128,192},{192,0},{1,65},{65,129},{129,193},{193,1... | collective-permute-start | bytes 589832 | tf_op jit(solution)/shard_map/ppermute | solution.py:279
  82.9 8.6 %collective-permute-start.7 = (f32[8,48,128]{2,1,0:T(8,128)S(1)}, f32[8,48,128]{2,1,0:T(8,128)S(1)}, u32[]{:S(2)}, u32[]{:S(2)}) collective-permute-start(f32[8,48,128]{2,1,0:T(8,128)S(1)} %get-tuple-element.34), channel_id=1, source_target_pairs={{0,64},{64,128},{128,192},{192,0},{1,65},{65,129},{129,193},{193,1... | collective-permute-start | bytes 589832 | tf_op jit(solution)/shard_map/ppermute | solution.py:279
  84.6 7.0 %collective-permute-start.9 = (f32[8,48,128]{2,1,0:T(8,128)S(1)}, f32[8,48,128]{2,1,0:T(8,128)S(1)}, u32[]{:S(2)}, u32[]{:S(2)}) collective-permute-start(f32[8,48,128]{2,1,0:T(8,128)S(1)} %add.22), channel_id=1, source_target_pairs={{0,192},{64,0},{128,64},{192,128},{1,193},{65,1},{129,65},{193,129... | collective-permute-start | bytes 589832 | tf_op jit(solution)/shard_map/ppermute | solution.py:279
  88.8 7.8 %collective-permute-start.10 = (f32[8,48,128]{2,1,0:T(8,128)S(1)}, f32[8,48,128]{2,1,0:T(8,128)S(1)}, u32[]{:S(2)}, u32[]{:S(2)}) collective-permute-start(f32[8,48,128]{2,1,0:T(8,128)S(1)} %add_add_fusion.1), channel_id=1, source_target_pairs={{0,64},{64,128},{128,192},{192,0},{1,65},{65,129},{129,193},{193,1... | collective-permute-start | bytes 589832 | tf_op jit(solution)/shard_map/ppermute | solution.py:279
  91.6 8.1 %collective-permute-start.13 = (f32[8,48,128]{2,1,0:T(8,128)S(1)}, f32[8,48,128]{2,1,0:T(8,128)S(1)}, u32[]{:S(2)}, u32[]{:S(2)}) collective-permute-start(f32[8,48,128]{2,1,0:T(8,128)S(1)} %add_add_fusion), channel_id=1, source_target_pairs={{0,192},{64,0},{128,64},{192,128},{1,193},{65,1},{129,65},{193,129... | collective-permute-start | bytes 589832 | tf_op jit(solution)/shard_map/ppermute | solution.py:279
  92.6 10.8 %collective-permute-start.12 = (f32[8,48,128]{2,1,0:T(8,128)S(1)}, f32[8,48,128]{2,1,0:T(8,128)S(1)}, u32[]{:S(2)}, u32[]{:S(2)}) collective-permute-start(f32[8,48,128]{2,1,0:T(8,128)S(1)} %add_add_fusion.1), channel_id=1, source_target_pairs={{0,192},{64,0},{128,64},{192,128},{1,193},{65,1},{129,65},{193,129... | collective-permute-start | bytes 589832 | tf_op jit(solution)/shard_map/ppermute | solution.py:279
  93.1 10.3 %collective-permute-start.11 = (f32[8,48,128]{2,1,0:T(8,128)S(1)}, f32[8,48,128]{2,1,0:T(8,128)S(1)}, u32[]{:S(2)}, u32[]{:S(2)}) collective-permute-start(f32[8,48,128]{2,1,0:T(8,128)S(1)} %add_add_fusion), channel_id=1, source_target_pairs={{0,64},{64,128},{128,192},{192,0},{1,65},{65,129},{129,193},{193,1... | collective-permute-start | bytes 589832 | tf_op jit(solution)/shard_map/ppermute | solution.py:279
  96.6 6.7 %collective-permute-start.14 = (f32[8,48,128]{2,1,0:T(8,128)S(1)}, f32[8,48,128]{2,1,0:T(8,128)S(1)}, u32[]{:S(2)}, u32[]{:S(2)}) collective-permute-start(f32[8,48,128]{2,1,0:T(8,128)S(1)} %collective-permute-done.10), channel_id=1, source_target_pairs={{0,64},{64,128},{128,192},{192,0},{1,65},{65,129},{129,193},{193,1... | collective-permute-start | bytes 589832 | tf_op jit(solution)/shard_map/ppermute | solution.py:279
  99.7 6.9 %collective-permute-start.15 = (f32[8,48,128]{2,1,0:T(8,128)S(1)}, f32[8,48,128]{2,1,0:T(8,128)S(1)}, u32[]{:S(2)}, u32[]{:S(2)}) collective-permute-start(f32[8,48,128]{2,1,0:T(8,128)S(1)} %collective-permute-done.13), channel_id=1, source_target_pairs={{0,192},{64,0},{128,64},{192,128},{1,193},{65,1},{129,65},{193,129... | collective-permute-start | bytes 589832 | tf_op jit(solution)/shard_map/ppermute | solution.py:279
  (5 other events, 7.2 us)

commit v4 on v3

v4 whole, which is shorter than its diff:
```python
import functools
import jax
import jax.numpy as jnp
from jax import lax
from jax.experimental import pallas as pl
from jax.experimental.pallas import tpu as pltpu
from jax.sharding import PartitionSpec as P

NX, NY, NZ = 3072, 64, 128
SLAB = 48
HALO = 16
WIDE = SLAB + 2 * HALO
SMAX = 8
QUARTER = NY // 4
TAPS_X, TAPS_Y, TAPS_Z = 31, 31, 61
HALF_X, HALF_Y, HALF_Z = 15, 15, 30
F32, BF16 = jnp.float32, jnp.bfloat16
VMEM_LIMIT = 48 * 1024 * 1024

SHORT = pl.CostEstimate(flops=1000, bytes_accessed=1000, transcendentals=0)
FAR_COST = pl.CostEstimate(flops=2 * 10**9, bytes_accessed=1000, transcendentals=0)
SMEM_SPEC = pl.BlockSpec(memory_space=pltpu.SMEM)
VMEM_SPEC = pl.BlockSpec(memory_space=pltpu.VMEM)
ANY_SPEC = pl.BlockSpec(memory_space=pl.ANY)
PARAMS = pltpu.CompilerParams(vmem_limit_bytes=VMEM_LIMIT)


def iota(shape, axis):
    return lax.broadcasted_iota(jnp.int32, shape, axis)


def split(value):
    high = value.astype(BF16)
    return high, (value - high.astype(F32)).astype(BF16)


def swap(block, over_link):
    size = lax.axis_size("block")
    start = 1 if over_link else 0
    pairs = [(i % size, (i + 1) % size) for i in range(start, size + start, 2)]
    return lax.ppermute(block, "block", pairs + [(target, source) for source, target in pairs])


PARTS = 4


def edges_kernel(block, estimate, far, near, held, in_sems, out_sems):
    odd = lax.rem(block[0], 2)
    half = HALO // 2
    takes, gives = [], []
    for index, (first, out_ref) in enumerate(((odd, far), (1 - odd, near))):
        for part in range(2):
            slot = 2 * index + part
            rows = estimate.at[pl.ds(first * (SLAB - HALO) + part * half, half)]
            takes.append(pltpu.make_async_copy(rows, held.at[slot], in_sems.at[slot]))
            gives.append(
                pltpu.make_async_copy(held.at[slot], out_ref.at[pl.ds(part * half, half)], out_sems.at[slot])
            )
    for copy in takes:
        copy.start()
    for take, give in zip(takes, gives):
        take.wait()
        give.start()
    for give in gives:
        give.wait()


def edges(block, estimate):
    return pl.pallas_call(
        edges_kernel,
        out_shape=[jax.ShapeDtypeStruct((HALO, NY, NZ), F32)] * 2,
        in_specs=[SMEM_SPEC, ANY_SPEC],
        out_specs=[ANY_SPEC] * 2,
        scratch_shapes=[
            pltpu.VMEM((4, HALO // 2, NY, NZ), F32),
            pltpu.SemaphoreType.DMA((4,)),
            pltpu.SemaphoreType.DMA((4,)),
        ],
        compiler_params=pltpu.CompilerParams(vmem_limit_bytes=60 * 1024 * 1024),
        cost_estimate=pl.CostEstimate(flops=1000, bytes_accessed=2**20, transcendentals=0),
        name="edges",
    )(block, estimate)


def roll_kernel(shift_ref, source, target, padded, rolled, sems):
    padded[pl.ds(SMAX, NX), :] = source[...]
    padded[pl.ds(0, SMAX), :] = source[pl.ds(NX - SMAX, SMAX), :]
    padded[pl.ds(SMAX + NX, SMAX), :] = source[pl.ds(0, SMAX), :]
    start = SMAX - shift_ref[0]
    size = NX // PARTS
    copies = []
    for part in range(PARTS):

        def move(block, carry, part=part):
            base = part * size + block * 128
            rolled[pl.ds(pl.multiple_of(base, 128), 128), :] = padded[pl.ds(start + base, 128), :]
            return carry

        lax.fori_loop(0, size // 128, move, 0)
        copy = pltpu.make_async_copy(
            rolled.at[pl.ds(part * size, size)], target.at[pl.ds(part * size, size)], sems.at[part]
        )
        copy.start()
        copies.append(copy)
    for copy in copies:
        copy.wait()


def roll_rows(recorded, shift):
    return pl.pallas_call(
        roll_kernel,
        out_shape=jax.ShapeDtypeStruct((NX, NZ), F32),
        in_specs=[SMEM_SPEC, VMEM_SPEC],
        out_specs=ANY_SPEC,
        scratch_shapes=[
            pltpu.VMEM((NX + 2 * SMAX, NZ), F32),
            pltpu.VMEM((NX, NZ), F32),
            pltpu.SemaphoreType.DMA((PARTS,)),
        ],
        compiler_params=PARAMS,
        cost_estimate=pl.CostEstimate(flops=10**6, bytes_accessed=3 * 2**20, transcendentals=0),
        name="roll_rows",
    )(shift, recorded.reshape(NX, NZ))


def pick_taps(taps_ref, count, tap_index, valid):
    total = taps_ref[0, 0]
    picked = jnp.zeros(tap_index.shape, F32)
    for tap in range(count):
        if tap:
            total = total + taps_ref[0, tap]
        picked = jnp.where(tap_index == tap, taps_ref[0, tap], picked)
    if valid is not None:
        picked = jnp.where(valid, picked, 0.0)
    return picked / jnp.full(tap_index.shape, total, F32)


def packed(matrix, part):
    high, low = split(matrix)
    return jnp.where(part < 2, high.astype(F32), low.astype(F32)).astype(BF16)


def x_places(first, odd, turned):
    shape = (SLAB, 3 * WIDE)
    row, col = iota(shape, 0), iota(shape, 1)
    part = jnp.where(col >= 2 * WIDE, 2, jnp.where(col >= WIDE, 1, 0))
    col = col - part * WIDE
    block = lax.div(col, HALO)
    other = 4 - block if turned else jnp.where((block == 0) | (block == 4), 4 - block, block)
    block_at = jnp.where(odd == 1, other, block)
    return first + row, block_at * HALO + lax.rem(col, HALO) - HALO - row, part


def bands_kernel(group, block, shift_ref, x_ref, y_ref, z_ref, yf_ref, yb_ref, zf_ref, zb_ref, xf_ref, xb_ref):
    shift = shift_ref[0]
    first = block[0] * SLAB
    shape = (NY, 3 * NY)
    row, col = iota(shape, 0), iota(shape, 1)
    part = jnp.where(col >= 2 * NY, 2, jnp.where(col >= NY, 1, 0))
    col = col - part * NY
    yf_ref[...] = packed(pick_taps(y_ref, TAPS_Y, col - row + HALF_Y, None), part)
    row = lax.rem(row + group[0] * QUARTER, NY)
    yb_ref[...] = packed(pick_taps(y_ref, TAPS_Y, row - col + HALF_Y, None), part)
    shape = (NZ, NZ)
    row, col = iota(shape, 0), iota(shape, 1)
    for ref, index in ((zf_ref, row - col + HALF_Z), (zb_ref, col - row + HALF_Z)):
        high, low = split(pick_taps(z_ref, TAPS_Z, index, None))
        ref[:NZ, :NZ] = high
        ref[NZ:, :NZ] = high
        ref[:NZ, NZ:] = low
        ref[NZ:, NZ:] = jnp.zeros(shape, BF16)
    odd = lax.rem(block[0], 2)
    place, step, part = x_places(first, odd, False)
    view_row = place - shift
    view_row = jnp.where(view_row < 0, view_row + NX, view_row)
    view_row = jnp.where(view_row >= NX, view_row - NX, view_row)
    met = view_row + shift + step
    xf_ref[...] = packed(pick_taps(x_ref, TAPS_X, step + HALF_X, (met >= 0) & (met < NX)), part)
    place, step, part = x_places(first, odd, True)
    met = place - shift + step
    xb_ref[...] = packed(pick_taps(x_ref, TAPS_X, HALF_X - step, (met >= 0) & (met < NX)), part)


def make_bands(group, block, shift, psf_x, psf_y, psf_z):
    shapes = [(NY, 3 * NY)] * 2 + [(2 * NZ, 2 * NZ)] * 2 + [(SLAB, 3 * WIDE)] * 2
    return pl.pallas_call(
        bands_kernel,
        out_shape=[jax.ShapeDtypeStruct(shape, BF16) for shape in shapes],
        in_specs=[SMEM_SPEC] * 6,
        out_specs=[VMEM_SPEC] * 6,
        compiler_params=PARAMS,
        name="make_bands",
    )(group, block, shift, psf_x, psf_y, psf_z)


def blur_z(value, band):
    both = jnp.dot(jnp.concatenate(split(value), axis=1), band, preferred_element_type=F32)
    return both[:, :NZ] + both[:, NZ:]


def blur_rows(band, left, right):
    high, low = split(jnp.concatenate([left, right], axis=1))
    both = jnp.dot(band, jnp.concatenate([high, low, high], axis=0), preferred_element_type=F32)
    return both[:, :NZ], both[:, NZ:]


def forward_kernel(far_ref, own_ref, near_ref, yf_ref, zf_ref, xf_ref, out_ref, blurred, wide):
    for ref, count, base in ((far_ref, HALO, 0), (own_ref, SLAB, HALO), (near_ref, HALO, HALO + SLAB)):

        def along_z(block, carry, ref=ref, base=base):
            rows = ref[pl.ds(block * 8, 8)].reshape(8 * NY, NZ)
            start = pl.multiple_of((base + block * 8) * NY, 8)
            blurred[pl.ds(start, 8 * NY), :] = blur_z(rows, zf_ref[...])
            return carry

        lax.fori_loop(0, count // 8, along_z, 0)

    def along_y(pair, carry):
        start = pl.multiple_of(pair * 2 * NY, 2 * NY)
        left, right = blur_rows(yf_ref[...], blurred[pl.ds(start, NY), :], blurred[pl.ds(start + NY, NY), :])
        wide[pl.ds(start, NY), :] = left
        wide[pl.ds(start + NY, NY), :] = right
        return carry

    lax.fori_loop(0, WIDE // 2, along_y, 0, unroll=4)

    def along_x(pair, carry):
        y = pair * 2
        left, right = blur_rows(
            xf_ref[...], wide[pl.ds(y, WIDE, stride=NY), :], wide[pl.ds(y + 1, WIDE, stride=NY), :]
        )
        out_ref[y] = left
        out_ref[y + 1] = right
        return carry

    lax.fori_loop(0, NY // 2, along_x, 0, unroll=4)


def forward(far, own, near, band_y, band_z, band_x):
    return pl.pallas_call(
        forward_kernel,
        out_shape=jax.ShapeDtypeStruct((NY, SLAB, NZ), F32),
        in_specs=[VMEM_SPEC] * 6,
        out_specs=VMEM_SPEC,
        scratch_shapes=[pltpu.VMEM((WIDE * NY, NZ), F32), pltpu.VMEM((WIDE * NY, NZ), F32)],
        compiler_params=PARAMS,
        cost_estimate=pl.CostEstimate(flops=2 * 10**11, bytes_accessed=6 * 2**20, transcendentals=0),
        name="forward",
    )(far, own, near, band_y, band_z, band_x)


def quotient_kernel(block, shift_ref, box_ref, seen_ref, predicted_ref, yb_ref, zb_ref, *rest):
    out_refs, (across_ref, rest_ref), (fetched, blurred, sems) = rest[:3], rest[3:5], rest[5:]
    odd = lax.rem(block[0], 2)
    size = NY // PARTS
    firsts = [pl.multiple_of(first, HALO) for first in (odd * (SLAB - HALO), (1 - odd) * (SLAB - HALO))] + [HALO]
    copies = [
        pltpu.make_async_copy(
            seen_ref.at[pl.ds(part * size, size), pl.ds(first, HALO), :],
            fetched.at[index, pl.ds(part * size, size)],
            sems.at[index, part],
        )
        for index, first in enumerate(firsts)
        for part in range(PARTS)
    ]
    for copy in copies:
        copy.start()
    for copy in copies:
        copy.wait()
    for index, first in enumerate(firsts):
        row = block[0] * SLAB + first - shift_ref[0] + iota((HALO, NZ), 0)
        row = jnp.where(row < 0, row + NX, row)
        row = jnp.where(row >= NX, row - NX, row)
        inside = (row >= box_ref[0, 0]) & (row < box_ref[0, 1])
        for part in range(PARTS):
            span = pl.ds(part * size, size)
            ratio = fetched[index, span] / predicted_ref[span, pl.ds(first, HALO), :]
            ratio = jnp.where(inside[None], ratio, 1.0).reshape(size * HALO, NZ)
            blurred[index, pl.ds(part * size * HALO, size * HALO), :] = blur_z(ratio, zb_ref[...])
        for x in range(0, HALO, 2):
            both = blur_rows(
                yb_ref[...],
                blurred[index, pl.ds(x, NY, stride=HALO), :],
                blurred[index, pl.ds(x + 1, NY, stride=HALO), :],
            )
            for side, plane in enumerate(both):
                out_refs[index][x + side] = plane
                if index == 0:
                    across_ref[x + side] = plane[2 * QUARTER : 3 * QUARTER]
                    rest_ref[x + side, : 2 * QUARTER] = plane[: 2 * QUARTER]
                    rest_ref[x + side, 2 * QUARTER :] = plane[3 * QUARTER :]


def quotient(block, shift, box, seen, predicted, band_y, band_z):
    sizes = (NY, NY, NY, QUARTER, 3 * QUARTER)
    return pl.pallas_call(
        quotient_kernel,
        out_shape=[jax.ShapeDtypeStruct((HALO, size, NZ), F32) for size in sizes],
        in_specs=[SMEM_SPEC] * 3 + [ANY_SPEC] + [VMEM_SPEC] * 3,
        out_specs=[VMEM_SPEC] * len(sizes),
        scratch_shapes=[
            pltpu.VMEM((3, NY, HALO, NZ), F32),
            pltpu.VMEM((3, NY * HALO, NZ), F32),
            pltpu.SemaphoreType.DMA((3, PARTS)),
        ],
        compiler_params=PARAMS,
        cost_estimate=SHORT,
        name="quotient",
    )(block, shift, box, seen, predicted, band_y, band_z)


def backward_kernel(parts, size, piece_ref, *rest):
    whole_refs, band_ref, out_refs = rest[:4], rest[4], rest[5:]
    for out_ref, (at, piece_at) in zip(out_refs, parts):
        for y in range(0, 8, 2):
            planes = [
                jnp.concatenate(
                    [piece_ref[pl.ds(piece_at + y + side, HALO, stride=size), :]]
                    + [ref[pl.ds(at + y + side, HALO, stride=NY), :] for ref in whole_refs],
                    axis=0,
                )
                for side in (0, 1)
            ]
            left, right = blur_rows(band_ref[...], *planes)
            out_ref[y] = left
            out_ref[y + 1] = right


def backward(parts, cost, piece, wholes, band_x):
    size = piece.shape[1]
    return pl.pallas_call(
        functools.partial(backward_kernel, parts, size),
        out_shape=[jax.ShapeDtypeStruct((8, SLAB, NZ), F32)] * len(parts),
        in_specs=[VMEM_SPEC] * 6,
        out_specs=[VMEM_SPEC] * len(parts),
        compiler_params=PARAMS,
        cost_estimate=cost,
        name="backward",
    )(piece.reshape(HALO * size, NZ), *[whole.reshape(HALO * NY, NZ) for whole in wholes], band_x)


def finish_rows(group, estimate_ref, piece_ref, turns, half, out_ref, out_base):
    base = pl.multiple_of(lax.rem(group[0] + turns, 4) * 16 + half * 8, 8)
    at = base if out_base is None else out_base

    def row(x, carry):
        value = piece_ref[pl.ds(x, 8, stride=SLAB), :]
        out_ref[x, pl.ds(at, 8), :] = estimate_ref[x, pl.ds(base, 8), :] * value * 0.25
        return carry

    lax.fori_loop(0, SLAB, row, 0, unroll=8)
    return base


def finish_kernel(parts, group, estimate_ref, *rest):
    piece_refs, out_ref = rest[:-1], rest[-1]
    for piece_ref, (turns, half) in zip(piece_refs, parts):
        finish_rows(group, estimate_ref, piece_ref, turns, half, out_ref, None)


def last_kernel(parts, group, estimate_ref, *rest):
    piece_refs, (_, out_ref, done, sems) = rest[: len(parts)], rest[len(parts) :]
    copies = []
    for index, (piece_ref, (turns, half)) in enumerate(zip(piece_refs, parts)):
        base = finish_rows(group, estimate_ref, piece_ref, turns, half, done, index * 8)
        copy = pltpu.make_async_copy(
            done.at[:, pl.ds(index * 8, 8), :], out_ref.at[:, pl.ds(base, 8), :], sems.at[index]
        )
        copy.start()
        copies.append(copy)
    for copy in copies:
        copy.wait()


def finish(parts, group, estimate, pieces, before=None):
    count = len(parts)
    pieces = [piece.reshape(8 * SLAB, NZ) for piece in pieces]
    shape = jax.ShapeDtypeStruct((SLAB, NY, NZ), F32)
    cost = SHORT
    in_specs = [SMEM_SPEC] + [VMEM_SPEC] * (count + 1)
    if before is None:
        return pl.pallas_call(
            functools.partial(finish_kernel, parts),
            out_shape=shape,
            in_specs=in_specs,
            out_specs=VMEM_SPEC,
            compiler_params=PARAMS,
            cost_estimate=cost,
            name="finish",
        )(group, estimate, *pieces)
    return pl.pallas_call(
        functools.partial(last_kernel, parts),
        out_shape=shape,
        in_specs=in_specs + [ANY_SPEC],
        out_specs=ANY_SPEC,
        scratch_shapes=[pltpu.VMEM((SLAB, 8 * count, NZ), F32), pltpu.SemaphoreType.DMA((count,))],
        input_output_aliases={count + 2: 0},
        compiler_params=PARAMS,
        cost_estimate=cost,
        name="finish_last",
    )(group, estimate, *pieces, before)


def turn(block, axis, step):
    size = lax.axis_size(axis)
    return lax.ppermute(block, axis, [(i, (i + step) % size) for i in range(size)])


def body(estimate, recorded, psf_x, psf_y, psf_z, view_shifts, view_boxes):
    group, block = lax.axis_index("group").reshape(1), lax.axis_index("block").reshape(1)
    far, near = edges(block, estimate)
    far, near = swap(far, True), swap(near, False)
    rolled = roll_rows(recorded, view_shifts)
    seen = lax.all_to_all(rolled.reshape(NY, SLAB, NZ), "block", 0, 0)
    yf, yb, zf, zb, xf, xb = make_bands(group, block, view_shifts, psf_x, psf_y, psf_z)
    predicted = forward(far, estimate, near, yf, zf, xf)

    far, near, middle, across, rest = quotient(block, view_shifts, view_boxes, seen, predicted, yb, zb)
    across, from_near, rest = swap(across, True), swap(near, False), swap(rest, True)
    wholes = (far, middle, near, from_near)

    far_a, far_b = backward(((32, 0), (40, 8)), FAR_COST, across, wholes, xb)
    far_a, far_b = turn(far_a, "group", 1), turn(far_b, "group", -1)
    far_a, far_b = lax.optimization_barrier((far_a, far_b))
    next_a, near_b, near_a, prev_b, own_a, own_b = backward(
        ((16, 16), (24, 24), (48, 32), (56, 40), (0, 0), (8, 8)), SHORT, rest, wholes, xb
    )
    sum_a = turn(next_a + far_a, "group", 1)
    sum_b = turn(prev_b + far_b, "group", -1)
    near_b, near_a = turn(near_b, "group", 1), turn(near_a, "group", -1)
    own_a = own_a + near_a + sum_a
    own_b = own_b + near_b + sum_b

    low_a, high_b = turn(own_a, "group", 1), turn(own_b, "group", -1)
    low_b, high_a = turn(own_b, "group", 1), turn(own_a, "group", -1)
    across_a, across_b = turn(low_a, "group", 1), turn(high_b, "group", -1)
    most = finish(
        ((0, 0), (0, 1), (3, 0), (3, 1), (1, 0), (1, 1)),
        group,
        estimate,
        (own_a, own_b, low_a, low_b, high_a, high_b),
    )
    return finish(((2, 0), (2, 1)), group, estimate, (across_a, across_b), most)


def solution(mesh):
    return jax.shard_map(
        body,
        mesh=mesh,
        in_specs=(
            P("block", None, None),
            P("group", "block", None, None),
            P("group", None),
            P("group", None),
            P("group", None),
            P("group"),
            P("group", None),
        ),
        out_specs=P("block", None, None),
        check_vma=False,
    )
```

time: 111 us -> 106 us (0.955); the launches traced: 109 us -> 106 us
  local copies, waits for them, and re-layouts: 6.11 us -> 3.7 us
  waiting for transfers between devices: 46.8 us -> 45.4 us
    ppermute x0 -> x5, starting transfers between devices: none -> 13.1 us  [swap(): lax.ppermute(block, 'block', pairs + [(target, source) for source, target...]
    ppermute x16 -> x12, starting transfers between devices: 26.9 us -> 15.8 us  [turn(): lax.ppermute(block, axis, [(i, (i + step) % size) for i in range(size)])]
    ppermute x16 -> x12, waiting for transfers between devices: 20.2 us -> 14.1 us  [turn(): lax.ppermute(block, axis, [(i, (i + step) % size) for i in range(size)])]
    ppermute x0 -> x5, waiting for transfers between devices: none -> 4.64 us  [swap(): lax.ppermute(block, 'block', pairs + [(target, source) for source, target...]
    slice x1 -> x0, local copies, waits for them, and re-layouts: 2.42 us -> none  [body(): high = turn(estimate[:HALO], 'block', -1)]
    all_to_all x1, starting transfers between devices: 7.72 us -> 5.95 us  [body(): seen = lax.all_to_all(rolled.reshape(NY, SLAB, NZ), 'block', 0, 0)]
    pallas_call x5 -> x6, Pallas kernels: 10.1 us -> 10.3 us  [the longest x1 3.71 us: quotient(): pl.pallas_call(quotient_kernel, out_shape=[jax.ShapeDtypeStruct((HALO, si...]
    unnamed x24 -> x20, local copies, waits for them, and re-layouts: 3.69 us -> 3.7 us
  transfers between devices with their start and end apart: 17 -> 18, of which waited for: 11 -> 12; matrix products, arithmetic and copies ran while one was open for 0% -> 0% of each run, Pallas kernels for 13% -> 13%
where the time goes in v4:
time: 106 us
  waiting for transfers between devices  45.4 us (43%)
  starting transfers between devices  34.8 us (33%)
  Pallas kernels  20.6 us (19%)
  local copies, waits for them, and re-layouts  3.7 us (3%)
    all_to_all x1, waiting for transfers between devices, body(): seen = lax.all_to_all(rolled.reshape(NY, SLAB, NZ), 'block', 0, 0)  26.7 us
    ppermute x12, starting transfers between devices, turn(): lax.ppermute(block, axis, [(i, (i + step) % size) for i in range(size)])  15.8 us
    ppermute x12, waiting for transfers between devices, turn(): lax.ppermute(block, axis, [(i, (i + step) % size) for i in range(size)])  14.1 us
    ppermute x5, starting transfers between devices, swap(): lax.ppermute(block, 'block', pairs + [(target, source) for source, target...  13.1 us
    pallas_call x1, Pallas kernels, forward(): pl.pallas_call(forward_kernel, out_shape=jax.ShapeDtypeStruct((NY, SLAB,...  7.04 us
    all_to_all x1, starting transfers between devices, body(): seen = lax.all_to_all(rolled.reshape(NY, SLAB, NZ), 'block', 0, 0)  5.95 us
    ppermute x5, waiting for transfers between devices, swap(): lax.ppermute(block, 'block', pairs + [(target, source) for source, target...  4.64 us
    pallas_call x1, Pallas kernels, quotient(): pl.pallas_call(quotient_kernel, out_shape=[jax.ShapeDtypeStruct((HALO, si...  3.71 us
  transfers between devices with their start and end apart: 18, of which 12 were waited for; matrix products, arithmetic and copies ran while one was open for 0% of the time, Pallas kernels for 13%

profile of v4, /device:TPU:24, one launch (start us, length us, event | category | flops | bytes accessed | tf_op | source)
XLA Modules:
  0.0 105.7 jit_solution(15746980678644805307)
XLA Ops:
  0.0 2.1 %edges.1 = (f32[16,64,128]{2,1,0:T(8,128)}, f32[16,64,128]{2,1,0:T(8,128)}) custom-call(s32[1]{0:T(128)} %bitcast.1.block, f32[48,64,128]{2,1,0:T(8,128)} %estimate_ref.3), custom_call_target="tpu_custom_call" | custom-call | flops 1000 | bytes 1048576 | tf_op jit(solution)/shard_map/edges/pallas_call | solution.py:69
  2.1 7.6 %collective-permute-start = (f32[16,64,128]{2,1,0:T(8,128)}, f32[16,64,128]{2,1,0:T(8,128)S(1)}, u32[]{:S(2)}, u32[]{:S(2)}) collective-permute-start(f32[16,64,128]{2,1,0:T(8,128)} %get-tuple-element.28), channel_id=1, source_target_pairs={{1,2},{3,4},{5,6},{7,8},{9,10},{11,12},{13,14},{15,16},{17,18},{19... | collective-permute-start | bytes 1572872 | tf_op jit(solution)/shard_map/ppermute | solution.py:41
  10.4 1.3 %roll_rows.1 = f32[3072,128]{1,0:T(8,128)} custom-call(s32[1]{0:T(128)S(6)} %copy.10.shift_ref, f32[3072,128]{1,0:T(8,128)S(1)} %bitcast.18), custom_call_target="tpu_custom_call" | custom-call | flops 1000000 | bytes 3145728 | tf_op jit(solution)/shard_map/roll_rows/pallas_call | solution.py:110
  11.8 6.0 %all-to-all-start = ((f32[64,48,128]{2,1,0:T(8,128)}), f32[64,48,128]{2,1,0:T(8,128)}, u32[]{:S(2)}, u32[]{:S(2)}) async-start(f32[64,48,128]{2,1,0:T(8,128)} %bitcast.3), calls=%async_computation | async-start | bytes 3145728 | tf_op jit(solution)/shard_map/all_to_all | solution.py:414
  17.8 1.9 %make_bands.1 = (bf16[64,192]{1,0:T(8,128)(2,1)S(1)}, bf16[64,192]{1,0:T(8,128)(2,1)S(1)}, bf16[256,256]{1,0:T(8,128)(2,1)S(1)}, bf16[256,256]{1,0:T(8,128)(2,1)...) custom-call(s32[1]{0:T(128)} %bitcast.group, s32[1]{0:T(128)} %bitcast.1.block, s32[1]{0:T(128)S(6)} %copy.10.shift_ref, ...), custom_call_target="tpu_custom_call" | custom-call | tf_op jit(solution)/shard_map/make_bands/pallas_call | solution.py:186
  23.4 7.0 %forward.1.predicted_ref = f32[64,48,128]{2,1,0:T(8,128)S(1)} custom-call(f32[16,64,128]{2,1,0:T(8,128)S(1)} %copy-done.7, f32[48,64,128]{2,1,0:T(8,128)S(1)} %copy-done, f32[16,64,128]{2,1,0:T(8,128)S(1)} %copy-done.9, bf16[64,192]{1,0:T(8,128)(2,1)S(1)} %get-tuple-element.30.yf_ref, bf16[256,256]{1,0:T(8,128)(2,1)S(1)} %get-tuple-element.31.zf_ref, ...), custom_call_target="tpu_custom_call" | custom-call | flops 199999995904 | bytes 6291456 | tf_op jit(solution)/shard_map/forward/pallas_call | solution.py:240
  30.4 26.7 %all-to-all-done.seen_ref = f32[64,48,128]{2,1,0:T(8,128)} async-done(((f32[64,48,128]{2,1,0:T(8,128)}), f32[64,48,128]{2,1,0:T(8,128)}, u32[]{:S(2)}, u32[]{:S(2)}) %all-to-all-start) | async-done | bytes 1572896 | tf_op jit(solution)/shard_map/all_to_all | solution.py:414
  57.1 3.7 %quotient.1 = (f32[16,64,128]{2,1,0:T(8,128)S(1)}, f32[16,64,128]{2,1,0:T(8,128)S(1)}, f32[16,64,128]{2,1,0:T(8,128)S(1)}, f32[16,16,128]{2,1,0:T(8,128)S(1)}, f32[16,48,128]{2,1,0:T(8,128)S(1)}) custom-call(s32[1]{0:T(128)} %bitcast.1.block, s32[1]{0:T(128)S(6)} %copy.10.shift_ref, s32[1,2]{1,0:T(1,128)S(1)} %copy-done.5, ...), custom_call_target="tpu_custom_call" | custom-call | flops 1000 | bytes 1000 | tf_op jit(solution)/shard_map/quotient/pallas_call | solution.py:296
  61.2 1.8 %collective-permute-start.5 = (f32[16,16,128]{2,1,0:T(8,128)S(1)}, f32[16,16,128]{2,1,0:T(8,128)S(1)}, u32[]{:S(2)}, u32[]{:S(2)}) collective-permute-start(f32[16,16,128]{2,1,0:T(8,128)S(1)} %get-tuple-element.43), channel_id=1, source_target_pairs={{1,2},{3,4},{5,6},{7,8},{9,10},{11,12},{13,14},{15,16},{17,18},{19... | collective-permute-start | bytes 393224 | tf_op jit(solution)/shard_map/ppermute | solution.py:41
  63.1 3.3 %collective-permute-start.2 = (f32[16,48,128]{2,1,0:T(8,128)S(1)}, f32[16,48,128]{2,1,0:T(8,128)S(1)}, u32[]{:S(2)}, u32[]{:S(2)}) collective-permute-start(f32[16,48,128]{2,1,0:T(8,128)S(1)} %get-tuple-element.35), channel_id=1, source_target_pairs={{1,2},{3,4},{5,6},{7,8},{9,10},{11,12},{13,14},{15,16},{17,18},{19... | collective-permute-start | bytes 1179656 | tf_op jit(solution)/shard_map/ppermute | solution.py:41
  66.3 2.6 %collective-permute-done.5 = f32[16,16,128]{2,1,0:T(8,128)S(1)} collective-permute-done((f32[16,16,128]{2,1,0:T(8,128)S(1)}, f32[16,16,128]{2,1,0:T(8,128)S(1)}, u32[]{:S(2)}, u32[]{:S(2)}) %collective-permute-start.5) | collective-permute-done | bytes 131104 | tf_op jit(solution)/shard_map/ppermute | solution.py:41
  69.8 1.8 %collective-permute-start.7 = (f32[8,48,128]{2,1,0:T(8,128)S(1)}, f32[8,48,128]{2,1,0:T(8,128)S(1)}, u32[]{:S(2)}, u32[]{:S(2)}) collective-permute-start(f32[8,48,128]{2,1,0:T(8,128)S(1)} %get-tuple-element.45), channel_id=1, source_target_pairs={{0,192},{64,0},{128,64},{192,128},{1,193},{65,1},{129,65},{193,129... | collective-permute-start | bytes 589832 | tf_op jit(solution)/shard_map/ppermute | solution.py:406
  71.6 2.0 %collective-permute-done.2 = f32[16,48,128]{2,1,0:T(8,128)S(1)} collective-permute-done((f32[16,48,128]{2,1,0:T(8,128)S(1)}, f32[16,48,128]{2,1,0:T(8,128)S(1)}, u32[]{:S(2)}, u32[]{:S(2)}) %collective-permute-start.2) | collective-permute-done | bytes 393248 | tf_op jit(solution)/shard_map/ppermute | solution.py:41
  75.7 2.1 %collective-permute-done.7 = f32[8,48,128]{2,1,0:T(8,128)S(1)} collective-permute-done((f32[8,48,128]{2,1,0:T(8,128)S(1)}, f32[8,48,128]{2,1,0:T(8,128)S(1)}, u32[]{:S(2)}, u32[]{:S(2)}) %collective-permute-start.7) | collective-permute-done | bytes 196640 | tf_op jit(solution)/shard_map/ppermute | solution.py:406
  77.9 1.5 %collective-permute-start.8 = (f32[8,48,128]{2,1,0:T(8,128)S(1)}, f32[8,48,128]{2,1,0:T(8,128)S(1)}, u32[]{:S(2)}, u32[]{:S(2)}) collective-permute-start(f32[8,48,128]{2,1,0:T(8,128)S(1)} %add.19), channel_id=1, source_target_pairs={{0,64},{64,128},{128,192},{192,0},{1,65},{65,129},{129,193},{193,1... | collective-permute-start | bytes 589832 | tf_op jit(solution)/shard_map/ppermute | solution.py:406
  79.3 1.5 %collective-permute-start.11 = (f32[8,48,128]{2,1,0:T(8,128)S(1)}, f32[8,48,128]{2,1,0:T(8,128)S(1)}, u32[]{:S(2)}, u32[]{:S(2)}) collective-permute-start(f32[8,48,128]{2,1,0:T(8,128)S(1)} %get-tuple-element.48), channel_id=1, source_target_pairs={{0,64},{64,128},{128,192},{192,0},{1,65},{65,129},{129,193},{193,1... | collective-permute-start | bytes 589832 | tf_op jit(solution)/shard_map/ppermute | solution.py:406
  81.5 1.5 %collective-permute-done.4 = f32[8,48,128]{2,1,0:T(8,128)S(1)} collective-permute-done((f32[8,48,128]{2,1,0:T(8,128)S(1)}, f32[8,48,128]{2,1,0:T(8,128)S(1)}, u32[]{:S(2)}, u32[]{:S(2)}) %collective-permute-start.4) | collective-permute-done | bytes 196640 | tf_op jit(solution)/shard_map/ppermute | solution.py:406
  83.0 2.5 %collective-permute-done.8 = f32[8,48,128]{2,1,0:T(8,128)S(1)} collective-permute-done((f32[8,48,128]{2,1,0:T(8,128)S(1)}, f32[8,48,128]{2,1,0:T(8,128)S(1)}, u32[]{:S(2)}, u32[]{:S(2)}) %collective-permute-start.8) | collective-permute-done | bytes 196640 | tf_op jit(solution)/shard_map/ppermute | solution.py:406
  85.6 2.5 %collective-permute-start.9 = (f32[8,48,128]{2,1,0:T(8,128)S(1)}, f32[8,48,128]{2,1,0:T(8,128)S(1)}, u32[]{:S(2)}, u32[]{:S(2)}) collective-permute-start(f32[8,48,128]{2,1,0:T(8,128)S(1)} %add_add_fusion.1), channel_id=1, source_target_pairs={{0,64},{64,128},{128,192},{192,0},{1,65},{65,129},{129,193},{193,1... | collective-permute-start | bytes 589832 | tf_op jit(solution)/shard_map/ppermute | solution.py:406
  89.9 3.1 %collective-permute-start.15 = (f32[8,48,128]{2,1,0:T(8,128)S(1)}, f32[8,48,128]{2,1,0:T(8,128)S(1)}, u32[]{:S(2)}, u32[]{:S(2)}) collective-permute-start(f32[8,48,128]{2,1,0:T(8,128)S(1)} %add_add_fusion), channel_id=1, source_target_pairs={{0,64},{64,128},{128,192},{192,0},{1,65},{65,129},{129,193},{193,1... | collective-permute-start | bytes 589832 | tf_op jit(solution)/shard_map/ppermute | solution.py:406
  93.4 3.4 %collective-permute-start.10 = (f32[8,48,128]{2,1,0:T(8,128)S(1)}, f32[8,48,128]{2,1,0:T(8,128)S(1)}, u32[]{:S(2)}, u32[]{:S(2)}) collective-permute-start(f32[8,48,128]{2,1,0:T(8,128)S(1)} %collective-permute-done.9), channel_id=1, source_target_pairs={{0,64},{64,128},{128,192},{192,0},{1,65},{65,129},{129,193},{193,1... | collective-permute-start | bytes 589832 | tf_op jit(solution)/shard_map/ppermute | solution.py:406
  97.7 2.1 %collective-permute-done.16 = f32[8,48,128]{2,1,0:T(8,128)S(1)} collective-permute-done((f32[8,48,128]{2,1,0:T(8,128)S(1)}, f32[8,48,128]{2,1,0:T(8,128)S(1)}, u32[]{:S(2)}, u32[]{:S(2)}) %collective-permute-start.16) | collective-permute-done | bytes 196640 | tf_op jit(solution)/shard_map/ppermute | solution.py:406
  99.8 1.8 %finish.1.rest_2_ = f32[48,64,128]{2,1,0:T(8,128)} custom-call(s32[1]{0:T(128)} %bitcast.group, f32[48,64,128]{2,1,0:T(8,128)S(1)} %copy-done, f32[384,128]{1,0:T(8,128)S(1)} %bitcast.19, f32[384,128]{1,0:T(8,128)S(1)} %bitcast.20, f32[384,128]{1,0:T(8,128)S(1)} %bitcast.30, f32[384,128]{1,0:T(8,128)S(1)} %bitcast.33, f32[384,128]{1,0:T(8,128)S(1)} %bitcast.32, ...), custom_call_target="tpu_custom_call" | custom-call | flops 1000 | bytes 1000 | tf_op jit(solution)/shard_map/finish/pallas_call | solution.py:382
  101.6 3.0 %collective-permute-done.14 = f32[8,48,128]{2,1,0:T(8,128)S(1)} collective-permute-done((f32[8,48,128]{2,1,0:T(8,128)S(1)}, f32[8,48,128]{2,1,0:T(8,128)S(1)}, u32[]{:S(2)}, u32[]{:S(2)}) %collective-permute-start.14) | collective-permute-done | bytes 196640 | tf_op jit(solution)/shard_map/ppermute | solution.py:406
  (45 shorter events, 11.9 us)
Async XLA Ops:
  0.0 10.4 %copy-start.1 = (f32[1,1,3072,128]{3,2,1,0:T(8,128)S(1)}, f32[1,1,3072,128]{3,2,1,0:T(8,128)}, u32[]{:S(2)}) copy-start(f32[1,1,3072,128]{3,2,1,0:T(8,128)} %param.8) | copy-start | bytes 4718596
  2.1 17.5 %collective-permute-start = (f32[16,64,128]{2,1,0:T(8,128)}, f32[16,64,128]{2,1,0:T(8,128)S(1)}, u32[]{:S(2)}, u32[]{:S(2)}) collective-permute-start(f32[16,64,128]{2,1,0:T(8,128)} %get-tuple-element.28), channel_id=1, source_target_pairs={{1,2},{3,4},{5,6},{7,8},{9,10},{11,12},{13,14},{15,16},{17,18},{19... | collective-permute-start | bytes 1572872 | tf_op jit(solution)/shard_map/ppermute | solution.py:41
  9.7 10.8 %collective-permute-start.1 = (f32[16,64,128]{2,1,0:T(8,128)}, f32[16,64,128]{2,1,0:T(8,128)S(1)}, u32[]{:S(2)}, u32[]{:S(2)}) collective-permute-start(f32[16,64,128]{2,1,0:T(8,128)} %get-tuple-element.29), channel_id=1, source_target_pairs={{0,1},{2,3},{4,5},{6,7},{8,9},{10,11},{12,13},{14,15},{16,17},{18,... | collective-permute-start | bytes 1572872 | tf_op jit(solution)/shard_map/ppermute | solution.py:41
  11.7 6.0 %copy-start.2 = (f32[1,31]{1,0:T(1,128)S(1)}, f32[1,31]{1,0:T(1,128)}, u32[]{:S(2)}) copy-start(f32[1,31]{1,0:T(1,128)} %x_ref.1) | copy-start | bytes 376
  11.7 6.0 %copy-start.3 = (f32[1,31]{1,0:T(1,128)S(1)}, f32[1,31]{1,0:T(1,128)}, u32[]{:S(2)}) copy-start(f32[1,31]{1,0:T(1,128)} %y_ref.1) | copy-start | bytes 376
  11.7 6.0 %copy-start.4 = (f32[1,61]{1,0:T(1,128)S(1)}, f32[1,61]{1,0:T(1,128)}, u32[]{:S(2)}) copy-start(f32[1,61]{1,0:T(1,128)} %z_ref.1) | copy-start | bytes 736
  11.7 9.5 %copy-start = (f32[48,64,128]{2,1,0:T(8,128)S(1)}, f32[48,64,128]{2,1,0:T(8,128)}, u32[]{:S(2)}) copy-start(f32[48,64,128]{2,1,0:T(8,128)} %estimate_ref.3) | copy-start | bytes 4718596
  11.8 45.3 %all-to-all-start = ((f32[64,48,128]{2,1,0:T(8,128)}), f32[64,48,128]{2,1,0:T(8,128)}, u32[]{:S(2)}, u32[]{:S(2)}) async-start(f32[64,48,128]{2,1,0:T(8,128)} %bitcast.3), calls=%async_computation | async-start | bytes 3145728 | tf_op jit(solution)/shard_map/all_to_all | solution.py:414
  23.4 33.7 %copy-start.5 = (s32[1,2]{1,0:T(1,128)S(1)}, s32[1,2]{1,0:T(1,128)}, u32[]{:S(2)}) copy-start(s32[1,2]{1,0:T(1,128)} %box_ref.1) | copy-start | bytes 28
  60.8 8.2 %collective-permute-start.3 = (f32[16,64,128]{2,1,0:T(8,128)S(1)}, f32[16,64,128]{2,1,0:T(8,128)S(1)}, u32[]{:S(2)}, u32[]{:S(2)}) collective-permute-start(f32[16,64,128]{2,1,0:T(8,128)S(1)} %get-tuple-element.38), channel_id=1, source_target_pairs={{0,1},{2,3},{4,5},{6,7},{8,9},{10,11},{12,13},{14,15},{16,17},{18,... | collective-permute-start | bytes 1572872 | tf_op jit(solution)/shard_map/ppermute | solution.py:41
  61.2 7.7 %collective-permute-start.5 = (f32[16,16,128]{2,1,0:T(8,128)S(1)}, f32[16,16,128]{2,1,0:T(8,128)S(1)}, u32[]{:S(2)}, u32[]{:S(2)}) collective-permute-start(f32[16,16,128]{2,1,0:T(8,128)S(1)} %get-tuple-element.43), channel_id=1, source_target_pairs={{1,2},{3,4},{5,6},{7,8},{9,10},{11,12},{13,14},{15,16},{17,18},{19... | collective-permute-start | bytes 393224 | tf_op jit(solution)/shard_map/ppermute | solution.py:41
  63.1 10.5 %collective-permute-start.2 = (f32[16,48,128]{2,1,0:T(8,128)S(1)}, f32[16,48,128]{2,1,0:T(8,128)S(1)}, u32[]{:S(2)}, u32[]{:S(2)}) collective-permute-start(f32[16,48,128]{2,1,0:T(8,128)S(1)} %get-tuple-element.35), channel_id=1, source_target_pairs={{1,2},{3,4},{5,6},{7,8},{9,10},{11,12},{13,14},{15,16},{17,18},{19... | collective-permute-start | bytes 1179656 | tf_op jit(solution)/shard_map/ppermute | solution.py:41
  69.5 6.2 %collective-permute-start.6 = (f32[8,48,128]{2,1,0:T(8,128)S(1)}, f32[8,48,128]{2,1,0:T(8,128)S(1)}, u32[]{:S(2)}, u32[]{:S(2)}) collective-permute-start(f32[8,48,128]{2,1,0:T(8,128)S(1)} %get-tuple-element.44), channel_id=1, source_target_pairs={{0,64},{64,128},{128,192},{192,0},{1,65},{65,129},{129,193},{193,1... | collective-permute-start | bytes 589832 | tf_op jit(solution)/shard_map/ppermute | solution.py:406
  69.8 8.1 %collective-permute-start.7 = (f32[8,48,128]{2,1,0:T(8,128)S(1)}, f32[8,48,128]{2,1,0:T(8,128)S(1)}, u32[]{:S(2)}, u32[]{:S(2)}) collective-permute-start(f32[8,48,128]{2,1,0:T(8,128)S(1)} %get-tuple-element.45), channel_id=1, source_target_pairs={{0,192},{64,0},{128,64},{192,128},{1,193},{65,1},{129,65},{193,129... | collective-permute-start | bytes 589832 | tf_op jit(solution)/shard_map/ppermute | solution.py:406
  74.9 8.1 %collective-permute-start.4 = (f32[8,48,128]{2,1,0:T(8,128)S(1)}, f32[8,48,128]{2,1,0:T(8,128)S(1)}, u32[]{:S(2)}, u32[]{:S(2)}) collective-permute-start(f32[8,48,128]{2,1,0:T(8,128)S(1)} %get-tuple-element.41), channel_id=1, source_target_pairs={{0,192},{64,0},{128,64},{192,128},{1,193},{65,1},{129,65},{193,129... | collective-permute-start | bytes 589832 | tf_op jit(solution)/shard_map/ppermute | solution.py:406
  77.9 7.7 %collective-permute-start.8 = (f32[8,48,128]{2,1,0:T(8,128)S(1)}, f32[8,48,128]{2,1,0:T(8,128)S(1)}, u32[]{:S(2)}, u32[]{:S(2)}) collective-permute-start(f32[8,48,128]{2,1,0:T(8,128)S(1)} %add.19), channel_id=1, source_target_pairs={{0,64},{64,128},{128,192},{192,0},{1,65},{65,129},{129,193},{193,1... | collective-permute-start | bytes 589832 | tf_op jit(solution)/shard_map/ppermute | solution.py:406
  79.3 9.9 %collective-permute-start.11 = (f32[8,48,128]{2,1,0:T(8,128)S(1)}, f32[8,48,128]{2,1,0:T(8,128)S(1)}, u32[]{:S(2)}, u32[]{:S(2)}) collective-permute-start(f32[8,48,128]{2,1,0:T(8,128)S(1)} %get-tuple-element.48), channel_id=1, source_target_pairs={{0,64},{64,128},{128,192},{192,0},{1,65},{65,129},{129,193},{193,1... | collective-permute-start | bytes 589832 | tf_op jit(solution)/shard_map/ppermute | solution.py:406
  80.8 8.7 %collective-permute-start.12 = (f32[8,48,128]{2,1,0:T(8,128)S(1)}, f32[8,48,128]{2,1,0:T(8,128)S(1)}, u32[]{:S(2)}, u32[]{:S(2)}) collective-permute-start(f32[8,48,128]{2,1,0:T(8,128)S(1)} %add.22), channel_id=1, source_target_pairs={{0,192},{64,0},{128,64},{192,128},{1,193},{65,1},{129,65},{193,129... | collective-permute-start | bytes 589832 | tf_op jit(solution)/shard_map/ppermute | solution.py:406
  85.6 7.9 %collective-permute-start.9 = (f32[8,48,128]{2,1,0:T(8,128)S(1)}, f32[8,48,128]{2,1,0:T(8,128)S(1)}, u32[]{:S(2)}, u32[]{:S(2)}) collective-permute-start(f32[8,48,128]{2,1,0:T(8,128)S(1)} %add_add_fusion.1), channel_id=1, source_target_pairs={{0,64},{64,128},{128,192},{192,0},{1,65},{65,129},{129,193},{193,1... | collective-permute-start | bytes 589832 | tf_op jit(solution)/shard_map/ppermute | solution.py:406
  89.6 8.1 %collective-permute-start.13 = (f32[8,48,128]{2,1,0:T(8,128)S(1)}, f32[8,48,128]{2,1,0:T(8,128)S(1)}, u32[]{:S(2)}, u32[]{:S(2)}) collective-permute-start(f32[8,48,128]{2,1,0:T(8,128)S(1)} %add_add_fusion), channel_id=1, source_target_pairs={{0,192},{64,0},{128,64},{192,128},{1,193},{65,1},{129,65},{193,129... | collective-permute-start | bytes 589832 | tf_op jit(solution)/shard_map/ppermute | solution.py:406
  89.7 10.1 %collective-permute-start.16 = (f32[8,48,128]{2,1,0:T(8,128)S(1)}, f32[8,48,128]{2,1,0:T(8,128)S(1)}, u32[]{:S(2)}, u32[]{:S(2)}) collective-permute-start(f32[8,48,128]{2,1,0:T(8,128)S(1)} %add_add_fusion.1), channel_id=1, source_target_pairs={{0,192},{64,0},{128,64},{192,128},{1,193},{65,1},{129,65},{193,129... | collective-permute-start | bytes 589832 | tf_op jit(solution)/shard_map/ppermute | solution.py:406
  89.9 9.9 %collective-permute-start.15 = (f32[8,48,128]{2,1,0:T(8,128)S(1)}, f32[8,48,128]{2,1,0:T(8,128)S(1)}, u32[]{:S(2)}, u32[]{:S(2)}) collective-permute-start(f32[8,48,128]{2,1,0:T(8,128)S(1)} %add_add_fusion), channel_id=1, source_target_pairs={{0,64},{64,128},{128,192},{192,0},{1,65},{65,129},{129,193},{193,1... | collective-permute-start | bytes 589832 | tf_op jit(solution)/shard_map/ppermute | solution.py:406
  93.4 8.2 %collective-permute-start.10 = (f32[8,48,128]{2,1,0:T(8,128)S(1)}, f32[8,48,128]{2,1,0:T(8,128)S(1)}, u32[]{:S(2)}, u32[]{:S(2)}) collective-permute-start(f32[8,48,128]{2,1,0:T(8,128)S(1)} %collective-permute-done.9), channel_id=1, source_target_pairs={{0,64},{64,128},{128,192},{192,0},{1,65},{65,129},{129,193},{193,1... | collective-permute-start | bytes 589832 | tf_op jit(solution)/shard_map/ppermute | solution.py:406
  97.7 6.9 %collective-permute-start.14 = (f32[8,48,128]{2,1,0:T(8,128)S(1)}, f32[8,48,128]{2,1,0:T(8,128)S(1)}, u32[]{:S(2)}, u32[]{:S(2)}) collective-permute-start(f32[8,48,128]{2,1,0:T(8,128)S(1)} %collective-permute-done.13), channel_id=1, source_target_pairs={{0,192},{64,0},{128,64},{192,128},{1,193},{65,1},{129,65},{193,129... | collective-permute-start | bytes 589832 | tf_op jit(solution)/shard_map/ppermute | solution.py:406
  (4 other events, 3.7 us)

commit v5 on v4

--- a/solution.py
+++ b/solution.py
@@ -44,20 +44,52 @@
 PARTS = 4
 
 
-def edges_kernel(block, estimate, far, near, held, in_sems, out_sems):
+def depart_kernel(
+    block, shift_hbm, source, estimate, target, far, near, shift_ref, padded, rolled, held, in_sems, out_sems, edge_in, edge_out
+):
     odd = lax.rem(block[0], 2)
-    half = HALO // 2
+    size, half = NX // PARTS, HALO // 2
+    shift_copy = pltpu.make_async_copy(shift_hbm, shift_ref, in_sems.at[PARTS + 2])
+    fetches = [
+        pltpu.make_async_copy(source.at[pl.ds(NX - SMAX, SMAX)], padded.at[pl.ds(0, SMAX)], in_sems.at[PARTS]),
+        pltpu.make_async_copy(source.at[pl.ds(0, SMAX)], padded.at[pl.ds(SMAX + NX, SMAX)], in_sems.at[PARTS + 1]),
+    ]
+    fetches += [
+        pltpu.make_async_copy(
+            source.at[pl.ds(part * size, size)], padded.at[pl.ds(SMAX + part * size, size)], in_sems.at[part]
+        )
+        for part in range(PARTS)
+    ]
     takes, gives = [], []
     for index, (first, out_ref) in enumerate(((odd, far), (1 - odd, near))):
         for part in range(2):
             slot = 2 * index + part
             rows = estimate.at[pl.ds(first * (SLAB - HALO) + part * half, half)]
-            takes.append(pltpu.make_async_copy(rows, held.at[slot], in_sems.at[slot]))
+            takes.append(pltpu.make_async_copy(rows, held.at[slot], edge_in.at[slot]))
             gives.append(
-                pltpu.make_async_copy(held.at[slot], out_ref.at[pl.ds(part * half, half)], out_sems.at[slot])
+                pltpu.make_async_copy(held.at[slot], out_ref.at[pl.ds(part * half, half)], edge_out.at[slot])
             )
-    for copy in takes:
+    for copy in [shift_copy] + fetches + takes:
         copy.start()
+    shift_copy.wait()
+    for copy in fetches[:3]:
+        copy.wait()
+    start = SMAX - shift_ref[0]
+    for part in range(PARTS):
+        if part + 1 < PARTS:
+            fetches[part + 3].wait()
+
+        def move(block, carry, part=part):
+            base = part * size + block * 128
+            rolled[pl.ds(pl.multiple_of(base, 128), 128), :] = padded[pl.ds(start + base, 128), :]
+            return carry
+
+        lax.fori_loop(0, size // 128, move, 0)
+        copy = pltpu.make_async_copy(
+            rolled.at[pl.ds(part * size, size)], target.at[pl.ds(part * size, size)], out_sems.at[part]
+        )
+        copy.start()
+        gives.append(copy)
     for take, give in zip(takes, gives):
         take.wait()
         give.start()
@@ -65,62 +97,27 @@
         give.wait()
 
 
-def edges(block, estimate):
-    return pl.pallas_call(
-        edges_kernel,
-        out_shape=[jax.ShapeDtypeStruct((HALO, NY, NZ), F32)] * 2,
-        in_specs=[SMEM_SPEC, ANY_SPEC],
-        out_specs=[ANY_SPEC] * 2,
+def depart(block, shift, recorded, estimate):
+    edge = jax.ShapeDtypeStruct((HALO, NY, NZ), F32)
+    return pl.pallas_call(
+        depart_kernel,
+        out_shape=[jax.ShapeDtypeStruct((NX, NZ), F32), edge, edge],
+        in_specs=[SMEM_SPEC, ANY_SPEC, ANY_SPEC, ANY_SPEC],
+        out_specs=[ANY_SPEC] * 3,
         scratch_shapes=[
+            pltpu.SMEM((1,), jnp.int32),
+            pltpu.VMEM((NX + 2 * SMAX, NZ), F32),
+            pltpu.VMEM((NX, NZ), F32),
             pltpu.VMEM((4, HALO // 2, NY, NZ), F32),
+            pltpu.SemaphoreType.DMA((PARTS + 3,)),
+            pltpu.SemaphoreType.DMA((PARTS,)),
             pltpu.SemaphoreType.DMA((4,)),
             pltpu.SemaphoreType.DMA((4,)),
         ],
         compiler_params=pltpu.CompilerParams(vmem_limit_bytes=60 * 1024 * 1024),
         cost_estimate=pl.CostEstimate(flops=1000, bytes_accessed=2**20, transcendentals=0),
-        name="edges",
-    )(block, estimate)
-
-
-def roll_kernel(shift_ref, source, target, padded, rolled, sems):
-    padded[pl.ds(SMAX, NX), :] = source[...]
-    padded[pl.ds(0, SMAX), :] = source[pl.ds(NX - SMAX, SMAX), :]
-    padded[pl.ds(SMAX + NX, SMAX), :] = source[pl.ds(0, SMAX), :]
-    start = SMAX - shift_ref[0]
-    size = NX // PARTS
-    copies = []
-    for part in range(PARTS):
-
-        def move(block, carry, part=part):
-            base = part * size + block * 128
-            rolled[pl.ds(pl.multiple_of(base, 128), 128), :] = padded[pl.ds(start + base, 128), :]
-            return carry
-
-        lax.fori_loop(0, size // 128, move, 0)
-        copy = pltpu.make_async_copy(
-            rolled.at[pl.ds(part * size, size)], target.at[pl.ds(part * size, size)], sems.at[part]
-        )
-        copy.start()
-        copies.append(copy)
-    for copy in copies:
-        copy.wait()
-
-
-def roll_rows(recorded, shift):
-    return pl.pallas_call(
-        roll_kernel,
-        out_shape=jax.ShapeDtypeStruct((NX, NZ), F32),
-        in_specs=[SMEM_SPEC, VMEM_SPEC],
-        out_specs=ANY_SPEC,
-        scratch_shapes=[
-            pltpu.VMEM((NX + 2 * SMAX, NZ), F32),
-            pltpu.VMEM((NX, NZ), F32),
-            pltpu.SemaphoreType.DMA((PARTS,)),
-        ],
-        compiler_params=PARAMS,
-        cost_estimate=pl.CostEstimate(flops=10**6, bytes_accessed=3 * 2**20, transcendentals=0),
-        name="roll_rows",
-    )(shift, recorded.reshape(NX, NZ))
+        name="depart",
+    )(block, shift, recorded.reshape(NX, NZ), estimate)
 
 
 def pick_taps(taps_ref, count, tap_index, valid):
@@ -265,9 +262,9 @@
     ]
     for copy in copies:
         copy.start()
-    for copy in copies:
-        copy.wait()
     for index, first in enumerate(firsts):
+        for copy in copies[index * PARTS : (index + 1) * PARTS]:
+            copy.wait()
         row = block[0] * SLAB + first - shift_ref[0] + iota((HALO, NZ), 0)
         row = jnp.where(row < 0, row + NX, row)
         row = jnp.where(row >= NX, row - NX, row)
@@ -408,9 +405,8 @@
 
 def body(estimate, recorded, psf_x, psf_y, psf_z, view_shifts, view_boxes):
     group, block = lax.axis_index("group").reshape(1), lax.axis_index("block").reshape(1)
-    far, near = edges(block, estimate)
+    rolled, far, near = depart(block, view_shifts, recorded, estimate)
     far, near = swap(far, True), swap(near, False)
-    rolled = roll_rows(recorded, view_shifts)
     seen = lax.all_to_all(rolled.reshape(NY, SLAB, NZ), "block", 0, 0)
     yf, yb, zf, zb, xf, xb = make_bands(group, block, view_shifts, psf_x, psf_y, psf_z)
     predicted = forward(far, estimate, near, yf, zf, xf)
@@ -428,6 +424,7 @@
     sum_a = turn(next_a + far_a, "group", 1)
     sum_b = turn(prev_b + far_b, "group", -1)
     near_b, near_a = turn(near_b, "group", 1), turn(near_a, "group", -1)
+    near_b, near_a = lax.optimization_barrier((near_b, near_a))
     own_a = own_a + near_a + sum_a
     own_b = own_b + near_b + sum_b
 

time: 106 us -> 102 us (0.962)
  waiting for transfers between devices: 45.4 us -> 43.5 us
  starting transfers between devices: 34.8 us -> 33.7 us
    ppermute x12, waiting for transfers between devices: 14.1 us -> 12.2 us  [turn(): lax.ppermute(block, axis, [(i, (i + step) % size) for i in range(size)])]
    ppermute x12, starting transfers between devices: 15.8 us -> 14.6 us  [turn(): lax.ppermute(block, axis, [(i, (i + step) % size) for i in range(size)])]
    pallas_call x2 -> x1, Pallas kernels: 3.45 us -> 3.06 us  [depart(): pl.pallas_call(depart_kernel, out_shape=[jax.ShapeDtypeStruct((NX, NZ), F...]
    unnamed x20 -> x18, local copies, waits for them, and re-layouts: 3.7 us -> 3.7 us
  transfers between devices with their start and end apart: 18 -> 18, of which waited for: 12 -> 10; matrix products, arithmetic and copies ran while one was open for 0% -> 0% of each run, Pallas kernels for 13% -> 12%
where the time goes in v5:
time: 102 us
  waiting for transfers between devices  43.5 us (43%)
  starting transfers between devices  33.7 us (33%)
  Pallas kernels  20.1 us (20%)
  local copies, waits for them, and re-layouts  3.7 us (4%)
    all_to_all x1, waiting for transfers between devices, body(): seen = lax.all_to_all(rolled.reshape(NY, SLAB, NZ), 'block', 0, 0)  26.6 us
    ppermute x12, starting transfers between devices, turn(): lax.ppermute(block, axis, [(i, (i + step) % size) for i in range(size)])  14.6 us
    ppermute x5, starting transfers between devices, swap(): lax.ppermute(block, 'block', pairs + [(target, source) for source, target...  13.1 us
    ppermute x12, waiting for transfers between devices, turn(): lax.ppermute(block, axis, [(i, (i + step) % size) for i in range(size)])  12.2 us
    pallas_call x1, Pallas kernels, forward(): pl.pallas_call(forward_kernel, out_shape=jax.ShapeDtypeStruct((NY, SLAB,...  7.04 us
    all_to_all x1, starting transfers between devices, body(): seen = lax.all_to_all(rolled.reshape(NY, SLAB, NZ), 'block', 0, 0)  5.94 us
    ppermute x5, waiting for transfers between devices, swap(): lax.ppermute(block, 'block', pairs + [(target, source) for source, target...  4.65 us
    unnamed x18, local copies, waits for them, and re-layouts  3.7 us
  transfers between devices with their start and end apart: 18, of which 10 were waited for; matrix products, arithmetic and copies ran while one was open for 0% of the time, Pallas kernels for 12%

profile of v5, /device:TPU:24, one launch (start us, length us, event | category | flops | bytes accessed | tf_op | source)
XLA Modules:
  0.0 102.0 jit_solution(14817291201671611801)
XLA Ops:
  0.7 3.1 %depart.1 = (f32[3072,128]{1,0:T(8,128)}, f32[16,64,128]{2,1,0:T(8,128)}, f32[16,64,128]{2,1,0:T(8,128)}) custom-call(s32[1]{0:T(128)} %bitcast.1.block, s32[1]{0:T(128)S(6)} %copy.10.shift_hbm.shift_ref, f32[3072,128]{1,0:T(8,128)} %bitcast.36, f32[48,64,128]{2,1,0:T(8,128)} %estimate_ref.3), custom_call_target="tpu_custom_call" | custom-call | flops 1000 | bytes 1048576 | tf_op jit(solution)/shard_map/depart/pallas_call | solution.py:102
  3.7 7.6 %collective-permute-start = (f32[16,64,128]{2,1,0:T(8,128)}, f32[16,64,128]{2,1,0:T(8,128)S(1)}, u32[]{:S(2)}, u32[]{:S(2)}) collective-permute-start(f32[16,64,128]{2,1,0:T(8,128)} %get-tuple-element.32), channel_id=1, source_target_pairs={{1,2},{3,4},{5,6},{7,8},{9,10},{11,12},{13,14},{15,16},{17,18},{19... | collective-permute-start | bytes 1572872 | tf_op jit(solution)/shard_map/ppermute | solution.py:41
  11.3 5.9 %all-to-all-start = ((f32[64,48,128]{2,1,0:T(8,128)}), f32[64,48,128]{2,1,0:T(8,128)}, u32[]{:S(2)}, u32[]{:S(2)}) async-start(f32[64,48,128]{2,1,0:T(8,128)} %bitcast.37), calls=%async_computation | async-start | bytes 3145728 | tf_op jit(solution)/shard_map/all_to_all | solution.py:410
  17.3 1.9 %make_bands.1 = (bf16[64,192]{1,0:T(8,128)(2,1)S(1)}, bf16[64,192]{1,0:T(8,128)(2,1)S(1)}, bf16[256,256]{1,0:T(8,128)(2,1)S(1)}, bf16[256,256]{1,0:T(8,128)(2,1)...) custom-call(s32[1]{0:T(128)} %bitcast.group, s32[1]{0:T(128)} %bitcast.1.block, ...), custom_call_target="tpu_custom_call" | custom-call | tf_op jit(solution)/shard_map/make_bands/pallas_call | solution.py:183
  22.9 7.0 %forward.1.predicted_ref = f32[64,48,128]{2,1,0:T(8,128)S(1)} custom-call(f32[16,64,128]{2,1,0:T(8,128)S(1)} %copy-done.6, f32[48,64,128]{2,1,0:T(8,128)S(1)} %copy-done, f32[16,64,128]{2,1,0:T(8,128)S(1)} %copy-done.8, bf16[64,192]{1,0:T(8,128)(2,1)S(1)} %get-tuple-element.34.yf_ref, bf16[256,256]{1,0:T(8,128)(2,1)S(1)} %get-tuple-element.35.zf_ref, ...), custom_call_target="tpu_custom_call" | custom-call | flops 199999995904 | bytes 6291456 | tf_op jit(solution)/shard_map/forward/pallas_call | solution.py:237
  30.0 26.6 %all-to-all-done.seen_ref = f32[64,48,128]{2,1,0:T(8,128)} async-done(((f32[64,48,128]{2,1,0:T(8,128)}), f32[64,48,128]{2,1,0:T(8,128)}, u32[]{:S(2)}, u32[]{:S(2)}) %all-to-all-start) | async-done | bytes 1572896 | tf_op jit(solution)/shard_map/all_to_all | solution.py:410
  56.6 3.6 %quotient.1 = (f32[16,64,128]{2,1,0:T(8,128)S(1)}, f32[16,64,128]{2,1,0:T(8,128)S(1)}, f32[16,64,128]{2,1,0:T(8,128)S(1)}, f32[16,16,128]{2,1,0:T(8,128)S(1)}, f32[16,48,128]{2,1,0:T(8,128)S(1)}) custom-call(s32[1]{0:T(128)} %bitcast.1.block, s32[1]{0:T(128)S(6)} %copy.10.shift_hbm.shift_ref, s32[1,2]{1,0:T(1,128)S(1)} %copy-done.4, ...), custom_call_target="tpu_custom_call" | custom-call | flops 1000 | bytes 1000 | tf_op jit(solution)/shard_map/quotient/pallas_call | solution.py:293
  60.7 1.8 %collective-permute-start.6 = (f32[16,16,128]{2,1,0:T(8,128)S(1)}, f32[16,16,128]{2,1,0:T(8,128)S(1)}, u32[]{:S(2)}, u32[]{:S(2)}) collective-permute-start(f32[16,16,128]{2,1,0:T(8,128)S(1)} %get-tuple-element.49), channel_id=1, source_target_pairs={{1,2},{3,4},{5,6},{7,8},{9,10},{11,12},{13,14},{15,16},{17,18},{19... | collective-permute-start | bytes 393224 | tf_op jit(solution)/shard_map/ppermute | solution.py:41
  62.5 3.3 %collective-permute-start.2 = (f32[16,48,128]{2,1,0:T(8,128)S(1)}, f32[16,48,128]{2,1,0:T(8,128)S(1)}, u32[]{:S(2)}, u32[]{:S(2)}) collective-permute-start(f32[16,48,128]{2,1,0:T(8,128)S(1)} %get-tuple-element.39), channel_id=1, source_target_pairs={{1,2},{3,4},{5,6},{7,8},{9,10},{11,12},{13,14},{15,16},{17,18},{19... | collective-permute-start | bytes 1179656 | tf_op jit(solution)/shard_map/ppermute | solution.py:41
  65.8 2.6 %collective-permute-done.6 = f32[16,16,128]{2,1,0:T(8,128)S(1)} collective-permute-done((f32[16,16,128]{2,1,0:T(8,128)S(1)}, f32[16,16,128]{2,1,0:T(8,128)S(1)}, u32[]{:S(2)}, u32[]{:S(2)}) %collective-permute-start.6) | collective-permute-done | bytes 131104 | tf_op jit(solution)/shard_map/ppermute | solution.py:41
  69.2 1.8 %collective-permute-start.8 = (f32[8,48,128]{2,1,0:T(8,128)S(1)}, f32[8,48,128]{2,1,0:T(8,128)S(1)}, u32[]{:S(2)}, u32[]{:S(2)}) collective-permute-start(f32[8,48,128]{2,1,0:T(8,128)S(1)} %get-tuple-element.51), channel_id=1, source_target_pairs={{0,192},{64,0},{128,64},{192,128},{1,193},{65,1},{129,65},{193,129... | collective-permute-start | bytes 589832 | tf_op jit(solution)/shard_map/ppermute | solution.py:403
  71.0 2.0 %collective-permute-done.2 = f32[16,48,128]{2,1,0:T(8,128)S(1)} collective-permute-done((f32[16,48,128]{2,1,0:T(8,128)S(1)}, f32[16,48,128]{2,1,0:T(8,128)S(1)}, u32[]{:S(2)}, u32[]{:S(2)}) %collective-permute-start.2) | collective-permute-done | bytes 393248 | tf_op jit(solution)/shard_map/ppermute | solution.py:41
  73.0 1.3 %backward.2 = (f32[8,48,128]{2,1,0:T(8,128)S(1)}, f32[8,48,128]{2,1,0:T(8,128)S(1)}, f32[8,48,128]{2,1,0:T(8,128)S(1)}, f32[8,48,128]{2,1,0:T(8,128)S(1)}, f32[8...) custom-call(f32[768,128]{1,0:T(8,128)S(1)} %bitcast.28, f32[1024,128]{1,0:T(8,128)S(1)} %bitcast.21, ...), custom_call_target="tpu_custom_call" | custom-call | flops 1000 | bytes 1000 | tf_op jit(solution)/shard_map/backward/pallas_call | solution.py:328
  74.6 1.8 %collective-permute-start.5 = (f32[8,48,128]{2,1,0:T(8,128)S(1)}, f32[8,48,128]{2,1,0:T(8,128)S(1)}, u32[]{:S(2)}, u32[]{:S(2)}) collective-permute-start(f32[8,48,128]{2,1,0:T(8,128)S(1)} %get-tuple-element.46), channel_id=1, source_target_pairs={{0,192},{64,0},{128,64},{192,128},{1,193},{65,1},{129,65},{193,129... | collective-permute-start | bytes 589832 | tf_op jit(solution)/shard_map/ppermute | solution.py:403
  78.0 1.2 %collective-permute-start.12 = (f32[8,48,128]{2,1,0:T(8,128)S(1)}, f32[8,48,128]{2,1,0:T(8,128)S(1)}, u32[]{:S(2)}, u32[]{:S(2)}) collective-permute-start(f32[8,48,128]{2,1,0:T(8,128)S(1)} %add.22), channel_id=1, source_target_pairs={{0,192},{64,0},{128,64},{192,128},{1,193},{65,1},{129,65},{193,129... | collective-permute-start | bytes 589832 | tf_op jit(solution)/shard_map/ppermute | solution.py:403
  79.2 1.8 %collective-permute-done.4 = f32[8,48,128]{2,1,0:T(8,128)S(1)} collective-permute-done((f32[8,48,128]{2,1,0:T(8,128)S(1)}, f32[8,48,128]{2,1,0:T(8,128)S(1)}, u32[]{:S(2)}, u32[]{:S(2)}) %collective-permute-start.4) | collective-permute-done | bytes 196640 | tf_op jit(solution)/shard_map/ppermute | solution.py:403
  81.0 1.4 %collective-permute-done.5 = f32[8,48,128]{2,1,0:T(8,128)S(1)} collective-permute-done((f32[8,48,128]{2,1,0:T(8,128)S(1)}, f32[8,48,128]{2,1,0:T(8,128)S(1)}, u32[]{:S(2)}, u32[]{:S(2)}) %collective-permute-start.5) | collective-permute-done | bytes 196640 | tf_op jit(solution)/shard_map/ppermute | solution.py:403
  83.6 1.4 %collective-permute-start.10 = (f32[8,48,128]{2,1,0:T(8,128)S(1)}, f32[8,48,128]{2,1,0:T(8,128)S(1)}, u32[]{:S(2)}, u32[]{:S(2)}) collective-permute-start(f32[8,48,128]{2,1,0:T(8,128)S(1)} %add_add_fusion.1), channel_id=1, source_target_pairs={{0,64},{64,128},{128,192},{192,0},{1,65},{65,129},{129,193},{193,1... | collective-permute-start | bytes 589832 | tf_op jit(solution)/shard_map/ppermute | solution.py:403
  86.6 2.5 %collective-permute-start.15 = (f32[8,48,128]{2,1,0:T(8,128)S(1)}, f32[8,48,128]{2,1,0:T(8,128)S(1)}, u32[]{:S(2)}, u32[]{:S(2)}) collective-permute-start(f32[8,48,128]{2,1,0:T(8,128)S(1)} %add_add_fusion), channel_id=1, source_target_pairs={{0,64},{64,128},{128,192},{192,0},{1,65},{65,129},{129,193},{193,1... | collective-permute-start | bytes 589832 | tf_op jit(solution)/shard_map/ppermute | solution.py:403
  89.1 2.1 %collective-permute-done.10 = f32[8,48,128]{2,1,0:T(8,128)S(1)} collective-permute-done((f32[8,48,128]{2,1,0:T(8,128)S(1)}, f32[8,48,128]{2,1,0:T(8,128)S(1)}, u32[]{:S(2)}, u32[]{:S(2)}) %collective-permute-start.10) | collective-permute-done | bytes 196640 | tf_op jit(solution)/shard_map/ppermute | solution.py:403
  91.2 2.8 %collective-permute-start.11 = (f32[8,48,128]{2,1,0:T(8,128)S(1)}, f32[8,48,128]{2,1,0:T(8,128)S(1)}, u32[]{:S(2)}, u32[]{:S(2)}) collective-permute-start(f32[8,48,128]{2,1,0:T(8,128)S(1)} %collective-permute-done.10), channel_id=1, source_target_pairs={{0,64},{64,128},{128,192},{192,0},{1,65},{65,129},{129,193},{193,1... | collective-permute-start | bytes 589832 | tf_op jit(solution)/shard_map/ppermute | solution.py:403
  94.0 2.2 %collective-permute-done.16 = f32[8,48,128]{2,1,0:T(8,128)S(1)} collective-permute-done((f32[8,48,128]{2,1,0:T(8,128)S(1)}, f32[8,48,128]{2,1,0:T(8,128)S(1)}, u32[]{:S(2)}, u32[]{:S(2)}) %collective-permute-start.16) | collective-permute-done | bytes 196640 | tf_op jit(solution)/shard_map/ppermute | solution.py:403
  96.2 1.8 %finish.1.rest_2_ = f32[48,64,128]{2,1,0:T(8,128)} custom-call(s32[1]{0:T(128)} %bitcast.group, f32[48,64,128]{2,1,0:T(8,128)S(1)} %copy-done, f32[384,128]{1,0:T(8,128)S(1)} %bitcast.18, f32[384,128]{1,0:T(8,128)S(1)} %bitcast.19, f32[384,128]{1,0:T(8,128)S(1)} %bitcast.29, f32[384,128]{1,0:T(8,128)S(1)} %bitcast.32, f32[384,128]{1,0:T(8,128)S(1)} %bitcast.31, ...), custom_call_target="tpu_custom_call" | custom-call | flops 1000 | bytes 1000 | tf_op jit(solution)/shard_map/finish/pallas_call | solution.py:379
  98.0 2.9 %collective-permute-done.14 = f32[8,48,128]{2,1,0:T(8,128)S(1)} collective-permute-done((f32[8,48,128]{2,1,0:T(8,128)S(1)}, f32[8,48,128]{2,1,0:T(8,128)S(1)}, u32[]{:S(2)}, u32[]{:S(2)}) %collective-permute-start.14) | collective-permute-done | bytes 196640 | tf_op jit(solution)/shard_map/ppermute | solution.py:403
  (42 shorter events, 10.5 us)
Async XLA Ops:
  3.7 15.5 %collective-permute-start = (f32[16,64,128]{2,1,0:T(8,128)}, f32[16,64,128]{2,1,0:T(8,128)S(1)}, u32[]{:S(2)}, u32[]{:S(2)}) collective-permute-start(f32[16,64,128]{2,1,0:T(8,128)} %get-tuple-element.32), channel_id=1, source_target_pairs={{1,2},{3,4},{5,6},{7,8},{9,10},{11,12},{13,14},{15,16},{17,18},{19... | collective-permute-start | bytes 1572872 | tf_op jit(solution)/shard_map/ppermute | solution.py:41
  11.3 8.8 %collective-permute-start.1 = (f32[16,64,128]{2,1,0:T(8,128)}, f32[16,64,128]{2,1,0:T(8,128)S(1)}, u32[]{:S(2)}, u32[]{:S(2)}) collective-permute-start(f32[16,64,128]{2,1,0:T(8,128)} %get-tuple-element.33), channel_id=1, source_target_pairs={{0,1},{2,3},{4,5},{6,7},{8,9},{10,11},{12,13},{14,15},{16,17},{18,... | collective-permute-start | bytes 1572872 | tf_op jit(solution)/shard_map/ppermute | solution.py:41
  11.3 6.0 %copy-start.1 = (f32[1,31]{1,0:T(1,128)S(1)}, f32[1,31]{1,0:T(1,128)}, u32[]{:S(2)}) copy-start(f32[1,31]{1,0:T(1,128)} %x_ref.1) | copy-start | bytes 376
  11.3 6.0 %copy-start.2 = (f32[1,31]{1,0:T(1,128)S(1)}, f32[1,31]{1,0:T(1,128)}, u32[]{:S(2)}) copy-start(f32[1,31]{1,0:T(1,128)} %y_ref.1) | copy-start | bytes 376
  11.3 6.0 %copy-start.3 = (f32[1,61]{1,0:T(1,128)S(1)}, f32[1,61]{1,0:T(1,128)}, u32[]{:S(2)}) copy-start(f32[1,61]{1,0:T(1,128)} %z_ref.1) | copy-start | bytes 736
  11.3 9.5 %copy-start = (f32[48,64,128]{2,1,0:T(8,128)S(1)}, f32[48,64,128]{2,1,0:T(8,128)}, u32[]{:S(2)}) copy-start(f32[48,64,128]{2,1,0:T(8,128)} %estimate_ref.3) | copy-start | bytes 4718596
  11.3 45.3 %all-to-all-start = ((f32[64,48,128]{2,1,0:T(8,128)}), f32[64,48,128]{2,1,0:T(8,128)}, u32[]{:S(2)}, u32[]{:S(2)}) async-start(f32[64,48,128]{2,1,0:T(8,128)} %bitcast.37), calls=%async_computation | async-start | bytes 3145728 | tf_op jit(solution)/shard_map/all_to_all | solution.py:410
  20.9 1.0 %copy-start.6 = (f32[16,64,128]{2,1,0:T(8,128)S(1)}, f32[16,64,128]{2,1,0:T(8,128)}, u32[]{:S(2)}) copy-start(f32[16,64,128]{2,1,0:T(8,128)} %copy-done.5) | copy-start | bytes 1572868
  22.9 33.7 %copy-start.4 = (s32[1,2]{1,0:T(1,128)S(1)}, s32[1,2]{1,0:T(1,128)}, u32[]{:S(2)}) copy-start(s32[1,2]{1,0:T(1,128)} %box_ref.1) | copy-start | bytes 28
  60.2 8.2 %collective-permute-start.3 = (f32[16,64,128]{2,1,0:T(8,128)S(1)}, f32[16,64,128]{2,1,0:T(8,128)S(1)}, u32[]{:S(2)}, u32[]{:S(2)}) collective-permute-start(f32[16,64,128]{2,1,0:T(8,128)S(1)} %get-tuple-element.42), channel_id=1, source_target_pairs={{0,1},{2,3},{4,5},{6,7},{8,9},{10,11},{12,13},{14,15},{16,17},{18,... | collective-permute-start | bytes 1572872 | tf_op jit(solution)/shard_map/ppermute | solution.py:41
  60.7 7.7 %collective-permute-start.6 = (f32[16,16,128]{2,1,0:T(8,128)S(1)}, f32[16,16,128]{2,1,0:T(8,128)S(1)}, u32[]{:S(2)}, u32[]{:S(2)}) collective-permute-start(f32[16,16,128]{2,1,0:T(8,128)S(1)} %get-tuple-element.49), channel_id=1, source_target_pairs={{1,2},{3,4},{5,6},{7,8},{9,10},{11,12},{13,14},{15,16},{17,18},{19... | collective-permute-start | bytes 393224 | tf_op jit(solution)/shard_map/ppermute | solution.py:41
  62.5 10.5 %collective-permute-start.2 = (f32[16,48,128]{2,1,0:T(8,128)S(1)}, f32[16,48,128]{2,1,0:T(8,128)S(1)}, u32[]{:S(2)}, u32[]{:S(2)}) collective-permute-start(f32[16,48,128]{2,1,0:T(8,128)S(1)} %get-tuple-element.39), channel_id=1, source_target_pairs={{1,2},{3,4},{5,6},{7,8},{9,10},{11,12},{13,14},{15,16},{17,18},{19... | collective-permute-start | bytes 1179656 | tf_op jit(solution)/shard_map/ppermute | solution.py:41
  68.9 7.5 %collective-permute-start.7 = (f32[8,48,128]{2,1,0:T(8,128)S(1)}, f32[8,48,128]{2,1,0:T(8,128)S(1)}, u32[]{:S(2)}, u32[]{:S(2)}) collective-permute-start(f32[8,48,128]{2,1,0:T(8,128)S(1)} %get-tuple-element.50), channel_id=1, source_target_pairs={{0,64},{64,128},{128,192},{192,0},{1,65},{65,129},{129,193},{193,1... | collective-permute-start | bytes 589832 | tf_op jit(solution)/shard_map/ppermute | solution.py:403
  69.2 7.8 %collective-permute-start.8 = (f32[8,48,128]{2,1,0:T(8,128)S(1)}, f32[8,48,128]{2,1,0:T(8,128)S(1)}, u32[]{:S(2)}, u32[]{:S(2)}) collective-permute-start(f32[8,48,128]{2,1,0:T(8,128)S(1)} %get-tuple-element.51), channel_id=1, source_target_pairs={{0,192},{64,0},{128,64},{192,128},{1,193},{65,1},{129,65},{193,129... | collective-permute-start | bytes 589832 | tf_op jit(solution)/shard_map/ppermute | solution.py:403
  74.3 6.7 %collective-permute-start.4 = (f32[8,48,128]{2,1,0:T(8,128)S(1)}, f32[8,48,128]{2,1,0:T(8,128)S(1)}, u32[]{:S(2)}, u32[]{:S(2)}) collective-permute-start(f32[8,48,128]{2,1,0:T(8,128)S(1)} %get-tuple-element.45), channel_id=1, source_target_pairs={{0,64},{64,128},{128,192},{192,0},{1,65},{65,129},{129,193},{193,1... | collective-permute-start | bytes 589832 | tf_op jit(solution)/shard_map/ppermute | solution.py:403
  74.6 7.8 %collective-permute-start.5 = (f32[8,48,128]{2,1,0:T(8,128)S(1)}, f32[8,48,128]{2,1,0:T(8,128)S(1)}, u32[]{:S(2)}, u32[]{:S(2)}) collective-permute-start(f32[8,48,128]{2,1,0:T(8,128)S(1)} %get-tuple-element.46), channel_id=1, source_target_pairs={{0,192},{64,0},{128,64},{192,128},{1,193},{65,1},{129,65},{193,129... | collective-permute-start | bytes 589832 | tf_op jit(solution)/shard_map/ppermute | solution.py:403
  77.0 6.6 %collective-permute-start.9 = (f32[8,48,128]{2,1,0:T(8,128)S(1)}, f32[8,48,128]{2,1,0:T(8,128)S(1)}, u32[]{:S(2)}, u32[]{:S(2)}) collective-permute-start(f32[8,48,128]{2,1,0:T(8,128)S(1)} %add.19), channel_id=1, source_target_pairs={{0,64},{64,128},{128,192},{192,0},{1,65},{65,129},{129,193},{193,1... | collective-permute-start | bytes 589832 | tf_op jit(solution)/shard_map/ppermute | solution.py:403
  78.0 7.0 %collective-permute-start.12 = (f32[8,48,128]{2,1,0:T(8,128)S(1)}, f32[8,48,128]{2,1,0:T(8,128)S(1)}, u32[]{:S(2)}, u32[]{:S(2)}) collective-permute-start(f32[8,48,128]{2,1,0:T(8,128)S(1)} %add.22), channel_id=1, source_target_pairs={{0,192},{64,0},{128,64},{192,128},{1,193},{65,1},{129,65},{193,129... | collective-permute-start | bytes 589832 | tf_op jit(solution)/shard_map/ppermute | solution.py:403
  83.6 7.6 %collective-permute-start.10 = (f32[8,48,128]{2,1,0:T(8,128)S(1)}, f32[8,48,128]{2,1,0:T(8,128)S(1)}, u32[]{:S(2)}, u32[]{:S(2)}) collective-permute-start(f32[8,48,128]{2,1,0:T(8,128)S(1)} %add_add_fusion.1), channel_id=1, source_target_pairs={{0,64},{64,128},{128,192},{192,0},{1,65},{65,129},{129,193},{193,1... | collective-permute-start | bytes 589832 | tf_op jit(solution)/shard_map/ppermute | solution.py:403
  85.1 9.0 %collective-permute-start.13 = (f32[8,48,128]{2,1,0:T(8,128)S(1)}, f32[8,48,128]{2,1,0:T(8,128)S(1)}, u32[]{:S(2)}, u32[]{:S(2)}) collective-permute-start(f32[8,48,128]{2,1,0:T(8,128)S(1)} %add_add_fusion), channel_id=1, source_target_pairs={{0,192},{64,0},{128,64},{192,128},{1,193},{65,1},{129,65},{193,129... | collective-permute-start | bytes 589832 | tf_op jit(solution)/shard_map/ppermute | solution.py:403
  85.8 10.4 %collective-permute-start.16 = (f32[8,48,128]{2,1,0:T(8,128)S(1)}, f32[8,48,128]{2,1,0:T(8,128)S(1)}, u32[]{:S(2)}, u32[]{:S(2)}) collective-permute-start(f32[8,48,128]{2,1,0:T(8,128)S(1)} %add_add_fusion.1), channel_id=1, source_target_pairs={{0,192},{64,0},{128,64},{192,128},{1,193},{65,1},{129,65},{193,129... | collective-permute-start | bytes 589832 | tf_op jit(solution)/shard_map/ppermute | solution.py:403
  86.6 9.7 %collective-permute-start.15 = (f32[8,48,128]{2,1,0:T(8,128)S(1)}, f32[8,48,128]{2,1,0:T(8,128)S(1)}, u32[]{:S(2)}, u32[]{:S(2)}) collective-permute-start(f32[8,48,128]{2,1,0:T(8,128)S(1)} %add_add_fusion), channel_id=1, source_target_pairs={{0,64},{64,128},{128,192},{192,0},{1,65},{65,129},{129,193},{193,1... | collective-permute-start | bytes 589832 | tf_op jit(solution)/shard_map/ppermute | solution.py:403
  91.2 6.8 %collective-permute-start.11 = (f32[8,48,128]{2,1,0:T(8,128)S(1)}, f32[8,48,128]{2,1,0:T(8,128)S(1)}, u32[]{:S(2)}, u32[]{:S(2)}) collective-permute-start(f32[8,48,128]{2,1,0:T(8,128)S(1)} %collective-permute-done.10), channel_id=1, source_target_pairs={{0,64},{64,128},{128,192},{192,0},{1,65},{65,129},{129,193},{193,1... | collective-permute-start | bytes 589832 | tf_op jit(solution)/shard_map/ppermute | solution.py:403
  94.0 6.9 %collective-permute-start.14 = (f32[8,48,128]{2,1,0:T(8,128)S(1)}, f32[8,48,128]{2,1,0:T(8,128)S(1)}, u32[]{:S(2)}, u32[]{:S(2)}) collective-permute-start(f32[8,48,128]{2,1,0:T(8,128)S(1)} %collective-permute-done.13), channel_id=1, source_target_pairs={{0,192},{64,0},{128,64},{192,128},{1,193},{65,1},{129,65},{193,129... | collective-permute-start | bytes 589832 | tf_op jit(solution)/shard_map/ppermute | solution.py:403
  (3 other events, 2.6 us)

commit v6 on v5

--- a/solution.py
+++ b/solution.py
@@ -41,46 +41,32 @@
     return lax.ppermute(block, "block", pairs + [(target, source) for source, target in pairs])
 
 
-PARTS = 4
+FETCHES = 2
 
 
 def depart_kernel(
-    block, shift_hbm, source, estimate, target, far, near, shift_ref, padded, rolled, held, in_sems, out_sems, edge_in, edge_out
+    block, shift_hbm, source, estimate, target, far, near, shift_ref, padded, rolled, held, shift_sem, in_sem, out_sems, edge_in, edge_out
 ):
     odd = lax.rem(block[0], 2)
-    size, half = NX // PARTS, HALO // 2
-    shift_copy = pltpu.make_async_copy(shift_hbm, shift_ref, in_sems.at[PARTS + 2])
-    fetches = [
-        pltpu.make_async_copy(source.at[pl.ds(NX - SMAX, SMAX)], padded.at[pl.ds(0, SMAX)], in_sems.at[PARTS]),
-        pltpu.make_async_copy(source.at[pl.ds(0, SMAX)], padded.at[pl.ds(SMAX + NX, SMAX)], in_sems.at[PARTS + 1]),
-    ]
-    fetches += [
-        pltpu.make_async_copy(
-            source.at[pl.ds(part * size, size)], padded.at[pl.ds(SMAX + part * size, size)], in_sems.at[part]
-        )
-        for part in range(PARTS)
-    ]
+    shift_copy = pltpu.make_async_copy(shift_hbm, shift_ref, shift_sem)
+    fetch = pltpu.make_async_copy(source, padded.at[pl.ds(SMAX, NX)], in_sem)
     takes, gives = [], []
-    for index, (first, out_ref) in enumerate(((odd, far), (1 - odd, near))):
-        for part in range(2):
-            slot = 2 * index + part
-            rows = estimate.at[pl.ds(first * (SLAB - HALO) + part * half, half)]
-            takes.append(pltpu.make_async_copy(rows, held.at[slot], edge_in.at[slot]))
-            gives.append(
-                pltpu.make_async_copy(held.at[slot], out_ref.at[pl.ds(part * half, half)], edge_out.at[slot])
-            )
-    for copy in [shift_copy] + fetches + takes:
+    for slot, (first, out_ref) in enumerate(((odd, far), (1 - odd, near))):
+        rows = estimate.at[pl.ds(first * (SLAB - HALO), HALO)]
+        takes.append(pltpu.make_async_copy(rows, held.at[slot], edge_in.at[slot]))
+        gives.append(pltpu.make_async_copy(held.at[slot], out_ref, edge_out.at[slot]))
+    for copy in [shift_copy, fetch] + takes:
         copy.start()
     shift_copy.wait()
-    for copy in fetches[:3]:
-        copy.wait()
+    fetch.wait()
+    padded[pl.ds(0, SMAX), :] = padded[pl.ds(NX, SMAX), :]
+    padded[pl.ds(SMAX + NX, SMAX), :] = padded[pl.ds(SMAX, SMAX), :]
     start = SMAX - shift_ref[0]
-    for part in range(PARTS):
-        if part + 1 < PARTS:
-            fetches[part + 3].wait()
-
-        def move(block, carry, part=part):
-            base = part * size + block * 128
+    size = NX // 2
+    for part in range(2):
+
+        def move(index, carry, part=part):
+            base = part * size + index * 128
             rolled[pl.ds(pl.multiple_of(base, 128), 128), :] = padded[pl.ds(start + base, 128), :]
             return carry
 
@@ -90,9 +76,8 @@
         )
         copy.start()
         gives.append(copy)
-    for take, give in zip(takes, gives):
-        take.wait()
-        give.start()
+        takes[part].wait()
+        gives[part].start()
     for give in gives:
         give.wait()
 
@@ -108,11 +93,12 @@
             pltpu.SMEM((1,), jnp.int32),
             pltpu.VMEM((NX + 2 * SMAX, NZ), F32),
             pltpu.VMEM((NX, NZ), F32),
-            pltpu.VMEM((4, HALO // 2, NY, NZ), F32),
-            pltpu.SemaphoreType.DMA((PARTS + 3,)),
-            pltpu.SemaphoreType.DMA((PARTS,)),
-            pltpu.SemaphoreType.DMA((4,)),
-            pltpu.SemaphoreType.DMA((4,)),
+            pltpu.VMEM((2, HALO, NY, NZ), F32),
+            pltpu.SemaphoreType.DMA,
+            pltpu.SemaphoreType.DMA,
+            pltpu.SemaphoreType.DMA((2,)),
+            pltpu.SemaphoreType.DMA((2,)),
+            pltpu.SemaphoreType.DMA((2,)),
         ],
         compiler_params=pltpu.CompilerParams(vmem_limit_bytes=60 * 1024 * 1024),
         cost_estimate=pl.CostEstimate(flops=1000, bytes_accessed=2**20, transcendentals=0),
@@ -246,39 +232,34 @@
     )(far, own, near, band_y, band_z, band_x)
 
 
-def quotient_kernel(block, shift_ref, box_ref, seen_ref, predicted_ref, yb_ref, zb_ref, *rest):
+def quotient_kernel(block, scalars, seen_ref, predicted_ref, yb_ref, zb_ref, *rest):
     out_refs, (across_ref, rest_ref), (fetched, blurred, sems) = rest[:3], rest[3:5], rest[5:]
     odd = lax.rem(block[0], 2)
-    size = NY // PARTS
-    firsts = [pl.multiple_of(first, HALO) for first in (odd * (SLAB - HALO), (1 - odd) * (SLAB - HALO))] + [HALO]
+    size = NY // FETCHES
     copies = [
         pltpu.make_async_copy(
-            seen_ref.at[pl.ds(part * size, size), pl.ds(first, HALO), :],
-            fetched.at[index, pl.ds(part * size, size)],
-            sems.at[index, part],
+            seen_ref.at[pl.ds(part * size, size)], fetched.at[pl.ds(part * size, size)], sems.at[part]
         )
-        for index, first in enumerate(firsts)
-        for part in range(PARTS)
+        for part in range(FETCHES)
     ]
     for copy in copies:
         copy.start()
-    for index, first in enumerate(firsts):
-        for copy in copies[index * PARTS : (index + 1) * PARTS]:
-            copy.wait()
-        row = block[0] * SLAB + first - shift_ref[0] + iota((HALO, NZ), 0)
-        row = jnp.where(row < 0, row + NX, row)
-        row = jnp.where(row >= NX, row - NX, row)
-        inside = (row >= box_ref[0, 0]) & (row < box_ref[0, 1])
-        for part in range(PARTS):
-            span = pl.ds(part * size, size)
-            ratio = fetched[index, span] / predicted_ref[span, pl.ds(first, HALO), :]
-            ratio = jnp.where(inside[None], ratio, 1.0).reshape(size * HALO, NZ)
-            blurred[index, pl.ds(part * size * HALO, size * HALO), :] = blur_z(ratio, zb_ref[...])
+    row = block[0] * SLAB - scalars[0] + iota((SLAB, NZ), 0)
+    row = jnp.where(row < 0, row + NX, row)
+    row = jnp.where(row >= NX, row - NX, row)
+    inside = (row >= scalars[1]) & (row < scalars[2])
+    for part in range(FETCHES):
+        copies[part].wait()
+        for y in range(part * size, (part + 1) * size, 16):
+            span = pl.ds(y, 16)
+            ratio = jnp.where(inside[None], fetched[span] / predicted_ref[span], 1.0)
+            blurred[pl.ds(y * SLAB, 16 * SLAB), :] = blur_z(ratio.reshape(16 * SLAB, NZ), zb_ref[...])
+    for index, first in enumerate((odd * (SLAB - HALO), (1 - odd) * (SLAB - HALO), HALO)):
         for x in range(0, HALO, 2):
             both = blur_rows(
                 yb_ref[...],
-                blurred[index, pl.ds(x, NY, stride=HALO), :],
-                blurred[index, pl.ds(x + 1, NY, stride=HALO), :],
+                blurred[pl.ds(first + x, NY, stride=SLAB), :],
+                blurred[pl.ds(first + x + 1, NY, stride=SLAB), :],
             )
             for side, plane in enumerate(both):
                 out_refs[index][x + side] = plane
@@ -288,22 +269,22 @@
                     rest_ref[x + side, 2 * QUARTER :] = plane[3 * QUARTER :]
 
 
-def quotient(block, shift, box, seen, predicted, band_y, band_z):
+def quotient(block, scalars, seen, predicted, band_y, band_z):
     sizes = (NY, NY, NY, QUARTER, 3 * QUARTER)
     return pl.pallas_call(
         quotient_kernel,
         out_shape=[jax.ShapeDtypeStruct((HALO, size, NZ), F32) for size in sizes],
-        in_specs=[SMEM_SPEC] * 3 + [ANY_SPEC] + [VMEM_SPEC] * 3,
+        in_specs=[SMEM_SPEC] * 2 + [ANY_SPEC] + [VMEM_SPEC] * 3,
         out_specs=[VMEM_SPEC] * len(sizes),
         scratch_shapes=[
-            pltpu.VMEM((3, NY, HALO, NZ), F32),
-            pltpu.VMEM((3, NY * HALO, NZ), F32),
-            pltpu.SemaphoreType.DMA((3, PARTS)),
+            pltpu.VMEM((NY, SLAB, NZ), F32),
+            pltpu.VMEM((NY * SLAB, NZ), F32),
+            pltpu.SemaphoreType.DMA((FETCHES,)),
         ],
         compiler_params=PARAMS,
         cost_estimate=SHORT,
         name="quotient",
-    )(block, shift, box, seen, predicted, band_y, band_z)
+    )(block, scalars, seen, predicted, band_y, band_z)
 
 
 def backward_kernel(parts, size, piece_ref, *rest):
@@ -406,12 +387,13 @@
 def body(estimate, recorded, psf_x, psf_y, psf_z, view_shifts, view_boxes):
     group, block = lax.axis_index("group").reshape(1), lax.axis_index("block").reshape(1)
     rolled, far, near = depart(block, view_shifts, recorded, estimate)
+    scalars = jnp.concatenate([view_shifts, view_boxes[0]])
     far, near = swap(far, True), swap(near, False)
     seen = lax.all_to_all(rolled.reshape(NY, SLAB, NZ), "block", 0, 0)
-    yf, yb, zf, zb, xf, xb = make_bands(group, block, view_shifts, psf_x, psf_y, psf_z)
+    yf, yb, zf, zb, xf, xb = make_bands(group, block, scalars, psf_x, psf_y, psf_z)
     predicted = forward(far, estimate, near, yf, zf, xf)
 
-    far, near, middle, across, rest = quotient(block, view_shifts, view_boxes, seen, predicted, yb, zb)
+    far, near, middle, across, rest = quotient(block, scalars, seen, predicted, yb, zb)
     across, from_near, rest = swap(across, True), swap(near, False), swap(rest, True)
     wholes = (far, middle, near, from_near)
 

time: 102 us -> 102 us (level)
    unnamed x18 -> x22, local copies, waits for them, and re-layouts: 3.7 us -> 3.69 us
where the time goes in v6:
time: 102 us
  waiting for transfers between devices  43.4 us (43%)
  starting transfers between devices  33.7 us (33%)
  Pallas kernels  19.9 us (20%)
  local copies, waits for them, and re-layouts  3.69 us (4%)
    all_to_all x1, waiting for transfers between devices, body(): seen = lax.all_to_all(rolled.reshape(NY, SLAB, NZ), 'block', 0, 0)  26.6 us
    ppermute x12, starting transfers between devices, turn(): lax.ppermute(block, axis, [(i, (i + step) % size) for i in range(size)])  14.6 us
    ppermute x5, starting transfers between devices, swap(): lax.ppermute(block, 'block', pairs + [(target, source) for source, target...  13.1 us
    ppermute x12, waiting for transfers between devices, turn(): lax.ppermute(block, axis, [(i, (i + step) % size) for i in range(size)])  12.2 us
    pallas_call x1, Pallas kernels, forward(): pl.pallas_call(forward_kernel, out_shape=jax.ShapeDtypeStruct((NY, SLAB,...  7.04 us
    all_to_all x1, starting transfers between devices, body(): seen = lax.all_to_all(rolled.reshape(NY, SLAB, NZ), 'block', 0, 0)  5.94 us
    ppermute x5, waiting for transfers between devices, swap(): lax.ppermute(block, 'block', pairs + [(target, source) for source, target...  4.65 us
    unnamed x22, local copies, waits for them, and re-layouts  3.69 us
  transfers between devices with their start and end apart: 18, of which 10 were waited for; matrix products, arithmetic and copies ran while one was open for 0% of the time, Pallas kernels for 12%

profile of v6, /device:TPU:24, one launch (start us, length us, event | category | flops | bytes accessed | tf_op | source)
XLA Modules:
  0.0 101.8 jit_solution(465278651548634588)
XLA Ops:
  0.7 3.2 %depart.1 = (f32[3072,128]{1,0:T(8,128)}, f32[16,64,128]{2,1,0:T(8,128)}, f32[16,64,128]{2,1,0:T(8,128)}) custom-call(s32[1]{0:T(128)} %bitcast.1.block, s32[1]{0:T(128)S(6)} %copy.10.shift_hbm, f32[3072,128]{1,0:T(8,128)} %bitcast.37, f32[48,64,128]{2,1,0:T(8,128)} %estimate_ref.3), custom_call_target="tpu_custom_call" | custom-call | flops 1000 | bytes 1048576 | tf_op jit(solution)/shard_map/depart/pallas_call | solution.py:87
  3.9 7.6 %collective-permute-start = (f32[16,64,128]{2,1,0:T(8,128)}, f32[16,64,128]{2,1,0:T(8,128)S(1)}, u32[]{:S(2)}, u32[]{:S(2)}) collective-permute-start(f32[16,64,128]{2,1,0:T(8,128)} %get-tuple-element.32), channel_id=1, source_target_pairs={{1,2},{3,4},{5,6},{7,8},{9,10},{11,12},{13,14},{15,16},{17,18},{19... | collective-permute-start | bytes 1572872 | tf_op jit(solution)/shard_map/ppermute | solution.py:41
  11.5 5.9 %all-to-all-start = ((f32[64,48,128]{2,1,0:T(8,128)}), f32[64,48,128]{2,1,0:T(8,128)}, u32[]{:S(2)}, u32[]{:S(2)}) async-start(f32[64,48,128]{2,1,0:T(8,128)} %bitcast.38), calls=%async_computation | async-start | bytes 3145728 | tf_op jit(solution)/shard_map/all_to_all | solution.py:392
  17.5 1.9 %make_bands.1 = (bf16[64,192]{1,0:T(8,128)(2,1)S(1)}, bf16[64,192]{1,0:T(8,128)(2,1)S(1)}, bf16[256,256]{1,0:T(8,128)(2,1)S(1)}, bf16[256,256]{1,0:T(8,128)(2,1)...) custom-call(s32[1]{0:T(128)} %bitcast.group, s32[1]{0:T(128)} %bitcast.1.block, ...), custom_call_target="tpu_custom_call" | custom-call | tf_op jit(solution)/shard_map/make_bands/pallas_call | solution.py:169
  23.2 7.0 %forward.1.predicted_ref = f32[64,48,128]{2,1,0:T(8,128)S(1)} custom-call(f32[16,64,128]{2,1,0:T(8,128)S(1)} %copy-done.7, f32[48,64,128]{2,1,0:T(8,128)S(1)} %copy-done, f32[16,64,128]{2,1,0:T(8,128)S(1)} %copy-done.9, bf16[64,192]{1,0:T(8,128)(2,1)S(1)} %get-tuple-element.34.yf_ref, bf16[256,256]{1,0:T(8,128)(2,1)S(1)} %get-tuple-element.35.zf_ref, ...), custom_call_target="tpu_custom_call" | custom-call | flops 199999995904 | bytes 6291456 | tf_op jit(solution)/shard_map/forward/pallas_call | solution.py:223
  30.2 26.6 %all-to-all-done.seen_ref = f32[64,48,128]{2,1,0:T(8,128)} async-done(((f32[64,48,128]{2,1,0:T(8,128)}), f32[64,48,128]{2,1,0:T(8,128)}, u32[]{:S(2)}, u32[]{:S(2)}) %all-to-all-start) | async-done | bytes 1572896 | tf_op jit(solution)/shard_map/all_to_all | solution.py:392
  56.8 3.2 %quotient.1 = (f32[16,64,128]{2,1,0:T(8,128)S(1)}, f32[16,64,128]{2,1,0:T(8,128)S(1)}, f32[16,64,128]{2,1,0:T(8,128)S(1)}, f32[16,16,128]{2,1,0:T(8,128)S(1)}, f32[16,48,128]{2,1,0:T(8,128)S(1)}) custom-call(s32[1]{0:T(128)} %bitcast.1.block, s32[3]{0:T(128)S(1)} %copy-done.2, f32[64,48,128]{2,1,0:T(8,128)} %all-to-all-done.seen_ref, ...), custom_call_target="tpu_custom_call" | custom-call | flops 1000 | bytes 1000 | tf_op jit(solution)/shard_map/quotient/pallas_call | solution.py:274
  60.5 1.8 %collective-permute-start.6 = (f32[16,16,128]{2,1,0:T(8,128)S(1)}, f32[16,16,128]{2,1,0:T(8,128)S(1)}, u32[]{:S(2)}, u32[]{:S(2)}) collective-permute-start(f32[16,16,128]{2,1,0:T(8,128)S(1)} %get-tuple-element.49), channel_id=1, source_target_pairs={{1,2},{3,4},{5,6},{7,8},{9,10},{11,12},{13,14},{15,16},{17,18},{19... | collective-permute-start | bytes 393224 | tf_op jit(solution)/shard_map/ppermute | solution.py:41
  62.3 3.3 %collective-permute-start.2 = (f32[16,48,128]{2,1,0:T(8,128)S(1)}, f32[16,48,128]{2,1,0:T(8,128)S(1)}, u32[]{:S(2)}, u32[]{:S(2)}) collective-permute-start(f32[16,48,128]{2,1,0:T(8,128)S(1)} %get-tuple-element.39), channel_id=1, source_target_pairs={{1,2},{3,4},{5,6},{7,8},{9,10},{11,12},{13,14},{15,16},{17,18},{19... | collective-permute-start | bytes 1179656 | tf_op jit(solution)/shard_map/ppermute | solution.py:41
  65.5 2.6 %collective-permute-done.6 = f32[16,16,128]{2,1,0:T(8,128)S(1)} collective-permute-done((f32[16,16,128]{2,1,0:T(8,128)S(1)}, f32[16,16,128]{2,1,0:T(8,128)S(1)}, u32[]{:S(2)}, u32[]{:S(2)}) %collective-permute-start.6) | collective-permute-done | bytes 131104 | tf_op jit(solution)/shard_map/ppermute | solution.py:41
  69.0 1.8 %collective-permute-start.8 = (f32[8,48,128]{2,1,0:T(8,128)S(1)}, f32[8,48,128]{2,1,0:T(8,128)S(1)}, u32[]{:S(2)}, u32[]{:S(2)}) collective-permute-start(f32[8,48,128]{2,1,0:T(8,128)S(1)} %get-tuple-element.51), channel_id=1, source_target_pairs={{0,192},{64,0},{128,64},{192,128},{1,193},{65,1},{129,65},{193,129... | collective-permute-start | bytes 589832 | tf_op jit(solution)/shard_map/ppermute | solution.py:384
  70.8 2.0 %collective-permute-done.2 = f32[16,48,128]{2,1,0:T(8,128)S(1)} collective-permute-done((f32[16,48,128]{2,1,0:T(8,128)S(1)}, f32[16,48,128]{2,1,0:T(8,128)S(1)}, u32[]{:S(2)}, u32[]{:S(2)}) %collective-permute-start.2) | collective-permute-done | bytes 393248 | tf_op jit(solution)/shard_map/ppermute | solution.py:41
  72.8 1.3 %backward.2 = (f32[8,48,128]{2,1,0:T(8,128)S(1)}, f32[8,48,128]{2,1,0:T(8,128)S(1)}, f32[8,48,128]{2,1,0:T(8,128)S(1)}, f32[8,48,128]{2,1,0:T(8,128)S(1)}, f32[8...) custom-call(f32[768,128]{1,0:T(8,128)S(1)} %bitcast.29, f32[1024,128]{1,0:T(8,128)S(1)} %bitcast.22, ...), custom_call_target="tpu_custom_call" | custom-call | flops 1000 | bytes 1000 | tf_op jit(solution)/shard_map/backward/pallas_call | solution.py:309
  74.4 1.8 %collective-permute-start.5 = (f32[8,48,128]{2,1,0:T(8,128)S(1)}, f32[8,48,128]{2,1,0:T(8,128)S(1)}, u32[]{:S(2)}, u32[]{:S(2)}) collective-permute-start(f32[8,48,128]{2,1,0:T(8,128)S(1)} %get-tuple-element.46), channel_id=1, source_target_pairs={{0,192},{64,0},{128,64},{192,128},{1,193},{65,1},{129,65},{193,129... | collective-permute-start | bytes 589832 | tf_op jit(solution)/shard_map/ppermute | solution.py:384
  77.8 1.2 %collective-permute-start.12 = (f32[8,48,128]{2,1,0:T(8,128)S(1)}, f32[8,48,128]{2,1,0:T(8,128)S(1)}, u32[]{:S(2)}, u32[]{:S(2)}) collective-permute-start(f32[8,48,128]{2,1,0:T(8,128)S(1)} %add.22), channel_id=1, source_target_pairs={{0,192},{64,0},{128,64},{192,128},{1,193},{65,1},{129,65},{193,129... | collective-permute-start | bytes 589832 | tf_op jit(solution)/shard_map/ppermute | solution.py:384
  79.0 1.8 %collective-permute-done.4 = f32[8,48,128]{2,1,0:T(8,128)S(1)} collective-permute-done((f32[8,48,128]{2,1,0:T(8,128)S(1)}, f32[8,48,128]{2,1,0:T(8,128)S(1)}, u32[]{:S(2)}, u32[]{:S(2)}) %collective-permute-start.4) | collective-permute-done | bytes 196640 | tf_op jit(solution)/shard_map/ppermute | solution.py:384
  80.8 1.4 %collective-permute-done.5 = f32[8,48,128]{2,1,0:T(8,128)S(1)} collective-permute-done((f32[8,48,128]{2,1,0:T(8,128)S(1)}, f32[8,48,128]{2,1,0:T(8,128)S(1)}, u32[]{:S(2)}, u32[]{:S(2)}) %collective-permute-start.5) | collective-permute-done | bytes 196640 | tf_op jit(solution)/shard_map/ppermute | solution.py:384
  83.4 1.4 %collective-permute-start.10 = (f32[8,48,128]{2,1,0:T(8,128)S(1)}, f32[8,48,128]{2,1,0:T(8,128)S(1)}, u32[]{:S(2)}, u32[]{:S(2)}) collective-permute-start(f32[8,48,128]{2,1,0:T(8,128)S(1)} %add_add_fusion.1), channel_id=1, source_target_pairs={{0,64},{64,128},{128,192},{192,0},{1,65},{65,129},{129,193},{193,1... | collective-permute-start | bytes 589832 | tf_op jit(solution)/shard_map/ppermute | solution.py:384
  86.3 2.5 %collective-permute-start.15 = (f32[8,48,128]{2,1,0:T(8,128)S(1)}, f32[8,48,128]{2,1,0:T(8,128)S(1)}, u32[]{:S(2)}, u32[]{:S(2)}) collective-permute-start(f32[8,48,128]{2,1,0:T(8,128)S(1)} %add_add_fusion), channel_id=1, source_target_pairs={{0,64},{64,128},{128,192},{192,0},{1,65},{65,129},{129,193},{193,1... | collective-permute-start | bytes 589832 | tf_op jit(solution)/shard_map/ppermute | solution.py:384
  88.8 2.1 %collective-permute-done.10 = f32[8,48,128]{2,1,0:T(8,128)S(1)} collective-permute-done((f32[8,48,128]{2,1,0:T(8,128)S(1)}, f32[8,48,128]{2,1,0:T(8,128)S(1)}, u32[]{:S(2)}, u32[]{:S(2)}) %collective-permute-start.10) | collective-permute-done | bytes 196640 | tf_op jit(solution)/shard_map/ppermute | solution.py:384
  91.0 2.8 %collective-permute-start.11 = (f32[8,48,128]{2,1,0:T(8,128)S(1)}, f32[8,48,128]{2,1,0:T(8,128)S(1)}, u32[]{:S(2)}, u32[]{:S(2)}) collective-permute-start(f32[8,48,128]{2,1,0:T(8,128)S(1)} %collective-permute-done.10), channel_id=1, source_target_pairs={{0,64},{64,128},{128,192},{192,0},{1,65},{65,129},{129,193},{193,1... | collective-permute-start | bytes 589832 | tf_op jit(solution)/shard_map/ppermute | solution.py:384
  93.8 2.2 %collective-permute-done.16 = f32[8,48,128]{2,1,0:T(8,128)S(1)} collective-permute-done((f32[8,48,128]{2,1,0:T(8,128)S(1)}, f32[8,48,128]{2,1,0:T(8,128)S(1)}, u32[]{:S(2)}, u32[]{:S(2)}) %collective-permute-start.16) | collective-permute-done | bytes 196640 | tf_op jit(solution)/shard_map/ppermute | solution.py:384
  96.0 1.8 %finish.1.rest_2_ = f32[48,64,128]{2,1,0:T(8,128)} custom-call(s32[1]{0:T(128)} %bitcast.group, f32[48,64,128]{2,1,0:T(8,128)S(1)} %copy-done, f32[384,128]{1,0:T(8,128)S(1)} %bitcast.19, f32[384,128]{1,0:T(8,128)S(1)} %bitcast.20, f32[384,128]{1,0:T(8,128)S(1)} %bitcast.30, f32[384,128]{1,0:T(8,128)S(1)} %bitcast.33, f32[384,128]{1,0:T(8,128)S(1)} %bitcast.32, ...), custom_call_target="tpu_custom_call" | custom-call | flops 1000 | bytes 1000 | tf_op jit(solution)/shard_map/finish/pallas_call | solution.py:360
  97.8 2.9 %collective-permute-done.14 = f32[8,48,128]{2,1,0:T(8,128)S(1)} collective-permute-done((f32[8,48,128]{2,1,0:T(8,128)S(1)}, f32[8,48,128]{2,1,0:T(8,128)S(1)}, u32[]{:S(2)}, u32[]{:S(2)}) %collective-permute-start.14) | collective-permute-done | bytes 196640 | tf_op jit(solution)/shard_map/ppermute | solution.py:384
  (47 shorter events, 10.6 us)
Async XLA Ops:
  3.9 15.6 %collective-permute-start = (f32[16,64,128]{2,1,0:T(8,128)}, f32[16,64,128]{2,1,0:T(8,128)S(1)}, u32[]{:S(2)}, u32[]{:S(2)}) collective-permute-start(f32[16,64,128]{2,1,0:T(8,128)} %get-tuple-element.32), channel_id=1, source_target_pairs={{1,2},{3,4},{5,6},{7,8},{9,10},{11,12},{13,14},{15,16},{17,18},{19... | collective-permute-start | bytes 1572872 | tf_op jit(solution)/shard_map/ppermute | solution.py:41
  11.4 8.8 %collective-permute-start.1 = (f32[16,64,128]{2,1,0:T(8,128)}, f32[16,64,128]{2,1,0:T(8,128)S(1)}, u32[]{:S(2)}, u32[]{:S(2)}) collective-permute-start(f32[16,64,128]{2,1,0:T(8,128)} %get-tuple-element.33), channel_id=1, source_target_pairs={{0,1},{2,3},{4,5},{6,7},{8,9},{10,11},{12,13},{14,15},{16,17},{18,... | collective-permute-start | bytes 1572872 | tf_op jit(solution)/shard_map/ppermute | solution.py:41
  11.4 6.0 %copy-start.10 = (s32[1,2]{1,0:T(1,128)S(1)}, s32[1,2]{1,0:T(1,128)}, u32[]{:S(2)}) copy-start(s32[1,2]{1,0:T(1,128)} %param.13) | copy-start | bytes 28
  11.4 6.1 %copy-start.3 = (f32[1,31]{1,0:T(1,128)S(1)}, f32[1,31]{1,0:T(1,128)}, u32[]{:S(2)}) copy-start(f32[1,31]{1,0:T(1,128)} %x_ref.1) | copy-start | bytes 376
  11.4 6.1 %copy-start.4 = (f32[1,31]{1,0:T(1,128)S(1)}, f32[1,31]{1,0:T(1,128)}, u32[]{:S(2)}) copy-start(f32[1,31]{1,0:T(1,128)} %y_ref.1) | copy-start | bytes 376
  11.5 6.1 %copy-start.5 = (f32[1,61]{1,0:T(1,128)S(1)}, f32[1,61]{1,0:T(1,128)}, u32[]{:S(2)}) copy-start(f32[1,61]{1,0:T(1,128)} %z_ref.1) | copy-start | bytes 736
  11.5 9.6 %copy-start = (f32[48,64,128]{2,1,0:T(8,128)S(1)}, f32[48,64,128]{2,1,0:T(8,128)}, u32[]{:S(2)}) copy-start(f32[48,64,128]{2,1,0:T(8,128)} %estimate_ref.3) | copy-start | bytes 4718596
  11.5 45.3 %all-to-all-start = ((f32[64,48,128]{2,1,0:T(8,128)}), f32[64,48,128]{2,1,0:T(8,128)}, u32[]{:S(2)}, u32[]{:S(2)}) async-start(f32[64,48,128]{2,1,0:T(8,128)} %bitcast.38), calls=%async_computation | async-start | bytes 3145728 | tf_op jit(solution)/shard_map/all_to_all | solution.py:392
  23.2 33.6 %copy-start.2 = (s32[3]{0:T(128)S(1)}, s32[3]{0:T(128)}, u32[]{:S(2)}) copy-start(s32[3]{0:T(128)} %copy-done.1) | copy-start | bytes 40
  60.0 8.2 %collective-permute-start.3 = (f32[16,64,128]{2,1,0:T(8,128)S(1)}, f32[16,64,128]{2,1,0:T(8,128)S(1)}, u32[]{:S(2)}, u32[]{:S(2)}) collective-permute-start(f32[16,64,128]{2,1,0:T(8,128)S(1)} %get-tuple-element.42), channel_id=1, source_target_pairs={{0,1},{2,3},{4,5},{6,7},{8,9},{10,11},{12,13},{14,15},{16,17},{18,... | collective-permute-start | bytes 1572872 | tf_op jit(solution)/shard_map/ppermute | solution.py:41
  60.5 7.7 %collective-permute-start.6 = (f32[16,16,128]{2,1,0:T(8,128)S(1)}, f32[16,16,128]{2,1,0:T(8,128)S(1)}, u32[]{:S(2)}, u32[]{:S(2)}) collective-permute-start(f32[16,16,128]{2,1,0:T(8,128)S(1)} %get-tuple-element.49), channel_id=1, source_target_pairs={{1,2},{3,4},{5,6},{7,8},{9,10},{11,12},{13,14},{15,16},{17,18},{19... | collective-permute-start | bytes 393224 | tf_op jit(solution)/shard_map/ppermute | solution.py:41
  62.3 10.5 %collective-permute-start.2 = (f32[16,48,128]{2,1,0:T(8,128)S(1)}, f32[16,48,128]{2,1,0:T(8,128)S(1)}, u32[]{:S(2)}, u32[]{:S(2)}) collective-permute-start(f32[16,48,128]{2,1,0:T(8,128)S(1)} %get-tuple-element.39), channel_id=1, source_target_pairs={{1,2},{3,4},{5,6},{7,8},{9,10},{11,12},{13,14},{15,16},{17,18},{19... | collective-permute-start | bytes 1179656 | tf_op jit(solution)/shard_map/ppermute | solution.py:41
  68.7 7.5 %collective-permute-start.7 = (f32[8,48,128]{2,1,0:T(8,128)S(1)}, f32[8,48,128]{2,1,0:T(8,128)S(1)}, u32[]{:S(2)}, u32[]{:S(2)}) collective-permute-start(f32[8,48,128]{2,1,0:T(8,128)S(1)} %get-tuple-element.50), channel_id=1, source_target_pairs={{0,64},{64,128},{128,192},{192,0},{1,65},{65,129},{129,193},{193,1... | collective-permute-start | bytes 589832 | tf_op jit(solution)/shard_map/ppermute | solution.py:384
  69.0 7.8 %collective-permute-start.8 = (f32[8,48,128]{2,1,0:T(8,128)S(1)}, f32[8,48,128]{2,1,0:T(8,128)S(1)}, u32[]{:S(2)}, u32[]{:S(2)}) collective-permute-start(f32[8,48,128]{2,1,0:T(8,128)S(1)} %get-tuple-element.51), channel_id=1, source_target_pairs={{0,192},{64,0},{128,64},{192,128},{1,193},{65,1},{129,65},{193,129... | collective-permute-start | bytes 589832 | tf_op jit(solution)/shard_map/ppermute | solution.py:384
  74.1 6.7 %collective-permute-start.4 = (f32[8,48,128]{2,1,0:T(8,128)S(1)}, f32[8,48,128]{2,1,0:T(8,128)S(1)}, u32[]{:S(2)}, u32[]{:S(2)}) collective-permute-start(f32[8,48,128]{2,1,0:T(8,128)S(1)} %get-tuple-element.45), channel_id=1, source_target_pairs={{0,64},{64,128},{128,192},{192,0},{1,65},{65,129},{129,193},{193,1... | collective-permute-start | bytes 589832 | tf_op jit(solution)/shard_map/ppermute | solution.py:384
  74.4 7.8 %collective-permute-start.5 = (f32[8,48,128]{2,1,0:T(8,128)S(1)}, f32[8,48,128]{2,1,0:T(8,128)S(1)}, u32[]{:S(2)}, u32[]{:S(2)}) collective-permute-start(f32[8,48,128]{2,1,0:T(8,128)S(1)} %get-tuple-element.46), channel_id=1, source_target_pairs={{0,192},{64,0},{128,64},{192,128},{1,193},{65,1},{129,65},{193,129... | collective-permute-start | bytes 589832 | tf_op jit(solution)/shard_map/ppermute | solution.py:384
  76.8 6.6 %collective-permute-start.9 = (f32[8,48,128]{2,1,0:T(8,128)S(1)}, f32[8,48,128]{2,1,0:T(8,128)S(1)}, u32[]{:S(2)}, u32[]{:S(2)}) collective-permute-start(f32[8,48,128]{2,1,0:T(8,128)S(1)} %add.19), channel_id=1, source_target_pairs={{0,64},{64,128},{128,192},{192,0},{1,65},{65,129},{129,193},{193,1... | collective-permute-start | bytes 589832 | tf_op jit(solution)/shard_map/ppermute | solution.py:384
  77.8 7.0 %collective-permute-start.12 = (f32[8,48,128]{2,1,0:T(8,128)S(1)}, f32[8,48,128]{2,1,0:T(8,128)S(1)}, u32[]{:S(2)}, u32[]{:S(2)}) collective-permute-start(f32[8,48,128]{2,1,0:T(8,128)S(1)} %add.22), channel_id=1, source_target_pairs={{0,192},{64,0},{128,64},{192,128},{1,193},{65,1},{129,65},{193,129... | collective-permute-start | bytes 589832 | tf_op jit(solution)/shard_map/ppermute | solution.py:384
  83.4 7.6 %collective-permute-start.10 = (f32[8,48,128]{2,1,0:T(8,128)S(1)}, f32[8,48,128]{2,1,0:T(8,128)S(1)}, u32[]{:S(2)}, u32[]{:S(2)}) collective-permute-start(f32[8,48,128]{2,1,0:T(8,128)S(1)} %add_add_fusion.1), channel_id=1, source_target_pairs={{0,64},{64,128},{128,192},{192,0},{1,65},{65,129},{129,193},{193,1... | collective-permute-start | bytes 589832 | tf_op jit(solution)/shard_map/ppermute | solution.py:384
  84.8 9.0 %collective-permute-start.13 = (f32[8,48,128]{2,1,0:T(8,128)S(1)}, f32[8,48,128]{2,1,0:T(8,128)S(1)}, u32[]{:S(2)}, u32[]{:S(2)}) collective-permute-start(f32[8,48,128]{2,1,0:T(8,128)S(1)} %add_add_fusion), channel_id=1, source_target_pairs={{0,192},{64,0},{128,64},{192,128},{1,193},{65,1},{129,65},{193,129... | collective-permute-start | bytes 589832 | tf_op jit(solution)/shard_map/ppermute | solution.py:384
  85.6 10.4 %collective-permute-start.16 = (f32[8,48,128]{2,1,0:T(8,128)S(1)}, f32[8,48,128]{2,1,0:T(8,128)S(1)}, u32[]{:S(2)}, u32[]{:S(2)}) collective-permute-start(f32[8,48,128]{2,1,0:T(8,128)S(1)} %add_add_fusion.1), channel_id=1, source_target_pairs={{0,192},{64,0},{128,64},{192,128},{1,193},{65,1},{129,65},{193,129... | collective-permute-start | bytes 589832 | tf_op jit(solution)/shard_map/ppermute | solution.py:384
  86.3 9.7 %collective-permute-start.15 = (f32[8,48,128]{2,1,0:T(8,128)S(1)}, f32[8,48,128]{2,1,0:T(8,128)S(1)}, u32[]{:S(2)}, u32[]{:S(2)}) collective-permute-start(f32[8,48,128]{2,1,0:T(8,128)S(1)} %add_add_fusion), channel_id=1, source_target_pairs={{0,64},{64,128},{128,192},{192,0},{1,65},{65,129},{129,193},{193,1... | collective-permute-start | bytes 589832 | tf_op jit(solution)/shard_map/ppermute | solution.py:384
  91.0 6.8 %collective-permute-start.11 = (f32[8,48,128]{2,1,0:T(8,128)S(1)}, f32[8,48,128]{2,1,0:T(8,128)S(1)}, u32[]{:S(2)}, u32[]{:S(2)}) collective-permute-start(f32[8,48,128]{2,1,0:T(8,128)S(1)} %collective-permute-done.10), channel_id=1, source_target_pairs={{0,64},{64,128},{128,192},{192,0},{1,65},{65,129},{129,193},{193,1... | collective-permute-start | bytes 589832 | tf_op jit(solution)/shard_map/ppermute | solution.py:384
  93.8 6.9 %collective-permute-start.14 = (f32[8,48,128]{2,1,0:T(8,128)S(1)}, f32[8,48,128]{2,1,0:T(8,128)S(1)}, u32[]{:S(2)}, u32[]{:S(2)}) collective-permute-start(f32[8,48,128]{2,1,0:T(8,128)S(1)} %collective-permute-done.13), channel_id=1, source_target_pairs={{0,192},{64,0},{128,64},{192,128},{1,193},{65,1},{129,65},{193,129... | collective-permute-start | bytes 589832 | tf_op jit(solution)/shard_map/ppermute | solution.py:384
  (5 other events, 7.2 us)

commit v7 on v6

--- a/solution.py
+++ b/solution.py
@@ -45,39 +45,51 @@
 
 
 def depart_kernel(
-    block, shift_hbm, source, estimate, target, far, near, shift_ref, padded, rolled, held, shift_sem, in_sem, out_sems, edge_in, edge_out
+    block, shift_hbm, source, estimate, target, far, near, shift_ref, padded, rolled, held, shift_sem, in_sems, out_sems, edge_in, edge_out
 ):
     odd = lax.rem(block[0], 2)
+    half = NX // 2
+    first = half + 2 * SMAX
     shift_copy = pltpu.make_async_copy(shift_hbm, shift_ref, shift_sem)
-    fetch = pltpu.make_async_copy(source, padded.at[pl.ds(SMAX, NX)], in_sem)
+    fetches = [
+        pltpu.make_async_copy(source.at[pl.ds(0, first)], padded.at[pl.ds(SMAX, first)], in_sems.at[0]),
+        pltpu.make_async_copy(source.at[pl.ds(NX - SMAX, SMAX)], padded.at[pl.ds(0, SMAX)], in_sems.at[1]),
+        pltpu.make_async_copy(
+            source.at[pl.ds(first, NX - first)], padded.at[pl.ds(SMAX + first, NX - first)], in_sems.at[2]
+        ),
+    ]
     takes, gives = [], []
-    for slot, (first, out_ref) in enumerate(((odd, far), (1 - odd, near))):
-        rows = estimate.at[pl.ds(first * (SLAB - HALO), HALO)]
+    for slot, (edge, out_ref) in enumerate(((odd, far), (1 - odd, near))):
+        rows = estimate.at[pl.ds(edge * (SLAB - HALO), HALO)]
         takes.append(pltpu.make_async_copy(rows, held.at[slot], edge_in.at[slot]))
         gives.append(pltpu.make_async_copy(held.at[slot], out_ref, edge_out.at[slot]))
-    for copy in [shift_copy, fetch] + takes:
+    for copy in [shift_copy] + fetches[:2] + takes + fetches[2:]:
         copy.start()
     shift_copy.wait()
-    fetch.wait()
-    padded[pl.ds(0, SMAX), :] = padded[pl.ds(NX, SMAX), :]
-    padded[pl.ds(SMAX + NX, SMAX), :] = padded[pl.ds(SMAX, SMAX), :]
     start = SMAX - shift_ref[0]
-    size = NX // 2
     for part in range(2):
+        if part == 0:
+            fetches[0].wait()
+            fetches[1].wait()
+        else:
+            fetches[2].wait()
+            padded[pl.ds(SMAX + NX, SMAX), :] = padded[pl.ds(SMAX, SMAX), :]
 
         def move(index, carry, part=part):
-            base = part * size + index * 128
+            base = part * half + index * 128
             rolled[pl.ds(pl.multiple_of(base, 128), 128), :] = padded[pl.ds(start + base, 128), :]
             return carry
 
-        lax.fori_loop(0, size // 128, move, 0)
+        lax.fori_loop(0, half // 128, move, 0)
         copy = pltpu.make_async_copy(
-            rolled.at[pl.ds(part * size, size)], target.at[pl.ds(part * size, size)], out_sems.at[part]
+            rolled.at[pl.ds(part * half, half)], target.at[pl.ds(part * half, half)], out_sems.at[part]
         )
         copy.start()
         gives.append(copy)
-        takes[part].wait()
-        gives[part].start()
+        if part == 0:
+            for slot in range(2):
+                takes[slot].wait()
+                gives[slot].start()
     for give in gives:
         give.wait()
 
@@ -95,7 +107,7 @@
             pltpu.VMEM((NX, NZ), F32),
             pltpu.VMEM((2, HALO, NY, NZ), F32),
             pltpu.SemaphoreType.DMA,
-            pltpu.SemaphoreType.DMA,
+            pltpu.SemaphoreType.DMA((3,)),
             pltpu.SemaphoreType.DMA((2,)),
             pltpu.SemaphoreType.DMA((2,)),
             pltpu.SemaphoreType.DMA((2,)),
@@ -419,7 +431,8 @@
         estimate,
         (own_a, own_b, low_a, low_b, high_a, high_b),
     )
-    return finish(((2, 0), (2, 1)), group, estimate, (across_a, across_b), most)
+    most = finish(((2, 0),), group, estimate, (across_a,), most)
+    return finish(((2, 1),), group, estimate, (across_b,), most)
 
 
 def solution(mesh):

time: 102 us -> 101 us (level)
  starting transfers between devices: 33.7 us -> 32.6 us
    ppermute x12, starting transfers between devices: 14.6 us -> 13.5 us  [turn(): lax.ppermute(block, axis, [(i, (i + step) % size) for i in range(size)])]
  transfers between devices with their start and end apart: 18 -> 18, of which waited for: 10 -> 10; matrix products, arithmetic and copies ran while one was open for 0% -> 0% of each run, Pallas kernels for 12% -> 13%
where the time goes in v7:
time: 101 us
  waiting for transfers between devices  43.3 us (43%)
  starting transfers between devices  32.6 us (32%)
  Pallas kernels  20.1 us (20%)
  local copies, waits for them, and re-layouts  3.69 us (4%)
    all_to_all x1, waiting for transfers between devices, body(): seen = lax.all_to_all(rolled.reshape(NY, SLAB, NZ), 'block', 0, 0)  26.6 us
    ppermute x12, starting transfers between devices, turn(): lax.ppermute(block, axis, [(i, (i + step) % size) for i in range(size)])  13.5 us
    ppermute x5, starting transfers between devices, swap(): lax.ppermute(block, 'block', pairs + [(target, source) for source, target...  13.1 us
    ppermute x12, waiting for transfers between devices, turn(): lax.ppermute(block, axis, [(i, (i + step) % size) for i in range(size)])  12.1 us
    pallas_call x1, Pallas kernels, forward(): pl.pallas_call(forward_kernel, out_shape=jax.ShapeDtypeStruct((NY, SLAB,...  7.04 us
    all_to_all x1, starting transfers between devices, body(): seen = lax.all_to_all(rolled.reshape(NY, SLAB, NZ), 'block', 0, 0)  5.94 us
    ppermute x5, waiting for transfers between devices, swap(): lax.ppermute(block, 'block', pairs + [(target, source) for source, target...  4.64 us
    unnamed x22, local copies, waits for them, and re-layouts  3.69 us
  transfers between devices with their start and end apart: 18, of which 10 were waited for; matrix products, arithmetic and copies ran while one was open for 0% of the time, Pallas kernels for 13%

profile of v7, /device:TPU:24, one launch (start us, length us, event | category | flops | bytes accessed | tf_op | source)
XLA Modules:
  0.0 100.8 jit_solution(2748100112661320299)
XLA Ops:
  0.7 2.8 %depart.1 = (f32[3072,128]{1,0:T(8,128)}, f32[16,64,128]{2,1,0:T(8,128)}, f32[16,64,128]{2,1,0:T(8,128)}) custom-call(s32[1]{0:T(128)} %bitcast.1.block, s32[1]{0:T(128)S(6)} %copy.12.shift_hbm, f32[3072,128]{1,0:T(8,128)} %bitcast.37, f32[48,64,128]{2,1,0:T(8,128)} %estimate_ref.5), custom_call_target="tpu_custom_call" | custom-call | flops 1000 | bytes 1048576 | tf_op jit(solution)/shard_map/depart/pallas_call | solution.py:99
  3.4 7.6 %collective-permute-start = (f32[16,64,128]{2,1,0:T(8,128)}, f32[16,64,128]{2,1,0:T(8,128)S(1)}, u32[]{:S(2)}, u32[]{:S(2)}) collective-permute-start(f32[16,64,128]{2,1,0:T(8,128)} %get-tuple-element.32), channel_id=1, source_target_pairs={{1,2},{3,4},{5,6},{7,8},{9,10},{11,12},{13,14},{15,16},{17,18},{19... | collective-permute-start | bytes 1572872 | tf_op jit(solution)/shard_map/ppermute | solution.py:41
  11.1 5.9 %all-to-all-start = ((f32[64,48,128]{2,1,0:T(8,128)}), f32[64,48,128]{2,1,0:T(8,128)}, u32[]{:S(2)}, u32[]{:S(2)}) async-start(f32[64,48,128]{2,1,0:T(8,128)} %bitcast.38), calls=%async_computation | async-start | bytes 3145728 | tf_op jit(solution)/shard_map/all_to_all | solution.py:404
  17.1 1.9 %make_bands.1 = (bf16[64,192]{1,0:T(8,128)(2,1)S(1)}, bf16[64,192]{1,0:T(8,128)(2,1)S(1)}, bf16[256,256]{1,0:T(8,128)(2,1)S(1)}, bf16[256,256]{1,0:T(8,128)(2,1)...) custom-call(s32[1]{0:T(128)} %bitcast.group, s32[1]{0:T(128)} %bitcast.1.block, ...), custom_call_target="tpu_custom_call" | custom-call | tf_op jit(solution)/shard_map/make_bands/pallas_call | solution.py:181
  22.7 7.0 %forward.1.predicted_ref = f32[64,48,128]{2,1,0:T(8,128)S(1)} custom-call(f32[16,64,128]{2,1,0:T(8,128)S(1)} %copy-done.7, f32[48,64,128]{2,1,0:T(8,128)S(1)} %copy-done, f32[16,64,128]{2,1,0:T(8,128)S(1)} %copy-done.9, bf16[64,192]{1,0:T(8,128)(2,1)S(1)} %get-tuple-element.34.yf_ref, bf16[256,256]{1,0:T(8,128)(2,1)S(1)} %get-tuple-element.35.zf_ref, ...), custom_call_target="tpu_custom_call" | custom-call | flops 199999995904 | bytes 6291456 | tf_op jit(solution)/shard_map/forward/pallas_call | solution.py:235
  29.8 26.6 %all-to-all-done.seen_ref = f32[64,48,128]{2,1,0:T(8,128)} async-done(((f32[64,48,128]{2,1,0:T(8,128)}), f32[64,48,128]{2,1,0:T(8,128)}, u32[]{:S(2)}, u32[]{:S(2)}) %all-to-all-start) | async-done | bytes 1572896 | tf_op jit(solution)/shard_map/all_to_all | solution.py:404
  56.4 3.2 %quotient.1 = (f32[16,64,128]{2,1,0:T(8,128)S(1)}, f32[16,64,128]{2,1,0:T(8,128)S(1)}, f32[16,64,128]{2,1,0:T(8,128)S(1)}, f32[16,16,128]{2,1,0:T(8,128)S(1)}, f32[16,48,128]{2,1,0:T(8,128)S(1)}) custom-call(s32[1]{0:T(128)} %bitcast.1.block, s32[3]{0:T(128)S(1)} %copy-done.2, f32[64,48,128]{2,1,0:T(8,128)} %all-to-all-done.seen_ref, ...), custom_call_target="tpu_custom_call" | custom-call | flops 1000 | bytes 1000 | tf_op jit(solution)/shard_map/quotient/pallas_call | solution.py:286
  60.0 1.8 %collective-permute-start.6 = (f32[16,16,128]{2,1,0:T(8,128)S(1)}, f32[16,16,128]{2,1,0:T(8,128)S(1)}, u32[]{:S(2)}, u32[]{:S(2)}) collective-permute-start(f32[16,16,128]{2,1,0:T(8,128)S(1)} %get-tuple-element.49), channel_id=1, source_target_pairs={{1,2},{3,4},{5,6},{7,8},{9,10},{11,12},{13,14},{15,16},{17,18},{19... | collective-permute-start | bytes 393224 | tf_op jit(solution)/shard_map/ppermute | solution.py:41
  61.8 3.3 %collective-permute-start.2 = (f32[16,48,128]{2,1,0:T(8,128)S(1)}, f32[16,48,128]{2,1,0:T(8,128)S(1)}, u32[]{:S(2)}, u32[]{:S(2)}) collective-permute-start(f32[16,48,128]{2,1,0:T(8,128)S(1)} %get-tuple-element.39), channel_id=1, source_target_pairs={{1,2},{3,4},{5,6},{7,8},{9,10},{11,12},{13,14},{15,16},{17,18},{19... | collective-permute-start | bytes 1179656 | tf_op jit(solution)/shard_map/ppermute | solution.py:41
  65.1 2.6 %collective-permute-done.6 = f32[16,16,128]{2,1,0:T(8,128)S(1)} collective-permute-done((f32[16,16,128]{2,1,0:T(8,128)S(1)}, f32[16,16,128]{2,1,0:T(8,128)S(1)}, u32[]{:S(2)}, u32[]{:S(2)}) %collective-permute-start.6) | collective-permute-done | bytes 131104 | tf_op jit(solution)/shard_map/ppermute | solution.py:41
  68.6 1.8 %collective-permute-start.8 = (f32[8,48,128]{2,1,0:T(8,128)S(1)}, f32[8,48,128]{2,1,0:T(8,128)S(1)}, u32[]{:S(2)}, u32[]{:S(2)}) collective-permute-start(f32[8,48,128]{2,1,0:T(8,128)S(1)} %get-tuple-element.51), channel_id=1, source_target_pairs={{0,192},{64,0},{128,64},{192,128},{1,193},{65,1},{129,65},{193,129... | collective-permute-start | bytes 589832 | tf_op jit(solution)/shard_map/ppermute | solution.py:396
  70.4 2.0 %collective-permute-done.2 = f32[16,48,128]{2,1,0:T(8,128)S(1)} collective-permute-done((f32[16,48,128]{2,1,0:T(8,128)S(1)}, f32[16,48,128]{2,1,0:T(8,128)S(1)}, u32[]{:S(2)}, u32[]{:S(2)}) %collective-permute-start.2) | collective-permute-done | bytes 393248 | tf_op jit(solution)/shard_map/ppermute | solution.py:41
  72.4 1.3 %backward.2 = (f32[8,48,128]{2,1,0:T(8,128)S(1)}, f32[8,48,128]{2,1,0:T(8,128)S(1)}, f32[8,48,128]{2,1,0:T(8,128)S(1)}, f32[8,48,128]{2,1,0:T(8,128)S(1)}, f32[8...) custom-call(f32[768,128]{1,0:T(8,128)S(1)} %bitcast.29, f32[1024,128]{1,0:T(8,128)S(1)} %bitcast.22, ...), custom_call_target="tpu_custom_call" | custom-call | flops 1000 | bytes 1000 | tf_op jit(solution)/shard_map/backward/pallas_call | solution.py:321
  74.0 1.8 %collective-permute-start.5 = (f32[8,48,128]{2,1,0:T(8,128)S(1)}, f32[8,48,128]{2,1,0:T(8,128)S(1)}, u32[]{:S(2)}, u32[]{:S(2)}) collective-permute-start(f32[8,48,128]{2,1,0:T(8,128)S(1)} %get-tuple-element.46), channel_id=1, source_target_pairs={{0,192},{64,0},{128,64},{192,128},{1,193},{65,1},{129,65},{193,129... | collective-permute-start | bytes 589832 | tf_op jit(solution)/shard_map/ppermute | solution.py:396
  77.4 1.2 %collective-permute-start.9 = (f32[8,48,128]{2,1,0:T(8,128)S(1)}, f32[8,48,128]{2,1,0:T(8,128)S(1)}, u32[]{:S(2)}, u32[]{:S(2)}) collective-permute-start(f32[8,48,128]{2,1,0:T(8,128)S(1)} %add.19), channel_id=1, source_target_pairs={{0,192},{64,0},{128,64},{192,128},{1,193},{65,1},{129,65},{193,129... | collective-permute-start | bytes 589832 | tf_op jit(solution)/shard_map/ppermute | solution.py:396
  78.6 1.8 %collective-permute-done.4 = f32[8,48,128]{2,1,0:T(8,128)S(1)} collective-permute-done((f32[8,48,128]{2,1,0:T(8,128)S(1)}, f32[8,48,128]{2,1,0:T(8,128)S(1)}, u32[]{:S(2)}, u32[]{:S(2)}) %collective-permute-start.4) | collective-permute-done | bytes 196640 | tf_op jit(solution)/shard_map/ppermute | solution.py:396
  80.3 1.4 %collective-permute-done.5 = f32[8,48,128]{2,1,0:T(8,128)S(1)} collective-permute-done((f32[8,48,128]{2,1,0:T(8,128)S(1)}, f32[8,48,128]{2,1,0:T(8,128)S(1)}, u32[]{:S(2)}, u32[]{:S(2)}) %collective-permute-start.5) | collective-permute-done | bytes 196640 | tf_op jit(solution)/shard_map/ppermute | solution.py:396
  83.0 1.4 %collective-permute-start.13 = (f32[8,48,128]{2,1,0:T(8,128)S(1)}, f32[8,48,128]{2,1,0:T(8,128)S(1)}, u32[]{:S(2)}, u32[]{:S(2)}) collective-permute-start(f32[8,48,128]{2,1,0:T(8,128)S(1)} %add_add_fusion), channel_id=1, source_target_pairs={{0,64},{64,128},{128,192},{192,0},{1,65},{65,129},{129,193},{193,1... | collective-permute-start | bytes 589832 | tf_op jit(solution)/shard_map/ppermute | solution.py:396
  85.2 2.5 %collective-permute-start.15 = (f32[8,48,128]{2,1,0:T(8,128)S(1)}, f32[8,48,128]{2,1,0:T(8,128)S(1)}, u32[]{:S(2)}, u32[]{:S(2)}) collective-permute-start(f32[8,48,128]{2,1,0:T(8,128)S(1)} %add_add_fusion.1), channel_id=1, source_target_pairs={{0,64},{64,128},{128,192},{192,0},{1,65},{65,129},{129,193},{193,1... | collective-permute-start | bytes 589832 | tf_op jit(solution)/shard_map/ppermute | solution.py:396
  87.7 2.8 %collective-permute-done.13 = f32[8,48,128]{2,1,0:T(8,128)S(1)} collective-permute-done((f32[8,48,128]{2,1,0:T(8,128)S(1)}, f32[8,48,128]{2,1,0:T(8,128)S(1)}, u32[]{:S(2)}, u32[]{:S(2)}) %collective-permute-start.13) | collective-permute-done | bytes 196640 | tf_op jit(solution)/shard_map/ppermute | solution.py:396
  90.6 2.4 %collective-permute-start.14 = (f32[8,48,128]{2,1,0:T(8,128)S(1)}, f32[8,48,128]{2,1,0:T(8,128)S(1)}, u32[]{:S(2)}, u32[]{:S(2)}) collective-permute-start(f32[8,48,128]{2,1,0:T(8,128)S(1)} %collective-permute-done.13), channel_id=1, source_target_pairs={{0,64},{64,128},{128,192},{192,0},{1,65},{65,129},{129,193},{193,1... | collective-permute-start | bytes 589832 | tf_op jit(solution)/shard_map/ppermute | solution.py:396
  93.0 2.7 %collective-permute-done.16 = f32[8,48,128]{2,1,0:T(8,128)S(1)} collective-permute-done((f32[8,48,128]{2,1,0:T(8,128)S(1)}, f32[8,48,128]{2,1,0:T(8,128)S(1)}, u32[]{:S(2)}, u32[]{:S(2)}) %collective-permute-start.16) | collective-permute-done | bytes 196640 | tf_op jit(solution)/shard_map/ppermute | solution.py:396
  95.7 1.8 %finish.1.rest_1_ = f32[48,64,128]{2,1,0:T(8,128)} custom-call(s32[1]{0:T(128)} %bitcast.group, f32[48,64,128]{2,1,0:T(8,128)S(1)} %copy-done, f32[384,128]{1,0:T(8,128)S(1)} %bitcast.19, f32[384,128]{1,0:T(8,128)S(1)} %bitcast.20, f32[384,128]{1,0:T(8,128)S(1)} %bitcast.30, f32[384,128]{1,0:T(8,128)S(1)} %bitcast.32, f32[384,128]{1,0:T(8,128)S(1)} %bitcast.33, ...), custom_call_target="tpu_custom_call" | custom-call | flops 1000 | bytes 1000 | tf_op jit(solution)/shard_map/finish/pallas_call | solution.py:372
  98.2 1.6 %collective-permute-done.11 = f32[8,48,128]{2,1,0:T(8,128)S(1)} collective-permute-done((f32[8,48,128]{2,1,0:T(8,128)S(1)}, f32[8,48,128]{2,1,0:T(8,128)S(1)}, u32[]{:S(2)}, u32[]{:S(2)}) %collective-permute-start.11) | collective-permute-done | bytes 196640 | tf_op jit(solution)/shard_map/ppermute | solution.py:396
  (48 shorter events, 10.5 us)
Async XLA Ops:
  3.4 15.6 %collective-permute-start = (f32[16,64,128]{2,1,0:T(8,128)}, f32[16,64,128]{2,1,0:T(8,128)S(1)}, u32[]{:S(2)}, u32[]{:S(2)}) collective-permute-start(f32[16,64,128]{2,1,0:T(8,128)} %get-tuple-element.32), channel_id=1, source_target_pairs={{1,2},{3,4},{5,6},{7,8},{9,10},{11,12},{13,14},{15,16},{17,18},{19... | collective-permute-start | bytes 1572872 | tf_op jit(solution)/shard_map/ppermute | solution.py:41
  11.0 8.8 %collective-permute-start.1 = (f32[16,64,128]{2,1,0:T(8,128)}, f32[16,64,128]{2,1,0:T(8,128)S(1)}, u32[]{:S(2)}, u32[]{:S(2)}) collective-permute-start(f32[16,64,128]{2,1,0:T(8,128)} %get-tuple-element.33), channel_id=1, source_target_pairs={{0,1},{2,3},{4,5},{6,7},{8,9},{10,11},{12,13},{14,15},{16,17},{18,... | collective-permute-start | bytes 1572872 | tf_op jit(solution)/shard_map/ppermute | solution.py:41
  11.0 6.0 %copy-start.10 = (s32[1,2]{1,0:T(1,128)S(1)}, s32[1,2]{1,0:T(1,128)}, u32[]{:S(2)}) copy-start(s32[1,2]{1,0:T(1,128)} %param.13) | copy-start | bytes 28
  11.0 6.1 %copy-start.3 = (f32[1,31]{1,0:T(1,128)S(1)}, f32[1,31]{1,0:T(1,128)}, u32[]{:S(2)}) copy-start(f32[1,31]{1,0:T(1,128)} %x_ref.1) | copy-start | bytes 376
  11.0 6.1 %copy-start.4 = (f32[1,31]{1,0:T(1,128)S(1)}, f32[1,31]{1,0:T(1,128)}, u32[]{:S(2)}) copy-start(f32[1,31]{1,0:T(1,128)} %y_ref.1) | copy-start | bytes 376
  11.0 6.1 %copy-start.5 = (f32[1,61]{1,0:T(1,128)S(1)}, f32[1,61]{1,0:T(1,128)}, u32[]{:S(2)}) copy-start(f32[1,61]{1,0:T(1,128)} %z_ref.1) | copy-start | bytes 736
  11.0 9.6 %copy-start = (f32[48,64,128]{2,1,0:T(8,128)S(1)}, f32[48,64,128]{2,1,0:T(8,128)}, u32[]{:S(2)}) copy-start(f32[48,64,128]{2,1,0:T(8,128)} %estimate_ref.5) | copy-start | bytes 4718596
  11.1 45.3 %all-to-all-start = ((f32[64,48,128]{2,1,0:T(8,128)}), f32[64,48,128]{2,1,0:T(8,128)}, u32[]{:S(2)}, u32[]{:S(2)}) async-start(f32[64,48,128]{2,1,0:T(8,128)} %bitcast.38), calls=%async_computation | async-start | bytes 3145728 | tf_op jit(solution)/shard_map/all_to_all | solution.py:404
  22.7 33.6 %copy-start.2 = (s32[3]{0:T(128)S(1)}, s32[3]{0:T(128)}, u32[]{:S(2)}) copy-start(s32[3]{0:T(128)} %copy-done.1) | copy-start | bytes 40
  59.6 8.2 %collective-permute-start.3 = (f32[16,64,128]{2,1,0:T(8,128)S(1)}, f32[16,64,128]{2,1,0:T(8,128)S(1)}, u32[]{:S(2)}, u32[]{:S(2)}) collective-permute-start(f32[16,64,128]{2,1,0:T(8,128)S(1)} %get-tuple-element.42), channel_id=1, source_target_pairs={{0,1},{2,3},{4,5},{6,7},{8,9},{10,11},{12,13},{14,15},{16,17},{18,... | collective-permute-start | bytes 1572872 | tf_op jit(solution)/shard_map/ppermute | solution.py:41
  60.0 7.7 %collective-permute-start.6 = (f32[16,16,128]{2,1,0:T(8,128)S(1)}, f32[16,16,128]{2,1,0:T(8,128)S(1)}, u32[]{:S(2)}, u32[]{:S(2)}) collective-permute-start(f32[16,16,128]{2,1,0:T(8,128)S(1)} %get-tuple-element.49), channel_id=1, source_target_pairs={{1,2},{3,4},{5,6},{7,8},{9,10},{11,12},{13,14},{15,16},{17,18},{19... | collective-permute-start | bytes 393224 | tf_op jit(solution)/shard_map/ppermute | solution.py:41
  61.8 10.5 %collective-permute-start.2 = (f32[16,48,128]{2,1,0:T(8,128)S(1)}, f32[16,48,128]{2,1,0:T(8,128)S(1)}, u32[]{:S(2)}, u32[]{:S(2)}) collective-permute-start(f32[16,48,128]{2,1,0:T(8,128)S(1)} %get-tuple-element.39), channel_id=1, source_target_pairs={{1,2},{3,4},{5,6},{7,8},{9,10},{11,12},{13,14},{15,16},{17,18},{19... | collective-permute-start | bytes 1179656 | tf_op jit(solution)/shard_map/ppermute | solution.py:41
  68.3 7.5 %collective-permute-start.7 = (f32[8,48,128]{2,1,0:T(8,128)S(1)}, f32[8,48,128]{2,1,0:T(8,128)S(1)}, u32[]{:S(2)}, u32[]{:S(2)}) collective-permute-start(f32[8,48,128]{2,1,0:T(8,128)S(1)} %get-tuple-element.50), channel_id=1, source_target_pairs={{0,64},{64,128},{128,192},{192,0},{1,65},{65,129},{129,193},{193,1... | collective-permute-start | bytes 589832 | tf_op jit(solution)/shard_map/ppermute | solution.py:396
  68.6 7.8 %collective-permute-start.8 = (f32[8,48,128]{2,1,0:T(8,128)S(1)}, f32[8,48,128]{2,1,0:T(8,128)S(1)}, u32[]{:S(2)}, u32[]{:S(2)}) collective-permute-start(f32[8,48,128]{2,1,0:T(8,128)S(1)} %get-tuple-element.51), channel_id=1, source_target_pairs={{0,192},{64,0},{128,64},{192,128},{1,193},{65,1},{129,65},{193,129... | collective-permute-start | bytes 589832 | tf_op jit(solution)/shard_map/ppermute | solution.py:396
  73.7 6.7 %collective-permute-start.4 = (f32[8,48,128]{2,1,0:T(8,128)S(1)}, f32[8,48,128]{2,1,0:T(8,128)S(1)}, u32[]{:S(2)}, u32[]{:S(2)}) collective-permute-start(f32[8,48,128]{2,1,0:T(8,128)S(1)} %get-tuple-element.45), channel_id=1, source_target_pairs={{0,64},{64,128},{128,192},{192,0},{1,65},{65,129},{129,193},{193,1... | collective-permute-start | bytes 589832 | tf_op jit(solution)/shard_map/ppermute | solution.py:396
  74.0 7.8 %collective-permute-start.5 = (f32[8,48,128]{2,1,0:T(8,128)S(1)}, f32[8,48,128]{2,1,0:T(8,128)S(1)}, u32[]{:S(2)}, u32[]{:S(2)}) collective-permute-start(f32[8,48,128]{2,1,0:T(8,128)S(1)} %get-tuple-element.46), channel_id=1, source_target_pairs={{0,192},{64,0},{128,64},{192,128},{1,193},{65,1},{129,65},{193,129... | collective-permute-start | bytes 589832 | tf_op jit(solution)/shard_map/ppermute | solution.py:396
  76.3 6.6 %collective-permute-start.12 = (f32[8,48,128]{2,1,0:T(8,128)S(1)}, f32[8,48,128]{2,1,0:T(8,128)S(1)}, u32[]{:S(2)}, u32[]{:S(2)}) collective-permute-start(f32[8,48,128]{2,1,0:T(8,128)S(1)} %add.22), channel_id=1, source_target_pairs={{0,64},{64,128},{128,192},{192,0},{1,65},{65,129},{129,193},{193,1... | collective-permute-start | bytes 589832 | tf_op jit(solution)/shard_map/ppermute | solution.py:396
  77.4 7.0 %collective-permute-start.9 = (f32[8,48,128]{2,1,0:T(8,128)S(1)}, f32[8,48,128]{2,1,0:T(8,128)S(1)}, u32[]{:S(2)}, u32[]{:S(2)}) collective-permute-start(f32[8,48,128]{2,1,0:T(8,128)S(1)} %add.19), channel_id=1, source_target_pairs={{0,192},{64,0},{128,64},{192,128},{1,193},{65,1},{129,65},{193,129... | collective-permute-start | bytes 589832 | tf_op jit(solution)/shard_map/ppermute | solution.py:396
  83.0 7.6 %collective-permute-start.13 = (f32[8,48,128]{2,1,0:T(8,128)S(1)}, f32[8,48,128]{2,1,0:T(8,128)S(1)}, u32[]{:S(2)}, u32[]{:S(2)}) collective-permute-start(f32[8,48,128]{2,1,0:T(8,128)S(1)} %add_add_fusion), channel_id=1, source_target_pairs={{0,64},{64,128},{128,192},{192,0},{1,65},{65,129},{129,193},{193,1... | collective-permute-start | bytes 589832 | tf_op jit(solution)/shard_map/ppermute | solution.py:396
  84.4 8.6 %collective-permute-start.10 = (f32[8,48,128]{2,1,0:T(8,128)S(1)}, f32[8,48,128]{2,1,0:T(8,128)S(1)}, u32[]{:S(2)}, u32[]{:S(2)}) collective-permute-start(f32[8,48,128]{2,1,0:T(8,128)S(1)} %add_add_fusion.1), channel_id=1, source_target_pairs={{0,192},{64,0},{128,64},{192,128},{1,193},{65,1},{129,65},{193,129... | collective-permute-start | bytes 589832 | tf_op jit(solution)/shard_map/ppermute | solution.py:396
  85.2 7.8 %collective-permute-start.15 = (f32[8,48,128]{2,1,0:T(8,128)S(1)}, f32[8,48,128]{2,1,0:T(8,128)S(1)}, u32[]{:S(2)}, u32[]{:S(2)}) collective-permute-start(f32[8,48,128]{2,1,0:T(8,128)S(1)} %add_add_fusion.1), channel_id=1, source_target_pairs={{0,64},{64,128},{128,192},{192,0},{1,65},{65,129},{129,193},{193,1... | collective-permute-start | bytes 589832 | tf_op jit(solution)/shard_map/ppermute | solution.py:396
  87.7 7.9 %collective-permute-start.16 = (f32[8,48,128]{2,1,0:T(8,128)S(1)}, f32[8,48,128]{2,1,0:T(8,128)S(1)}, u32[]{:S(2)}, u32[]{:S(2)}) collective-permute-start(f32[8,48,128]{2,1,0:T(8,128)S(1)} %add_add_fusion), channel_id=1, source_target_pairs={{0,192},{64,0},{128,64},{192,128},{1,193},{65,1},{129,65},{193,129... | collective-permute-start | bytes 589832 | tf_op jit(solution)/shard_map/ppermute | solution.py:396
  90.6 6.9 %collective-permute-start.14 = (f32[8,48,128]{2,1,0:T(8,128)S(1)}, f32[8,48,128]{2,1,0:T(8,128)S(1)}, u32[]{:S(2)}, u32[]{:S(2)}) collective-permute-start(f32[8,48,128]{2,1,0:T(8,128)S(1)} %collective-permute-done.13), channel_id=1, source_target_pairs={{0,64},{64,128},{128,192},{192,0},{1,65},{65,129},{129,193},{193,1... | collective-permute-start | bytes 589832 | tf_op jit(solution)/shard_map/ppermute | solution.py:396
  93.0 6.9 %collective-permute-start.11 = (f32[8,48,128]{2,1,0:T(8,128)S(1)}, f32[8,48,128]{2,1,0:T(8,128)S(1)}, u32[]{:S(2)}, u32[]{:S(2)}) collective-permute-start(f32[8,48,128]{2,1,0:T(8,128)S(1)} %collective-permute-done.10), channel_id=1, source_target_pairs={{0,192},{64,0},{128,64},{192,128},{1,193},{65,1},{129,65},{193,129... | collective-permute-start | bytes 589832 | tf_op jit(solution)/shard_map/ppermute | solution.py:396
  (5 other events, 7.2 us)

commit v8 on v7

--- a/solution.py
+++ b/solution.py
@@ -18,7 +18,7 @@
 VMEM_LIMIT = 48 * 1024 * 1024
 
 SHORT = pl.CostEstimate(flops=1000, bytes_accessed=1000, transcendentals=0)
-FAR_COST = pl.CostEstimate(flops=2 * 10**9, bytes_accessed=1000, transcendentals=0)
+FAR_COST = pl.CostEstimate(flops=5 * 10**9, bytes_accessed=1000, transcendentals=0)
 SMEM_SPEC = pl.BlockSpec(memory_space=pltpu.SMEM)
 VMEM_SPEC = pl.BlockSpec(memory_space=pltpu.VMEM)
 ANY_SPEC = pl.BlockSpec(memory_space=pl.ANY)
@@ -244,8 +244,27 @@
     )(far, own, near, band_y, band_z, band_x)
 
 
+def store(ref, x, plane, spans):
+    at = 0
+    for low, high in spans:
+        ref[x, at : at + high - low] = plane[low:high]
+        at += high - low
+
+
+WHOLE = ((0, NY),)
+FAR_FIRST, FAR_REST = ((32, 56),), ((0, 32), (56, 64))
+NEAR_FIRST, NEAR_REST = ((32, 48),), ((0, 32), (48, 64))
+
+
+def rows_of(spans):
+    return sum(high - low for low, high in spans)
+
+
+SENT = ((0, FAR_FIRST), (0, FAR_REST), (1, NEAR_FIRST), (1, NEAR_REST))
+
+
 def quotient_kernel(block, scalars, seen_ref, predicted_ref, yb_ref, zb_ref, *rest):
-    out_refs, (across_ref, rest_ref), (fetched, blurred, sems) = rest[:3], rest[3:5], rest[5:]
+    out_refs, piece_refs, (fetched, blurred, sems) = rest[:3], rest[3:-3], rest[-3:]
     odd = lax.rem(block[0], 2)
     size = NY // FETCHES
     copies = [
@@ -275,14 +294,13 @@
             )
             for side, plane in enumerate(both):
                 out_refs[index][x + side] = plane
-                if index == 0:
-                    across_ref[x + side] = plane[2 * QUARTER : 3 * QUARTER]
-                    rest_ref[x + side, : 2 * QUARTER] = plane[: 2 * QUARTER]
-                    rest_ref[x + side, 2 * QUARTER :] = plane[3 * QUARTER :]
+                for ref, (of, spans) in zip(piece_refs, SENT):
+                    if of == index:
+                        store(ref, x + side, plane, spans)
 
 
 def quotient(block, scalars, seen, predicted, band_y, band_z):
-    sizes = (NY, NY, NY, QUARTER, 3 * QUARTER)
+    sizes = [NY] * 3 + [rows_of(spans) for _, spans in SENT]
     return pl.pallas_call(
         quotient_kernel,
         out_shape=[jax.ShapeDtypeStruct((HALO, size, NZ), F32) for size in sizes],
@@ -299,34 +317,54 @@
     )(block, scalars, seen, predicted, band_y, band_z)
 
 
-def backward_kernel(parts, size, piece_ref, *rest):
-    whole_refs, band_ref, out_refs = rest[:4], rest[4], rest[5:]
-    for out_ref, (at, piece_at) in zip(out_refs, parts):
-        for y in range(0, 8, 2):
+def find(spans, row):
+    at = 0
+    for low, high in spans:
+        if low <= row < high:
+            return at + row - low
+        at += high - low
+    return None
+
+
+def backward_kernel(starts, spans, *refs):
+    count = len(spans)
+    received, own, band_ref, out_refs = refs[:count], refs[count : count + 3], refs[count + 3], refs[count + 4 :]
+
+    def rows(ref, size, at):
+        return ref[pl.ds(at, HALO, stride=size), :]
+
+    def arrived(side, row):
+        for ref, (of, piece) in zip(received, spans):
+            at = find(piece, row) if of == side else None
+            if at is not None:
+                return rows(ref, rows_of(piece), at)
+        raise ValueError(row)
+
+    for out_ref, start in zip(out_refs, starts):
+        for y in range(start, start + 8, 2):
             planes = [
                 jnp.concatenate(
-                    [piece_ref[pl.ds(piece_at + y + side, HALO, stride=size), :]]
-                    + [ref[pl.ds(at + y + side, HALO, stride=NY), :] for ref in whole_refs],
-                    axis=0,
+                    [arrived("far", row)] + [rows(ref, NY, row) for ref in own] + [arrived("near", row)], axis=0
                 )
-                for side in (0, 1)
+                for row in (y, y + 1)
             ]
             left, right = blur_rows(band_ref[...], *planes)
-            out_ref[y] = left
-            out_ref[y + 1] = right
-
-
-def backward(parts, cost, piece, wholes, band_x):
-    size = piece.shape[1]
-    return pl.pallas_call(
-        functools.partial(backward_kernel, parts, size),
-        out_shape=[jax.ShapeDtypeStruct((8, SLAB, NZ), F32)] * len(parts),
-        in_specs=[VMEM_SPEC] * 6,
-        out_specs=[VMEM_SPEC] * len(parts),
+            out_ref[y - start] = left
+            out_ref[y - start + 1] = right
+
+
+def backward(starts, cost, received, own, band_x):
+    spans = tuple((side, piece) for side, piece, _ in received)
+    flat = [value.reshape(-1, NZ) for _, _, value in received] + [value.reshape(-1, NZ) for value in own]
+    return pl.pallas_call(
+        functools.partial(backward_kernel, starts, spans),
+        out_shape=[jax.ShapeDtypeStruct((8, SLAB, NZ), F32)] * len(starts),
+        in_specs=[VMEM_SPEC] * (len(flat) + 1),
+        out_specs=[VMEM_SPEC] * len(starts),
         compiler_params=PARAMS,
         cost_estimate=cost,
         name="backward",
-    )(piece.reshape(HALO * size, NZ), *[whole.reshape(HALO * NY, NZ) for whole in wholes], band_x)
+    )(*flat, band_x)
 
 
 def finish_rows(group, estimate_ref, piece_ref, turns, half, out_ref, out_base):
@@ -405,15 +443,17 @@
     yf, yb, zf, zb, xf, xb = make_bands(group, block, scalars, psf_x, psf_y, psf_z)
     predicted = forward(far, estimate, near, yf, zf, xf)
 
-    far, near, middle, across, rest = quotient(block, scalars, seen, predicted, yb, zb)
-    across, from_near, rest = swap(across, True), swap(near, False), swap(rest, True)
-    wholes = (far, middle, near, from_near)
-
-    far_a, far_b = backward(((32, 0), (40, 8)), FAR_COST, across, wholes, xb)
+    far, near, middle, far_first, far_rest, near_first, near_rest = quotient(block, scalars, seen, predicted, yb, zb)
+    far_first = ("far", FAR_FIRST, swap(far_first, True))
+    far_rest = ("far", FAR_REST, swap(far_rest, True))
+    near_first = ("near", NEAR_FIRST, swap(near_first, False))
+    near_rest = ("near", NEAR_REST, swap(near_rest, False))
+    slab = (far, middle, near)
+
+    far_a, far_b = backward((32, 40), FAR_COST, (far_first, near_first), slab, xb)
     far_a, far_b = turn(far_a, "group", 1), turn(far_b, "group", -1)
-    far_a, far_b = lax.optimization_barrier((far_a, far_b))
     next_a, near_b, near_a, prev_b, own_a, own_b = backward(
-        ((16, 16), (24, 24), (48, 32), (56, 40), (0, 0), (8, 8)), SHORT, rest, wholes, xb
+        (16, 24, 48, 56, 0, 8), SHORT, (far_first, far_rest, near_rest), slab, xb
     )
     sum_a = turn(next_a + far_a, "group", 1)
     sum_b = turn(prev_b + far_b, "group", -1)

time: 101 us -> 102 us (level)
    ppermute x5 -> x6, waiting for transfers between devices: 4.64 us -> 4.29 us  [swap(): lax.ppermute(block, 'block', pairs + [(target, source) for source, target...]
    ppermute x5 -> x6, starting transfers between devices: 13.1 us -> 12.7 us  [swap(): lax.ppermute(block, 'block', pairs + [(target, source) for source, target...]
  transfers between devices with their start and end apart: 18 -> 19, of which waited for: 10 -> 12; matrix products, arithmetic and copies ran while one was open for 0% -> 0% of each run, Pallas kernels for 13% -> 13%
where the time goes in v8:
time: 102 us; the launch traced here: 101 us
  waiting for transfers between devices  43.8 us (43%)
  starting transfers between devices  32.7 us (32%)
  Pallas kernels  20 us (20%)
  local copies, waits for them, and re-layouts  3.72 us (4%)
    all_to_all x1, waiting for transfers between devices, body(): seen = lax.all_to_all(rolled.reshape(NY, SLAB, NZ), 'block', 0, 0)  26.6 us
    ppermute x12, starting transfers between devices, turn(): lax.ppermute(block, axis, [(i, (i + step) % size) for i in range(size)])  14 us
    ppermute x12, waiting for transfers between devices, turn(): lax.ppermute(block, axis, [(i, (i + step) % size) for i in range(size)])  13 us
    ppermute x6, starting transfers between devices, swap(): lax.ppermute(block, 'block', pairs + [(target, source) for source, target...  12.7 us
    pallas_call x1, Pallas kernels, forward(): pl.pallas_call(forward_kernel, out_shape=jax.ShapeDtypeStruct((NY, SLAB,...  7.05 us
    all_to_all x1, starting transfers between devices, body(): seen = lax.all_to_all(rolled.reshape(NY, SLAB, NZ), 'block', 0, 0)  5.94 us
    ppermute x6, waiting for transfers between devices, swap(): lax.ppermute(block, 'block', pairs + [(target, source) for source, target...  4.29 us
    unnamed x22, local copies, waits for them, and re-layouts  3.72 us
  transfers between devices with their start and end apart: 19, of which 12 were waited for; matrix products, arithmetic and copies ran while one was open for 0% of the time, Pallas kernels for 13%

profile of v8, /device:TPU:24, one launch (start us, length us, event | category | flops | bytes accessed | tf_op | source)
XLA Modules:
  0.0 101.3 jit_solution(13415290835262935212)
XLA Ops:
  0.7 2.8 %depart.1 = (f32[3072,128]{1,0:T(8,128)}, f32[16,64,128]{2,1,0:T(8,128)}, f32[16,64,128]{2,1,0:T(8,128)}) custom-call(s32[1]{0:T(128)} %bitcast.1.block, s32[1]{0:T(128)S(6)} %copy.12.shift_hbm, f32[3072,128]{1,0:T(8,128)} %bitcast.39, f32[48,64,128]{2,1,0:T(8,128)} %estimate_ref.5), custom_call_target="tpu_custom_call" | custom-call | flops 1000 | bytes 1048576 | tf_op jit(solution)/shard_map/depart/pallas_call | solution.py:99
  3.4 7.6 %collective-permute-start = (f32[16,64,128]{2,1,0:T(8,128)}, f32[16,64,128]{2,1,0:T(8,128)S(1)}, u32[]{:S(2)}, u32[]{:S(2)}) collective-permute-start(f32[16,64,128]{2,1,0:T(8,128)} %get-tuple-element.32), channel_id=1, source_target_pairs={{1,2},{3,4},{5,6},{7,8},{9,10},{11,12},{13,14},{15,16},{17,18},{19... | collective-permute-start | bytes 1572872 | tf_op jit(solution)/shard_map/ppermute | solution.py:41
  11.1 5.9 %all-to-all-start = ((f32[64,48,128]{2,1,0:T(8,128)}), f32[64,48,128]{2,1,0:T(8,128)}, u32[]{:S(2)}, u32[]{:S(2)}) async-start(f32[64,48,128]{2,1,0:T(8,128)} %bitcast.40), calls=%async_computation | async-start | bytes 3145728 | tf_op jit(solution)/shard_map/all_to_all | solution.py:442
  17.1 1.9 %make_bands.1 = (bf16[64,192]{1,0:T(8,128)(2,1)S(1)}, bf16[64,192]{1,0:T(8,128)(2,1)S(1)}, bf16[256,256]{1,0:T(8,128)(2,1)S(1)}, bf16[256,256]{1,0:T(8,128)(2,1)...) custom-call(s32[1]{0:T(128)} %bitcast.group, s32[1]{0:T(128)} %bitcast.1.block, ...), custom_call_target="tpu_custom_call" | custom-call | tf_op jit(solution)/shard_map/make_bands/pallas_call | solution.py:181
  20.7 1.0 %copy-done.7 = f32[16,64,128]{2,1,0:T(8,128)S(1)} copy-done((f32[16,64,128]{2,1,0:T(8,128)S(1)}, f32[16,64,128]{2,1,0:T(8,128)}, u32[]{:S(2)}) %copy-start.7) | copy-done | bytes 524312
  21.7 1.0 %copy-done.9 = f32[16,64,128]{2,1,0:T(8,128)S(1)} copy-done((f32[16,64,128]{2,1,0:T(8,128)S(1)}, f32[16,64,128]{2,1,0:T(8,128)}, u32[]{:S(2)}) %copy-start.9) | copy-done | bytes 524312
  22.8 7.0 %forward.1.predicted_ref = f32[64,48,128]{2,1,0:T(8,128)S(1)} custom-call(f32[16,64,128]{2,1,0:T(8,128)S(1)} %copy-done.7, f32[48,64,128]{2,1,0:T(8,128)S(1)} %copy-done, f32[16,64,128]{2,1,0:T(8,128)S(1)} %copy-done.9, bf16[64,192]{1,0:T(8,128)(2,1)S(1)} %get-tuple-element.34.yf_ref, bf16[256,256]{1,0:T(8,128)(2,1)S(1)} %get-tuple-element.35.zf_ref, ...), custom_call_target="tpu_custom_call" | custom-call | flops 199999995904 | bytes 6291456 | tf_op jit(solution)/shard_map/forward/pallas_call | solution.py:235
  29.8 26.6 %all-to-all-done.seen_ref = f32[64,48,128]{2,1,0:T(8,128)} async-done(((f32[64,48,128]{2,1,0:T(8,128)}), f32[64,48,128]{2,1,0:T(8,128)}, u32[]{:S(2)}, u32[]{:S(2)}) %all-to-all-start) | async-done | bytes 1572896 | tf_op jit(solution)/shard_map/all_to_all | solution.py:442
  56.4 3.2 %quotient.1 = (f32[16,64,128]{2,1,0:T(8,128)S(1)}, f32[16,64,128]{2,1,0:T(8,128)S(1)}, f32[16,64,128]{2,1,0:T(8,128)S(1)}, f32[16,24,128]{2,1,0:T(8,128)S(1)}, f...) custom-call(s32[1]{0:T(128)} %bitcast.1.block, s32[3]{0:T(128)S(1)} %copy-done.2, ...), custom_call_target="tpu_custom_call" | custom-call | flops 1000 | bytes 1000 | tf_op jit(solution)/shard_map/quotient/pallas_call | solution.py:304
  59.6 1.4 %collective-permute-start.2 = (f32[16,24,128]{2,1,0:T(8,128)S(1)}, f32[16,24,128]{2,1,0:T(8,128)S(1)}, u32[]{:S(2)}, u32[]{:S(2)}) collective-permute-start(f32[16,24,128]{2,1,0:T(8,128)S(1)} %get-tuple-element.39), channel_id=1, source_target_pairs={{1,2},{3,4},{5,6},{7,8},{9,10},{11,12},{13,14},{15,16},{17,18},{19... | collective-permute-start | bytes 589832 | tf_op jit(solution)/shard_map/ppermute | solution.py:41
  61.0 3.7 %collective-permute-start.3 = (f32[16,40,128]{2,1,0:T(8,128)S(1)}, f32[16,40,128]{2,1,0:T(8,128)S(1)}, u32[]{:S(2)}, u32[]{:S(2)}) collective-permute-start(f32[16,40,128]{2,1,0:T(8,128)S(1)} %get-tuple-element.40), channel_id=1, source_target_pairs={{1,2},{3,4},{5,6},{7,8},{9,10},{11,12},{13,14},{15,16},{17,18},{19... | collective-permute-start | bytes 983048 | tf_op jit(solution)/shard_map/ppermute | solution.py:41
  64.8 3.3 %collective-permute-done.2 = f32[16,24,128]{2,1,0:T(8,128)S(1)} collective-permute-done((f32[16,24,128]{2,1,0:T(8,128)S(1)}, f32[16,24,128]{2,1,0:T(8,128)S(1)}, u32[]{:S(2)}, u32[]{:S(2)}) %collective-permute-start.2) | collective-permute-done | bytes 196640 | tf_op jit(solution)/shard_map/ppermute | solution.py:41
  68.9 1.8 %collective-permute-start.8 = (f32[8,48,128]{2,1,0:T(8,128)S(1)}, f32[8,48,128]{2,1,0:T(8,128)S(1)}, u32[]{:S(2)}, u32[]{:S(2)}) collective-permute-start(f32[8,48,128]{2,1,0:T(8,128)S(1)} %get-tuple-element.52), channel_id=1, source_target_pairs={{0,192},{64,0},{128,64},{192,128},{1,193},{65,1},{129,65},{193,129... | collective-permute-start | bytes 589832 | tf_op jit(solution)/shard_map/ppermute | solution.py:434
  71.6 1.2 %backward.2 = (f32[8,48,128]{2,1,0:T(8,128)S(1)}, f32[8,48,128]{2,1,0:T(8,128)S(1)}, f32[8,48,128]{2,1,0:T(8,128)S(1)}, f32[8,48,128]{2,1,0:T(8,128)S(1)}, f32[8...) custom-call(f32[384,128]{1,0:T(8,128)S(1)} %bitcast.37, f32[640,128]{1,0:T(8,128)S(1)} %bitcast.29, ...), custom_call_target="tpu_custom_call" | custom-call | flops 1000 | bytes 1000 | tf_op jit(solution)/shard_map/backward/pallas_call | solution.py:359
  73.4 1.5 %collective-permute-start.6 = (f32[8,48,128]{2,1,0:T(8,128)S(1)}, f32[8,48,128]{2,1,0:T(8,128)S(1)}, u32[]{:S(2)}, u32[]{:S(2)}) collective-permute-start(f32[8,48,128]{2,1,0:T(8,128)S(1)} %get-tuple-element.48), channel_id=1, source_target_pairs={{0,192},{64,0},{128,64},{192,128},{1,193},{65,1},{129,65},{193,129... | collective-permute-start | bytes 589832 | tf_op jit(solution)/shard_map/ppermute | solution.py:434
  76.0 1.4 %collective-permute-start.13 = (f32[8,48,128]{2,1,0:T(8,128)S(1)}, f32[8,48,128]{2,1,0:T(8,128)S(1)}, u32[]{:S(2)}, u32[]{:S(2)}) collective-permute-start(f32[8,48,128]{2,1,0:T(8,128)S(1)} %add.22), channel_id=1, source_target_pairs={{0,64},{64,128},{128,192},{192,0},{1,65},{65,129},{129,193},{193,1... | collective-permute-start | bytes 589832 | tf_op jit(solution)/shard_map/ppermute | solution.py:434
  78.3 2.4 %collective-permute-done.5 = f32[8,48,128]{2,1,0:T(8,128)S(1)} collective-permute-done((f32[8,48,128]{2,1,0:T(8,128)S(1)}, f32[8,48,128]{2,1,0:T(8,128)S(1)}, u32[]{:S(2)}, u32[]{:S(2)}) %collective-permute-start.5) | collective-permute-done | bytes 196640 | tf_op jit(solution)/shard_map/ppermute | solution.py:434
  80.7 1.4 %collective-permute-done.6 = f32[8,48,128]{2,1,0:T(8,128)S(1)} collective-permute-done((f32[8,48,128]{2,1,0:T(8,128)S(1)}, f32[8,48,128]{2,1,0:T(8,128)S(1)}, u32[]{:S(2)}, u32[]{:S(2)}) %collective-permute-start.6) | collective-permute-done | bytes 196640 | tf_op jit(solution)/shard_map/ppermute | solution.py:434
  82.8 1.6 %collective-permute-start.14 = (f32[8,48,128]{2,1,0:T(8,128)S(1)}, f32[8,48,128]{2,1,0:T(8,128)S(1)}, u32[]{:S(2)}, u32[]{:S(2)}) collective-permute-start(f32[8,48,128]{2,1,0:T(8,128)S(1)} %add_add_fusion), channel_id=1, source_target_pairs={{0,64},{64,128},{128,192},{192,0},{1,65},{65,129},{129,193},{193,1... | collective-permute-start | bytes 589832 | tf_op jit(solution)/shard_map/ppermute | solution.py:434
  85.0 2.7 %collective-permute-start.16 = (f32[8,48,128]{2,1,0:T(8,128)S(1)}, f32[8,48,128]{2,1,0:T(8,128)S(1)}, u32[]{:S(2)}, u32[]{:S(2)}) collective-permute-start(f32[8,48,128]{2,1,0:T(8,128)S(1)} %add_add_fusion.1), channel_id=1, source_target_pairs={{0,64},{64,128},{128,192},{192,0},{1,65},{65,129},{129,193},{193,1... | collective-permute-start | bytes 589832 | tf_op jit(solution)/shard_map/ppermute | solution.py:434
  87.8 3.0 %collective-permute-done.14 = f32[8,48,128]{2,1,0:T(8,128)S(1)} collective-permute-done((f32[8,48,128]{2,1,0:T(8,128)S(1)}, f32[8,48,128]{2,1,0:T(8,128)S(1)}, u32[]{:S(2)}, u32[]{:S(2)}) %collective-permute-start.14) | collective-permute-done | bytes 196640 | tf_op jit(solution)/shard_map/ppermute | solution.py:434
  90.7 2.6 %collective-permute-start.15 = (f32[8,48,128]{2,1,0:T(8,128)S(1)}, f32[8,48,128]{2,1,0:T(8,128)S(1)}, u32[]{:S(2)}, u32[]{:S(2)}) collective-permute-start(f32[8,48,128]{2,1,0:T(8,128)S(1)} %collective-permute-done.14), channel_id=1, source_target_pairs={{0,64},{64,128},{128,192},{192,0},{1,65},{65,129},{129,193},{193,1... | collective-permute-start | bytes 589832 | tf_op jit(solution)/shard_map/ppermute | solution.py:434
  94.0 2.9 %collective-permute-done.17 = f32[8,48,128]{2,1,0:T(8,128)S(1)} collective-permute-done((f32[8,48,128]{2,1,0:T(8,128)S(1)}, f32[8,48,128]{2,1,0:T(8,128)S(1)}, u32[]{:S(2)}, u32[]{:S(2)}) %collective-permute-start.17) | collective-permute-done | bytes 196640 | tf_op jit(solution)/shard_map/ppermute | solution.py:434
  96.9 1.8 %finish.1.rest_1_ = f32[48,64,128]{2,1,0:T(8,128)} custom-call(s32[1]{0:T(128)} %bitcast.group, f32[48,64,128]{2,1,0:T(8,128)S(1)} %copy-done, f32[384,128]{1,0:T(8,128)S(1)} %bitcast.20, f32[384,128]{1,0:T(8,128)S(1)} %bitcast.21, f32[384,128]{1,0:T(8,128)S(1)} %bitcast.30, f32[384,128]{1,0:T(8,128)S(1)} %bitcast.32, f32[384,128]{1,0:T(8,128)S(1)} %bitcast.33, ...), custom_call_target="tpu_custom_call" | custom-call | flops 1000 | bytes 1000 | tf_op jit(solution)/shard_map/finish/pallas_call | solution.py:410
  (50 shorter events, 10.4 us)
Async XLA Ops:
  3.4 15.6 %collective-permute-start = (f32[16,64,128]{2,1,0:T(8,128)}, f32[16,64,128]{2,1,0:T(8,128)S(1)}, u32[]{:S(2)}, u32[]{:S(2)}) collective-permute-start(f32[16,64,128]{2,1,0:T(8,128)} %get-tuple-element.32), channel_id=1, source_target_pairs={{1,2},{3,4},{5,6},{7,8},{9,10},{11,12},{13,14},{15,16},{17,18},{19... | collective-permute-start | bytes 1572872 | tf_op jit(solution)/shard_map/ppermute | solution.py:41
  11.0 8.9 %collective-permute-start.1 = (f32[16,64,128]{2,1,0:T(8,128)}, f32[16,64,128]{2,1,0:T(8,128)S(1)}, u32[]{:S(2)}, u32[]{:S(2)}) collective-permute-start(f32[16,64,128]{2,1,0:T(8,128)} %get-tuple-element.33), channel_id=1, source_target_pairs={{0,1},{2,3},{4,5},{6,7},{8,9},{10,11},{12,13},{14,15},{16,17},{18,... | collective-permute-start | bytes 1572872 | tf_op jit(solution)/shard_map/ppermute | solution.py:41
  11.0 6.1 %copy-start.3 = (f32[1,31]{1,0:T(1,128)S(1)}, f32[1,31]{1,0:T(1,128)}, u32[]{:S(2)}) copy-start(f32[1,31]{1,0:T(1,128)} %x_ref.1) | copy-start | bytes 376
  11.0 6.1 %copy-start.4 = (f32[1,31]{1,0:T(1,128)S(1)}, f32[1,31]{1,0:T(1,128)}, u32[]{:S(2)}) copy-start(f32[1,31]{1,0:T(1,128)} %y_ref.1) | copy-start | bytes 376
  11.0 6.1 %copy-start.5 = (f32[1,61]{1,0:T(1,128)S(1)}, f32[1,61]{1,0:T(1,128)}, u32[]{:S(2)}) copy-start(f32[1,61]{1,0:T(1,128)} %z_ref.1) | copy-start | bytes 736
  11.0 9.6 %copy-start = (f32[48,64,128]{2,1,0:T(8,128)S(1)}, f32[48,64,128]{2,1,0:T(8,128)}, u32[]{:S(2)}) copy-start(f32[48,64,128]{2,1,0:T(8,128)} %estimate_ref.5) | copy-start | bytes 4718596
  11.1 45.3 %all-to-all-start = ((f32[64,48,128]{2,1,0:T(8,128)}), f32[64,48,128]{2,1,0:T(8,128)}, u32[]{:S(2)}, u32[]{:S(2)}) async-start(f32[64,48,128]{2,1,0:T(8,128)} %bitcast.40), calls=%async_computation | async-start | bytes 3145728 | tf_op jit(solution)/shard_map/all_to_all | solution.py:442
  22.8 33.6 %copy-start.2 = (s32[3]{0:T(128)S(1)}, s32[3]{0:T(128)}, u32[]{:S(2)}) copy-start(s32[3]{0:T(128)} %copy-done.1) | copy-start | bytes 40
  59.6 8.5 %collective-permute-start.2 = (f32[16,24,128]{2,1,0:T(8,128)S(1)}, f32[16,24,128]{2,1,0:T(8,128)S(1)}, u32[]{:S(2)}, u32[]{:S(2)}) collective-permute-start(f32[16,24,128]{2,1,0:T(8,128)S(1)} %get-tuple-element.39), channel_id=1, source_target_pairs={{1,2},{3,4},{5,6},{7,8},{9,10},{11,12},{13,14},{15,16},{17,18},{19... | collective-permute-start | bytes 589832 | tf_op jit(solution)/shard_map/ppermute | solution.py:41
  61.0 3.7 %collective-permute-start.7 = (f32[16,16,128]{2,1,0:T(8,128)S(1)}, f32[16,16,128]{2,1,0:T(8,128)S(1)}, u32[]{:S(2)}, u32[]{:S(2)}) collective-permute-start(f32[16,16,128]{2,1,0:T(8,128)S(1)} %get-tuple-element.51), channel_id=1, source_target_pairs={{0,1},{2,3},{4,5},{6,7},{8,9},{10,11},{12,13},{14,15},{16,17},{18,... | collective-permute-start | bytes 393224 | tf_op jit(solution)/shard_map/ppermute | solution.py:41
  61.0 10.6 %collective-permute-start.3 = (f32[16,40,128]{2,1,0:T(8,128)S(1)}, f32[16,40,128]{2,1,0:T(8,128)S(1)}, u32[]{:S(2)}, u32[]{:S(2)}) collective-permute-start(f32[16,40,128]{2,1,0:T(8,128)S(1)} %get-tuple-element.40), channel_id=1, source_target_pairs={{1,2},{3,4},{5,6},{7,8},{9,10},{11,12},{13,14},{15,16},{17,18},{19... | collective-permute-start | bytes 983048 | tf_op jit(solution)/shard_map/ppermute | solution.py:41
  64.8 6.9 %collective-permute-start.4 = (f32[16,48,128]{2,1,0:T(8,128)S(1)}, f32[16,48,128]{2,1,0:T(8,128)S(1)}, u32[]{:S(2)}, u32[]{:S(2)}) collective-permute-start(f32[16,48,128]{2,1,0:T(8,128)S(1)} %get-tuple-element.41), channel_id=1, source_target_pairs={{0,1},{2,3},{4,5},{6,7},{8,9},{10,11},{12,13},{14,15},{16,17},{18,... | collective-permute-start | bytes 1179656 | tf_op jit(solution)/shard_map/ppermute | solution.py:41
  68.6 7.3 %collective-permute-start.12 = (f32[8,48,128]{2,1,0:T(8,128)S(1)}, f32[8,48,128]{2,1,0:T(8,128)S(1)}, u32[]{:S(2)}, u32[]{:S(2)}) collective-permute-start(f32[8,48,128]{2,1,0:T(8,128)S(1)} %get-tuple-element.56), channel_id=1, source_target_pairs={{0,64},{64,128},{128,192},{192,0},{1,65},{65,129},{129,193},{193,1... | collective-permute-start | bytes 589832 | tf_op jit(solution)/shard_map/ppermute | solution.py:434
  68.9 8.5 %collective-permute-start.8 = (f32[8,48,128]{2,1,0:T(8,128)S(1)}, f32[8,48,128]{2,1,0:T(8,128)S(1)}, u32[]{:S(2)}, u32[]{:S(2)}) collective-permute-start(f32[8,48,128]{2,1,0:T(8,128)S(1)} %get-tuple-element.52), channel_id=1, source_target_pairs={{0,192},{64,0},{128,64},{192,128},{1,193},{65,1},{129,65},{193,129... | collective-permute-start | bytes 589832 | tf_op jit(solution)/shard_map/ppermute | solution.py:434
  72.8 7.9 %collective-permute-start.5 = (f32[8,48,128]{2,1,0:T(8,128)S(1)}, f32[8,48,128]{2,1,0:T(8,128)S(1)}, u32[]{:S(2)}, u32[]{:S(2)}) collective-permute-start(f32[8,48,128]{2,1,0:T(8,128)S(1)} %get-tuple-element.47), channel_id=1, source_target_pairs={{0,64},{64,128},{128,192},{192,0},{1,65},{65,129},{129,193},{193,1... | collective-permute-start | bytes 589832 | tf_op jit(solution)/shard_map/ppermute | solution.py:434
  73.4 8.7 %collective-permute-start.6 = (f32[8,48,128]{2,1,0:T(8,128)S(1)}, f32[8,48,128]{2,1,0:T(8,128)S(1)}, u32[]{:S(2)}, u32[]{:S(2)}) collective-permute-start(f32[8,48,128]{2,1,0:T(8,128)S(1)} %get-tuple-element.48), channel_id=1, source_target_pairs={{0,192},{64,0},{128,64},{192,128},{1,193},{65,1},{129,65},{193,129... | collective-permute-start | bytes 589832 | tf_op jit(solution)/shard_map/ppermute | solution.py:434
  76.0 6.8 %collective-permute-start.13 = (f32[8,48,128]{2,1,0:T(8,128)S(1)}, f32[8,48,128]{2,1,0:T(8,128)S(1)}, u32[]{:S(2)}, u32[]{:S(2)}) collective-permute-start(f32[8,48,128]{2,1,0:T(8,128)S(1)} %add.22), channel_id=1, source_target_pairs={{0,64},{64,128},{128,192},{192,0},{1,65},{65,129},{129,193},{193,1... | collective-permute-start | bytes 589832 | tf_op jit(solution)/shard_map/ppermute | solution.py:434
  77.4 7.0 %collective-permute-start.9 = (f32[8,48,128]{2,1,0:T(8,128)S(1)}, f32[8,48,128]{2,1,0:T(8,128)S(1)}, u32[]{:S(2)}, u32[]{:S(2)}) collective-permute-start(f32[8,48,128]{2,1,0:T(8,128)S(1)} %add.19), channel_id=1, source_target_pairs={{0,192},{64,0},{128,64},{192,128},{1,193},{65,1},{129,65},{193,129... | collective-permute-start | bytes 589832 | tf_op jit(solution)/shard_map/ppermute | solution.py:434
  82.8 7.9 %collective-permute-start.14 = (f32[8,48,128]{2,1,0:T(8,128)S(1)}, f32[8,48,128]{2,1,0:T(8,128)S(1)}, u32[]{:S(2)}, u32[]{:S(2)}) collective-permute-start(f32[8,48,128]{2,1,0:T(8,128)S(1)} %add_add_fusion), channel_id=1, source_target_pairs={{0,64},{64,128},{128,192},{192,0},{1,65},{65,129},{129,193},{193,1... | collective-permute-start | bytes 589832 | tf_op jit(solution)/shard_map/ppermute | solution.py:434
  84.4 9.0 %collective-permute-start.10 = (f32[8,48,128]{2,1,0:T(8,128)S(1)}, f32[8,48,128]{2,1,0:T(8,128)S(1)}, u32[]{:S(2)}, u32[]{:S(2)}) collective-permute-start(f32[8,48,128]{2,1,0:T(8,128)S(1)} %add_add_fusion.1), channel_id=1, source_target_pairs={{0,192},{64,0},{128,64},{192,128},{1,193},{65,1},{129,65},{193,129... | collective-permute-start | bytes 589832 | tf_op jit(solution)/shard_map/ppermute | solution.py:434
  85.0 8.9 %collective-permute-start.16 = (f32[8,48,128]{2,1,0:T(8,128)S(1)}, f32[8,48,128]{2,1,0:T(8,128)S(1)}, u32[]{:S(2)}, u32[]{:S(2)}) collective-permute-start(f32[8,48,128]{2,1,0:T(8,128)S(1)} %add_add_fusion.1), channel_id=1, source_target_pairs={{0,64},{64,128},{128,192},{192,0},{1,65},{65,129},{129,193},{193,1... | collective-permute-start | bytes 589832 | tf_op jit(solution)/shard_map/ppermute | solution.py:434
  87.8 9.1 %collective-permute-start.17 = (f32[8,48,128]{2,1,0:T(8,128)S(1)}, f32[8,48,128]{2,1,0:T(8,128)S(1)}, u32[]{:S(2)}, u32[]{:S(2)}) collective-permute-start(f32[8,48,128]{2,1,0:T(8,128)S(1)} %add_add_fusion), channel_id=1, source_target_pairs={{0,192},{64,0},{128,64},{192,128},{1,193},{65,1},{129,65},{193,129... | collective-permute-start | bytes 589832 | tf_op jit(solution)/shard_map/ppermute | solution.py:434
  90.7 7.9 %collective-permute-start.15 = (f32[8,48,128]{2,1,0:T(8,128)S(1)}, f32[8,48,128]{2,1,0:T(8,128)S(1)}, u32[]{:S(2)}, u32[]{:S(2)}) collective-permute-start(f32[8,48,128]{2,1,0:T(8,128)S(1)} %collective-permute-done.14), channel_id=1, source_target_pairs={{0,64},{64,128},{128,192},{192,0},{1,65},{65,129},{129,193},{193,1... | collective-permute-start | bytes 589832 | tf_op jit(solution)/shard_map/ppermute | solution.py:434
  93.5 6.9 %collective-permute-start.11 = (f32[8,48,128]{2,1,0:T(8,128)S(1)}, f32[8,48,128]{2,1,0:T(8,128)S(1)}, u32[]{:S(2)}, u32[]{:S(2)}) collective-permute-start(f32[8,48,128]{2,1,0:T(8,128)S(1)} %collective-permute-done.10), channel_id=1, source_target_pairs={{0,192},{64,0},{128,64},{192,128},{1,193},{65,1},{129,65},{193,129... | collective-permute-start | bytes 589832 | tf_op jit(solution)/shard_map/ppermute | solution.py:434
  (6 other events, 13.3 us)

commit v9 on v7

--- a/solution.py
+++ b/solution.py
@@ -411,7 +411,6 @@
 
     far_a, far_b = backward(((32, 0), (40, 8)), FAR_COST, across, wholes, xb)
     far_a, far_b = turn(far_a, "group", 1), turn(far_b, "group", -1)
-    far_a, far_b = lax.optimization_barrier((far_a, far_b))
     next_a, near_b, near_a, prev_b, own_a, own_b = backward(
         ((16, 16), (24, 24), (48, 32), (56, 40), (0, 0), (8, 8)), SHORT, rest, wholes, xb
     )

time: 101 us -> 101 us (level)
  transfers between devices with their start and end apart: 18 -> 18, of which waited for: 10 -> 9; matrix products, arithmetic and copies ran while one was open for 0% -> 0% of each run, Pallas kernels for 13% -> 13%
where the time goes in v9:
time: 101 us
  waiting for transfers between devices  43.3 us (43%)
  starting transfers between devices  32.6 us (32%)
  Pallas kernels  20.1 us (20%)
  local copies, waits for them, and re-layouts  3.69 us (4%)
    all_to_all x1, waiting for transfers between devices, body(): seen = lax.all_to_all(rolled.reshape(NY, SLAB, NZ), 'block', 0, 0)  26.6 us
    ppermute x12, starting transfers between devices, turn(): lax.ppermute(block, axis, [(i, (i + step) % size) for i in range(size)])  13.5 us
    ppermute x5, starting transfers between devices, swap(): lax.ppermute(block, 'block', pairs + [(target, source) for source, target...  13.1 us
    ppermute x12, waiting for transfers between devices, turn(): lax.ppermute(block, axis, [(i, (i + step) % size) for i in range(size)])  12.1 us
    pallas_call x1, Pallas kernels, forward(): pl.pallas_call(forward_kernel, out_shape=jax.ShapeDtypeStruct((NY, SLAB,...  7.04 us
    all_to_all x1, starting transfers between devices, body(): seen = lax.all_to_all(rolled.reshape(NY, SLAB, NZ), 'block', 0, 0)  5.94 us
    ppermute x5, waiting for transfers between devices, swap(): lax.ppermute(block, 'block', pairs + [(target, source) for source, target...  4.64 us
    unnamed x22, local copies, waits for them, and re-layouts  3.69 us
  transfers between devices with their start and end apart: 18, of which 9 were waited for; matrix products, arithmetic and copies ran while one was open for 0% of the time, Pallas kernels for 13%

profile of v9, /device:TPU:24, one launch (start us, length us, event | category | flops | bytes accessed | tf_op | source)
XLA Modules:
  0.0 100.8 jit_solution(3477657931393492199)
XLA Ops:
  0.7 2.8 %depart.1 = (f32[3072,128]{1,0:T(8,128)}, f32[16,64,128]{2,1,0:T(8,128)}, f32[16,64,128]{2,1,0:T(8,128)}) custom-call(s32[1]{0:T(128)} %bitcast.1.block, s32[1]{0:T(128)S(6)} %copy.12.shift_hbm, f32[3072,128]{1,0:T(8,128)} %bitcast.37, f32[48,64,128]{2,1,0:T(8,128)} %estimate_ref.5), custom_call_target="tpu_custom_call" | custom-call | flops 1000 | bytes 1048576 | tf_op jit(solution)/shard_map/depart/pallas_call | solution.py:99
  3.4 7.6 %collective-permute-start = (f32[16,64,128]{2,1,0:T(8,128)}, f32[16,64,128]{2,1,0:T(8,128)S(1)}, u32[]{:S(2)}, u32[]{:S(2)}) collective-permute-start(f32[16,64,128]{2,1,0:T(8,128)} %get-tuple-element.30), channel_id=1, source_target_pairs={{1,2},{3,4},{5,6},{7,8},{9,10},{11,12},{13,14},{15,16},{17,18},{19... | collective-permute-start | bytes 1572872 | tf_op jit(solution)/shard_map/ppermute | solution.py:41
  11.1 5.9 %all-to-all-start = ((f32[64,48,128]{2,1,0:T(8,128)}), f32[64,48,128]{2,1,0:T(8,128)}, u32[]{:S(2)}, u32[]{:S(2)}) async-start(f32[64,48,128]{2,1,0:T(8,128)} %bitcast.38), calls=%async_computation | async-start | bytes 3145728 | tf_op jit(solution)/shard_map/all_to_all | solution.py:404
  17.1 1.9 %make_bands.1 = (bf16[64,192]{1,0:T(8,128)(2,1)S(1)}, bf16[64,192]{1,0:T(8,128)(2,1)S(1)}, bf16[256,256]{1,0:T(8,128)(2,1)S(1)}, bf16[256,256]{1,0:T(8,128)(2,1)...) custom-call(s32[1]{0:T(128)} %bitcast.group, s32[1]{0:T(128)} %bitcast.1.block, ...), custom_call_target="tpu_custom_call" | custom-call | tf_op jit(solution)/shard_map/make_bands/pallas_call | solution.py:181
  22.7 7.0 %forward.1.predicted_ref = f32[64,48,128]{2,1,0:T(8,128)S(1)} custom-call(f32[16,64,128]{2,1,0:T(8,128)S(1)} %copy-done.7, f32[48,64,128]{2,1,0:T(8,128)S(1)} %copy-done, f32[16,64,128]{2,1,0:T(8,128)S(1)} %copy-done.9, bf16[64,192]{1,0:T(8,128)(2,1)S(1)} %get-tuple-element.32.yf_ref, bf16[256,256]{1,0:T(8,128)(2,1)S(1)} %get-tuple-element.33.zf_ref, ...), custom_call_target="tpu_custom_call" | custom-call | flops 199999995904 | bytes 6291456 | tf_op jit(solution)/shard_map/forward/pallas_call | solution.py:235
  29.8 26.6 %all-to-all-done.seen_ref = f32[64,48,128]{2,1,0:T(8,128)} async-done(((f32[64,48,128]{2,1,0:T(8,128)}), f32[64,48,128]{2,1,0:T(8,128)}, u32[]{:S(2)}, u32[]{:S(2)}) %all-to-all-start) | async-done | bytes 1572896 | tf_op jit(solution)/shard_map/all_to_all | solution.py:404
  56.4 3.2 %quotient.1 = (f32[16,64,128]{2,1,0:T(8,128)S(1)}, f32[16,64,128]{2,1,0:T(8,128)S(1)}, f32[16,64,128]{2,1,0:T(8,128)S(1)}, f32[16,16,128]{2,1,0:T(8,128)S(1)}, f32[16,48,128]{2,1,0:T(8,128)S(1)}) custom-call(s32[1]{0:T(128)} %bitcast.1.block, s32[3]{0:T(128)S(1)} %copy-done.2, f32[64,48,128]{2,1,0:T(8,128)} %all-to-all-done.seen_ref, ...), custom_call_target="tpu_custom_call" | custom-call | flops 1000 | bytes 1000 | tf_op jit(solution)/shard_map/quotient/pallas_call | solution.py:286
  60.0 1.8 %collective-permute-start.6 = (f32[16,16,128]{2,1,0:T(8,128)S(1)}, f32[16,16,128]{2,1,0:T(8,128)S(1)}, u32[]{:S(2)}, u32[]{:S(2)}) collective-permute-start(f32[16,16,128]{2,1,0:T(8,128)S(1)} %get-tuple-element.47), channel_id=1, source_target_pairs={{1,2},{3,4},{5,6},{7,8},{9,10},{11,12},{13,14},{15,16},{17,18},{19... | collective-permute-start | bytes 393224 | tf_op jit(solution)/shard_map/ppermute | solution.py:41
  61.8 3.3 %collective-permute-start.2 = (f32[16,48,128]{2,1,0:T(8,128)S(1)}, f32[16,48,128]{2,1,0:T(8,128)S(1)}, u32[]{:S(2)}, u32[]{:S(2)}) collective-permute-start(f32[16,48,128]{2,1,0:T(8,128)S(1)} %get-tuple-element.37), channel_id=1, source_target_pairs={{1,2},{3,4},{5,6},{7,8},{9,10},{11,12},{13,14},{15,16},{17,18},{19... | collective-permute-start | bytes 1179656 | tf_op jit(solution)/shard_map/ppermute | solution.py:41
  65.1 2.6 %collective-permute-done.6 = f32[16,16,128]{2,1,0:T(8,128)S(1)} collective-permute-done((f32[16,16,128]{2,1,0:T(8,128)S(1)}, f32[16,16,128]{2,1,0:T(8,128)S(1)}, u32[]{:S(2)}, u32[]{:S(2)}) %collective-permute-start.6) | collective-permute-done | bytes 131104 | tf_op jit(solution)/shard_map/ppermute | solution.py:41
  68.6 1.8 %collective-permute-start.7 = (f32[8,48,128]{2,1,0:T(8,128)S(1)}, f32[8,48,128]{2,1,0:T(8,128)S(1)}, u32[]{:S(2)}, u32[]{:S(2)}) collective-permute-start(f32[8,48,128]{2,1,0:T(8,128)S(1)} %get-tuple-element.48), channel_id=1, source_target_pairs={{0,192},{64,0},{128,64},{192,128},{1,193},{65,1},{129,65},{193,129... | collective-permute-start | bytes 589832 | tf_op jit(solution)/shard_map/ppermute | solution.py:396
  70.4 2.0 %collective-permute-done.2 = f32[16,48,128]{2,1,0:T(8,128)S(1)} collective-permute-done((f32[16,48,128]{2,1,0:T(8,128)S(1)}, f32[16,48,128]{2,1,0:T(8,128)S(1)}, u32[]{:S(2)}, u32[]{:S(2)}) %collective-permute-start.2) | collective-permute-done | bytes 393248 | tf_op jit(solution)/shard_map/ppermute | solution.py:41
  72.4 1.3 %backward.2 = (f32[8,48,128]{2,1,0:T(8,128)S(1)}, f32[8,48,128]{2,1,0:T(8,128)S(1)}, f32[8,48,128]{2,1,0:T(8,128)S(1)}, f32[8,48,128]{2,1,0:T(8,128)S(1)}, f32[8...) custom-call(f32[768,128]{1,0:T(8,128)S(1)} %bitcast.29, f32[1024,128]{1,0:T(8,128)S(1)} %bitcast.22, ...), custom_call_target="tpu_custom_call" | custom-call | flops 1000 | bytes 1000 | tf_op jit(solution)/shard_map/backward/pallas_call | solution.py:321
  74.0 1.8 %collective-permute-start.5 = (f32[8,48,128]{2,1,0:T(8,128)S(1)}, f32[8,48,128]{2,1,0:T(8,128)S(1)}, u32[]{:S(2)}, u32[]{:S(2)}) collective-permute-start(f32[8,48,128]{2,1,0:T(8,128)S(1)} %get-tuple-element.44), channel_id=1, source_target_pairs={{0,192},{64,0},{128,64},{192,128},{1,193},{65,1},{129,65},{193,129... | collective-permute-start | bytes 589832 | tf_op jit(solution)/shard_map/ppermute | solution.py:396
  75.8 1.6 %collective-permute-start.12 = (f32[8,48,128]{2,1,0:T(8,128)S(1)}, f32[8,48,128]{2,1,0:T(8,128)S(1)}, u32[]{:S(2)}, u32[]{:S(2)}) collective-permute-start(f32[8,48,128]{2,1,0:T(8,128)S(1)} %add.22), channel_id=1, source_target_pairs={{0,64},{64,128},{128,192},{192,0},{1,65},{65,129},{129,193},{193,1... | collective-permute-start | bytes 589832 | tf_op jit(solution)/shard_map/ppermute | solution.py:396
  78.0 2.3 %collective-permute-done.4 = f32[8,48,128]{2,1,0:T(8,128)S(1)} collective-permute-done((f32[8,48,128]{2,1,0:T(8,128)S(1)}, f32[8,48,128]{2,1,0:T(8,128)S(1)}, u32[]{:S(2)}, u32[]{:S(2)}) %collective-permute-start.4) | collective-permute-done | bytes 196640 | tf_op jit(solution)/shard_map/ppermute | solution.py:396
  80.3 1.4 %collective-permute-done.5 = f32[8,48,128]{2,1,0:T(8,128)S(1)} collective-permute-done((f32[8,48,128]{2,1,0:T(8,128)S(1)}, f32[8,48,128]{2,1,0:T(8,128)S(1)}, u32[]{:S(2)}, u32[]{:S(2)}) %collective-permute-start.5) | collective-permute-done | bytes 196640 | tf_op jit(solution)/shard_map/ppermute | solution.py:396
  83.0 1.4 %collective-permute-start.13 = (f32[8,48,128]{2,1,0:T(8,128)S(1)}, f32[8,48,128]{2,1,0:T(8,128)S(1)}, u32[]{:S(2)}, u32[]{:S(2)}) collective-permute-start(f32[8,48,128]{2,1,0:T(8,128)S(1)} %add_add_fusion), channel_id=1, source_target_pairs={{0,64},{64,128},{128,192},{192,0},{1,65},{65,129},{129,193},{193,1... | collective-permute-start | bytes 589832 | tf_op jit(solution)/shard_map/ppermute | solution.py:396
  85.2 2.5 %collective-permute-start.15 = (f32[8,48,128]{2,1,0:T(8,128)S(1)}, f32[8,48,128]{2,1,0:T(8,128)S(1)}, u32[]{:S(2)}, u32[]{:S(2)}) collective-permute-start(f32[8,48,128]{2,1,0:T(8,128)S(1)} %add_add_fusion.1), channel_id=1, source_target_pairs={{0,64},{64,128},{128,192},{192,0},{1,65},{65,129},{129,193},{193,1... | collective-permute-start | bytes 589832 | tf_op jit(solution)/shard_map/ppermute | solution.py:396
  87.7 2.8 %collective-permute-done.13 = f32[8,48,128]{2,1,0:T(8,128)S(1)} collective-permute-done((f32[8,48,128]{2,1,0:T(8,128)S(1)}, f32[8,48,128]{2,1,0:T(8,128)S(1)}, u32[]{:S(2)}, u32[]{:S(2)}) %collective-permute-start.13) | collective-permute-done | bytes 196640 | tf_op jit(solution)/shard_map/ppermute | solution.py:396
  90.6 2.4 %collective-permute-start.14 = (f32[8,48,128]{2,1,0:T(8,128)S(1)}, f32[8,48,128]{2,1,0:T(8,128)S(1)}, u32[]{:S(2)}, u32[]{:S(2)}) collective-permute-start(f32[8,48,128]{2,1,0:T(8,128)S(1)} %collective-permute-done.13), channel_id=1, source_target_pairs={{0,64},{64,128},{128,192},{192,0},{1,65},{65,129},{129,193},{193,1... | collective-permute-start | bytes 589832 | tf_op jit(solution)/shard_map/ppermute | solution.py:396
  93.0 2.7 %collective-permute-done.16 = f32[8,48,128]{2,1,0:T(8,128)S(1)} collective-permute-done((f32[8,48,128]{2,1,0:T(8,128)S(1)}, f32[8,48,128]{2,1,0:T(8,128)S(1)}, u32[]{:S(2)}, u32[]{:S(2)}) %collective-permute-start.16) | collective-permute-done | bytes 196640 | tf_op jit(solution)/shard_map/ppermute | solution.py:396
  95.7 1.8 %finish.1.rest_1_ = f32[48,64,128]{2,1,0:T(8,128)} custom-call(s32[1]{0:T(128)} %bitcast.group, f32[48,64,128]{2,1,0:T(8,128)S(1)} %copy-done, f32[384,128]{1,0:T(8,128)S(1)} %bitcast.19, f32[384,128]{1,0:T(8,128)S(1)} %bitcast.20, f32[384,128]{1,0:T(8,128)S(1)} %bitcast.30, f32[384,128]{1,0:T(8,128)S(1)} %bitcast.32, f32[384,128]{1,0:T(8,128)S(1)} %bitcast.33, ...), custom_call_target="tpu_custom_call" | custom-call | flops 1000 | bytes 1000 | tf_op jit(solution)/shard_map/finish/pallas_call | solution.py:372
  98.2 1.6 %collective-permute-done.10 = f32[8,48,128]{2,1,0:T(8,128)S(1)} collective-permute-done((f32[8,48,128]{2,1,0:T(8,128)S(1)}, f32[8,48,128]{2,1,0:T(8,128)S(1)}, u32[]{:S(2)}, u32[]{:S(2)}) %collective-permute-start.10) | collective-permute-done | bytes 196640 | tf_op jit(solution)/shard_map/ppermute | solution.py:396
  (48 shorter events, 9.6 us)
Async XLA Ops:
  3.4 15.6 %collective-permute-start = (f32[16,64,128]{2,1,0:T(8,128)}, f32[16,64,128]{2,1,0:T(8,128)S(1)}, u32[]{:S(2)}, u32[]{:S(2)}) collective-permute-start(f32[16,64,128]{2,1,0:T(8,128)} %get-tuple-element.30), channel_id=1, source_target_pairs={{1,2},{3,4},{5,6},{7,8},{9,10},{11,12},{13,14},{15,16},{17,18},{19... | collective-permute-start | bytes 1572872 | tf_op jit(solution)/shard_map/ppermute | solution.py:41
  11.0 8.8 %collective-permute-start.1 = (f32[16,64,128]{2,1,0:T(8,128)}, f32[16,64,128]{2,1,0:T(8,128)S(1)}, u32[]{:S(2)}, u32[]{:S(2)}) collective-permute-start(f32[16,64,128]{2,1,0:T(8,128)} %get-tuple-element.31), channel_id=1, source_target_pairs={{0,1},{2,3},{4,5},{6,7},{8,9},{10,11},{12,13},{14,15},{16,17},{18,... | collective-permute-start | bytes 1572872 | tf_op jit(solution)/shard_map/ppermute | solution.py:41
  11.0 6.0 %copy-start.10 = (s32[1,2]{1,0:T(1,128)S(1)}, s32[1,2]{1,0:T(1,128)}, u32[]{:S(2)}) copy-start(s32[1,2]{1,0:T(1,128)} %param.13) | copy-start | bytes 28
  11.0 6.1 %copy-start.3 = (f32[1,31]{1,0:T(1,128)S(1)}, f32[1,31]{1,0:T(1,128)}, u32[]{:S(2)}) copy-start(f32[1,31]{1,0:T(1,128)} %x_ref.1) | copy-start | bytes 376
  11.0 6.1 %copy-start.4 = (f32[1,31]{1,0:T(1,128)S(1)}, f32[1,31]{1,0:T(1,128)}, u32[]{:S(2)}) copy-start(f32[1,31]{1,0:T(1,128)} %y_ref.1) | copy-start | bytes 376
  11.0 6.1 %copy-start.5 = (f32[1,61]{1,0:T(1,128)S(1)}, f32[1,61]{1,0:T(1,128)}, u32[]{:S(2)}) copy-start(f32[1,61]{1,0:T(1,128)} %z_ref.1) | copy-start | bytes 736
  11.0 9.6 %copy-start = (f32[48,64,128]{2,1,0:T(8,128)S(1)}, f32[48,64,128]{2,1,0:T(8,128)}, u32[]{:S(2)}) copy-start(f32[48,64,128]{2,1,0:T(8,128)} %estimate_ref.5) | copy-start | bytes 4718596
  11.1 45.3 %all-to-all-start = ((f32[64,48,128]{2,1,0:T(8,128)}), f32[64,48,128]{2,1,0:T(8,128)}, u32[]{:S(2)}, u32[]{:S(2)}) async-start(f32[64,48,128]{2,1,0:T(8,128)} %bitcast.38), calls=%async_computation | async-start | bytes 3145728 | tf_op jit(solution)/shard_map/all_to_all | solution.py:404
  22.7 33.6 %copy-start.2 = (s32[3]{0:T(128)S(1)}, s32[3]{0:T(128)}, u32[]{:S(2)}) copy-start(s32[3]{0:T(128)} %copy-done.1) | copy-start | bytes 40
  59.6 8.2 %collective-permute-start.3 = (f32[16,64,128]{2,1,0:T(8,128)S(1)}, f32[16,64,128]{2,1,0:T(8,128)S(1)}, u32[]{:S(2)}, u32[]{:S(2)}) collective-permute-start(f32[16,64,128]{2,1,0:T(8,128)S(1)} %get-tuple-element.40), channel_id=1, source_target_pairs={{0,1},{2,3},{4,5},{6,7},{8,9},{10,11},{12,13},{14,15},{16,17},{18,... | collective-permute-start | bytes 1572872 | tf_op jit(solution)/shard_map/ppermute | solution.py:41
  60.0 7.7 %collective-permute-start.6 = (f32[16,16,128]{2,1,0:T(8,128)S(1)}, f32[16,16,128]{2,1,0:T(8,128)S(1)}, u32[]{:S(2)}, u32[]{:S(2)}) collective-permute-start(f32[16,16,128]{2,1,0:T(8,128)S(1)} %get-tuple-element.47), channel_id=1, source_target_pairs={{1,2},{3,4},{5,6},{7,8},{9,10},{11,12},{13,14},{15,16},{17,18},{19... | collective-permute-start | bytes 393224 | tf_op jit(solution)/shard_map/ppermute | solution.py:41
  61.8 10.5 %collective-permute-start.2 = (f32[16,48,128]{2,1,0:T(8,128)S(1)}, f32[16,48,128]{2,1,0:T(8,128)S(1)}, u32[]{:S(2)}, u32[]{:S(2)}) collective-permute-start(f32[16,48,128]{2,1,0:T(8,128)S(1)} %get-tuple-element.37), channel_id=1, source_target_pairs={{1,2},{3,4},{5,6},{7,8},{9,10},{11,12},{13,14},{15,16},{17,18},{19... | collective-permute-start | bytes 1179656 | tf_op jit(solution)/shard_map/ppermute | solution.py:41
  68.3 7.5 %collective-permute-start.11 = (f32[8,48,128]{2,1,0:T(8,128)S(1)}, f32[8,48,128]{2,1,0:T(8,128)S(1)}, u32[]{:S(2)}, u32[]{:S(2)}) collective-permute-start(f32[8,48,128]{2,1,0:T(8,128)S(1)} %get-tuple-element.52), channel_id=1, source_target_pairs={{0,64},{64,128},{128,192},{192,0},{1,65},{65,129},{129,193},{193,1... | collective-permute-start | bytes 589832 | tf_op jit(solution)/shard_map/ppermute | solution.py:396
  68.6 8.8 %collective-permute-start.7 = (f32[8,48,128]{2,1,0:T(8,128)S(1)}, f32[8,48,128]{2,1,0:T(8,128)S(1)}, u32[]{:S(2)}, u32[]{:S(2)}) collective-permute-start(f32[8,48,128]{2,1,0:T(8,128)S(1)} %get-tuple-element.48), channel_id=1, source_target_pairs={{0,192},{64,0},{128,64},{192,128},{1,193},{65,1},{129,65},{193,129... | collective-permute-start | bytes 589832 | tf_op jit(solution)/shard_map/ppermute | solution.py:396
  73.7 6.7 %collective-permute-start.4 = (f32[8,48,128]{2,1,0:T(8,128)S(1)}, f32[8,48,128]{2,1,0:T(8,128)S(1)}, u32[]{:S(2)}, u32[]{:S(2)}) collective-permute-start(f32[8,48,128]{2,1,0:T(8,128)S(1)} %get-tuple-element.43), channel_id=1, source_target_pairs={{0,64},{64,128},{128,192},{192,0},{1,65},{65,129},{129,193},{193,1... | collective-permute-start | bytes 589832 | tf_op jit(solution)/shard_map/ppermute | solution.py:396
  74.0 7.8 %collective-permute-start.5 = (f32[8,48,128]{2,1,0:T(8,128)S(1)}, f32[8,48,128]{2,1,0:T(8,128)S(1)}, u32[]{:S(2)}, u32[]{:S(2)}) collective-permute-start(f32[8,48,128]{2,1,0:T(8,128)S(1)} %get-tuple-element.44), channel_id=1, source_target_pairs={{0,192},{64,0},{128,64},{192,128},{1,193},{65,1},{129,65},{193,129... | collective-permute-start | bytes 589832 | tf_op jit(solution)/shard_map/ppermute | solution.py:396
  75.8 7.1 %collective-permute-start.12 = (f32[8,48,128]{2,1,0:T(8,128)S(1)}, f32[8,48,128]{2,1,0:T(8,128)S(1)}, u32[]{:S(2)}, u32[]{:S(2)}) collective-permute-start(f32[8,48,128]{2,1,0:T(8,128)S(1)} %add.22), channel_id=1, source_target_pairs={{0,64},{64,128},{128,192},{192,0},{1,65},{65,129},{129,193},{193,1... | collective-permute-start | bytes 589832 | tf_op jit(solution)/shard_map/ppermute | solution.py:396
  77.4 7.0 %collective-permute-start.8 = (f32[8,48,128]{2,1,0:T(8,128)S(1)}, f32[8,48,128]{2,1,0:T(8,128)S(1)}, u32[]{:S(2)}, u32[]{:S(2)}) collective-permute-start(f32[8,48,128]{2,1,0:T(8,128)S(1)} %add.19), channel_id=1, source_target_pairs={{0,192},{64,0},{128,64},{192,128},{1,193},{65,1},{129,65},{193,129... | collective-permute-start | bytes 589832 | tf_op jit(solution)/shard_map/ppermute | solution.py:396
  83.0 7.6 %collective-permute-start.13 = (f32[8,48,128]{2,1,0:T(8,128)S(1)}, f32[8,48,128]{2,1,0:T(8,128)S(1)}, u32[]{:S(2)}, u32[]{:S(2)}) collective-permute-start(f32[8,48,128]{2,1,0:T(8,128)S(1)} %add_add_fusion), channel_id=1, source_target_pairs={{0,64},{64,128},{128,192},{192,0},{1,65},{65,129},{129,193},{193,1... | collective-permute-start | bytes 589832 | tf_op jit(solution)/shard_map/ppermute | solution.py:396
  84.4 8.6 %collective-permute-start.9 = (f32[8,48,128]{2,1,0:T(8,128)S(1)}, f32[8,48,128]{2,1,0:T(8,128)S(1)}, u32[]{:S(2)}, u32[]{:S(2)}) collective-permute-start(f32[8,48,128]{2,1,0:T(8,128)S(1)} %add_add_fusion.1), channel_id=1, source_target_pairs={{0,192},{64,0},{128,64},{192,128},{1,193},{65,1},{129,65},{193,129... | collective-permute-start | bytes 589832 | tf_op jit(solution)/shard_map/ppermute | solution.py:396
  85.2 7.8 %collective-permute-start.15 = (f32[8,48,128]{2,1,0:T(8,128)S(1)}, f32[8,48,128]{2,1,0:T(8,128)S(1)}, u32[]{:S(2)}, u32[]{:S(2)}) collective-permute-start(f32[8,48,128]{2,1,0:T(8,128)S(1)} %add_add_fusion.1), channel_id=1, source_target_pairs={{0,64},{64,128},{128,192},{192,0},{1,65},{65,129},{129,193},{193,1... | collective-permute-start | bytes 589832 | tf_op jit(solution)/shard_map/ppermute | solution.py:396
  87.7 7.9 %collective-permute-start.16 = (f32[8,48,128]{2,1,0:T(8,128)S(1)}, f32[8,48,128]{2,1,0:T(8,128)S(1)}, u32[]{:S(2)}, u32[]{:S(2)}) collective-permute-start(f32[8,48,128]{2,1,0:T(8,128)S(1)} %add_add_fusion), channel_id=1, source_target_pairs={{0,192},{64,0},{128,64},{192,128},{1,193},{65,1},{129,65},{193,129... | collective-permute-start | bytes 589832 | tf_op jit(solution)/shard_map/ppermute | solution.py:396
  90.6 6.9 %collective-permute-start.14 = (f32[8,48,128]{2,1,0:T(8,128)S(1)}, f32[8,48,128]{2,1,0:T(8,128)S(1)}, u32[]{:S(2)}, u32[]{:S(2)}) collective-permute-start(f32[8,48,128]{2,1,0:T(8,128)S(1)} %collective-permute-done.13), channel_id=1, source_target_pairs={{0,64},{64,128},{128,192},{192,0},{1,65},{65,129},{129,193},{193,1... | collective-permute-start | bytes 589832 | tf_op jit(solution)/shard_map/ppermute | solution.py:396
  93.0 6.9 %collective-permute-start.10 = (f32[8,48,128]{2,1,0:T(8,128)S(1)}, f32[8,48,128]{2,1,0:T(8,128)S(1)}, u32[]{:S(2)}, u32[]{:S(2)}) collective-permute-start(f32[8,48,128]{2,1,0:T(8,128)S(1)} %collective-permute-done.9), channel_id=1, source_target_pairs={{0,192},{64,0},{128,64},{192,128},{1,193},{65,1},{129,65},{193,129... | collective-permute-start | bytes 589832 | tf_op jit(solution)/shard_map/ppermute | solution.py:396
  (5 other events, 7.2 us)
